TPU v7x, 32 devices: a whole 2x2x4 slice. The times are simulated.
32 devices in a mesh: groups: 2 (over x), pool: 16 (over z, y, core).
Axes of the slice: x: 2, y: 2, z: 4, core: 2. Of those that a mesh axis runs over, the one named last changes fastest.
Arguments:
- hidden: bfloat16 [64, 8192], P(('groups', 'pool')), parts along dimension 0, may hold values from -6 to 6
- gain: float32 [8192], replicated, may hold values from 0.1 to 1.9
- query_weight: bfloat16 [8192, 8192], P(None, 'pool'), may hold values from -0.0625 to 0.0625
- key_value_weight: bfloat16 [8192, 2048], P(None, 'pool'), may hold values from -0.0625 to 0.0625
- output_weight: bfloat16 [8192, 8192], P('pool'), may hold values from -0.5 to 0.5
- query_down_factor: bfloat16 [128, 8192, 16], P(('groups', 'pool')), parts along dimension 0, may hold values from -0.0625 to 0.0625
- query_up_factor: bfloat16 [128, 16, 8192], P(('groups', 'pool')), parts along dimension 0, may hold values from -1.5 to 1.5
- output_down_factor: bfloat16 [128, 8192, 16], P(('groups', 'pool')), parts along dimension 0, may hold values from -0.5 to 0.5
- output_up_factor: bfloat16 [128, 16, 8192], P(('groups', 'pool')), parts along dimension 0, may hold values from -1.5 to 1.5
- key_cache: bfloat16 [64, 512, 1024], P(('groups', 'pool')), parts along dimension 0, may hold values from -400 to 400
- value_cache: bfloat16 [64, 512, 1024], P(('groups', 'pool')), parts along dimension 0, may hold values from -6 to 6
- lengths: int32 [64], P(('groups', 'pool')), parts along dimension 0, may hold values from 1 to 512, as said below
- request_adapter: int32 [64], P(('groups', 'pool')), parts along dimension 0, may hold values from 0 to 63
- adapter_slot: int32 [128], P('groups'), parts along dimension 0, may hold values from 0 to 63, each once
Outputs:
- attn_out: bfloat16 [64, 8192], P(('groups', 'pool')), parts along dimension 0
There are 2 independent parts, one for each index of `groups`. A program takes and returns all parts, laid end to end along the dimension named above; an argument that names none is the same for every part. Nothing has to cross between parts.
Inputs may be any that keep to these rules, and one draw needn't show every extreme that they name: `lengths`: some request of every replica holds exactly 512 positions. `adapter_slot`: each slot holds exactly one adapter; the slot s lies on the device of pool index s // 4.
All inputs are finite; a program needn't handle non-finite values.
Results may differ from a plain program's by a relative error of at most 0.007.
The roundings to bfloat16 on the way count: a program that leaves them out, or rounds other values in their place, can miss the bound.
Values may be sent and summed in bfloat16 or wider, within the bound.
No kernel may reach another device: no remote copies, remote signals or barrier semaphores. Data moves between devices by JAX's collectives and lax.ppermute only.
A program may use at most 128 MiB of HBM per device.

v0:
```python
import jax
import jax.numpy as jnp
from jax import lax
from jax.sharding import PartitionSpec as P

MODEL_WIDTH = 8192
H = 64
KVH = 8
HEAD_WIDTH = 128
ADAPTER_RANK = 16
ADAPTER_SLOTS = 4
CACHE = 512
DKV = 1024


adapter_scale = 0.5
norm_eps = 1e-05


def norm_rows(hidden, gain):
    values = hidden.astype(jnp.float32)
    factor = lax.rsqrt(jnp.mean(values * values, axis=-1, keepdims=True) + norm_eps)
    return (values * factor * gain).astype(jnp.bfloat16)


def lookup_slots(all_ids, adapter_slot):
    table_size = adapter_slot.shape[0]
    matches = all_ids[:, None] == jnp.arange(table_size, dtype=jnp.int32)[None, :]
    return jnp.sum(jnp.where(matches, adapter_slot[None, :], 0), axis=1)


def attend(query_rows, keyval_rows, key_cache, value_cache, lengths):
    group_size = H // KVH
    local_rows = query_rows.shape[0]
    heads_q = query_rows.reshape(local_rows, KVH, group_size, HEAD_WIDTH)
    new_keys = keyval_rows[:, :DKV].reshape(local_rows, KVH, HEAD_WIDTH)
    new_values = keyval_rows[:, DKV:].reshape(local_rows, KVH, HEAD_WIDTH)
    cached_keys = key_cache.reshape(local_rows, CACHE, KVH, HEAD_WIDTH)
    cached_values = value_cache.reshape(local_rows, CACHE, KVH, HEAD_WIDTH)
    factor = HEAD_WIDTH ** (-0.5)
    scores = (
        jnp.einsum("rkgd,rckd->rkgc", heads_q, cached_keys, preferred_element_type=jnp.float32)
        * factor
    )
    own_score = (
        jnp.einsum("rkgd,rkd->rkg", heads_q, new_keys, preferred_element_type=jnp.float32) * factor
    )
    in_cache = (jnp.arange(CACHE, dtype=jnp.int32)[None, :] < lengths[:, None])[:, None, None, :]
    scores = jnp.where(in_cache, scores, -1e30)
    highest = jnp.maximum(jnp.max(scores, axis=-1), own_score)
    cached_exp = jnp.where(in_cache, jnp.exp(scores - highest[..., None]), 0.0)
    own_exp = jnp.exp(own_score - highest)
    softmax_sum = jnp.sum(cached_exp, axis=-1) + own_exp
    cached_weight = (cached_exp / softmax_sum[..., None]).astype(jnp.bfloat16)
    own_weight = (own_exp / softmax_sum).astype(jnp.bfloat16)
    mixture = jnp.einsum(
        "rkgc,rckd->rkgd", cached_weight, cached_values, preferred_element_type=jnp.float32
    )
    mixture = (
        mixture
        + own_weight.astype(jnp.float32)[..., None] * new_values.astype(jnp.float32)[:, :, None, :]
    )
    return mixture.reshape(local_rows, KVH * group_size * HEAD_WIDTH).astype(jnp.bfloat16)


def owner_shrunk(every_row, output_down_factor, owner_mask):
    output_partial = jnp.einsum(
        "we,bey->wby", every_row, output_down_factor, preferred_element_type=jnp.float32
    )
    return jnp.sum(jnp.where(owner_mask[:, :, None], output_partial, 0.0), axis=1)


def body(
    hidden,
    gain,
    query_weight,
    key_value_weight,
    output_weight,
    query_down_factor,
    query_up_factor,
    output_down_factor,
    output_up_factor,
    key_cache,
    value_cache,
    lengths,
    request_adapter,
    adapter_slot,
):
    normalized_input = norm_rows(hidden, gain)
    gathered_rows, all_ids = (
        lax.all_gather(normalized_input, "pool", axis=0, tiled=True),
        lax.all_gather(request_adapter, "pool", axis=0, tiled=True),
    )
    request_total = gathered_rows.shape[0]
    slot_total = adapter_slot.shape[0]
    slot_ids = lookup_slots(all_ids, adapter_slot)
    slot_table = slot_ids[:, None] == jnp.arange(slot_total, dtype=jnp.int32)[None, :]
    first_slot = lax.axis_index("pool") * ADAPTER_SLOTS
    owner_mask = (
        slot_ids[:, None] == first_slot + jnp.arange(ADAPTER_SLOTS, dtype=jnp.int32)[None, :]
    )
    bf_zero = jnp.zeros((), jnp.bfloat16)
    query_partial = jnp.einsum(
        "vg,wgl->vwl", gathered_rows, query_down_factor, preferred_element_type=jnp.float32
    )
    query_partial = jnp.sum(jnp.where(owner_mask[:, :, None], query_partial, 0.0), axis=1)
    shrunk_q = lax.psum(query_partial, "pool").astype(jnp.bfloat16)
    column_up_factor = lax.all_to_all(
        query_up_factor, "pool", split_axis=2, concat_axis=0, tiled=True
    )
    picked = jnp.where(slot_table[:, :, None], shrunk_q[:, None, :], bf_zero)
    picked = picked.reshape(request_total, slot_total * ADAPTER_RANK)
    query_delta = jnp.dot(
        picked,
        column_up_factor.reshape(slot_total * ADAPTER_RANK, -1),
        preferred_element_type=jnp.float32,
    )
    query_cols = (
        jnp.dot(gathered_rows, query_weight, preferred_element_type=jnp.float32)
        + adapter_scale * query_delta
    ).astype(jnp.bfloat16)
    keyval_cols = jnp.dot(
        gathered_rows, key_value_weight, preferred_element_type=jnp.float32
    ).astype(jnp.bfloat16)
    query_rows, keyval_rows = (
        lax.all_to_all(query_cols, "pool", split_axis=0, concat_axis=1, tiled=True),
        lax.all_to_all(keyval_cols, "pool", split_axis=0, concat_axis=1, tiled=True),
    )
    attention_output = attend(query_rows, keyval_rows, key_cache, value_cache, lengths)
    col_width = output_weight.shape[0]
    every_row = lax.all_gather(attention_output, "pool", axis=0, tiled=True)
    columns = lax.dynamic_slice_in_dim(every_row, lax.axis_index("pool") * col_width, col_width, 1)
    output_shrunk = owner_shrunk(every_row, output_down_factor, owner_mask).astype(jnp.bfloat16)
    lifted_rows = jnp.where(owner_mask[:, :, None], output_shrunk[:, None, :], bf_zero).reshape(
        request_total, ADAPTER_SLOTS * ADAPTER_RANK
    )
    down_product = output_up_factor.reshape(ADAPTER_SLOTS * ADAPTER_RANK, MODEL_WIDTH)
    base_product = jnp.dot(columns, output_weight, preferred_element_type=jnp.float32)
    summed_rows = lax.psum_scatter(
        base_product
        + adapter_scale * jnp.dot(lifted_rows, down_product, preferred_element_type=jnp.float32),
        "pool",
        scatter_dimension=0,
        tiled=True,
    )
    return summed_rows.astype(jnp.bfloat16)


def solution(mesh):
    placed = (
        P(("groups", "pool"), None),
        P(),
        P(None, "pool"),
        P(None, "pool"),
        P("pool", None),
        P(("groups", "pool"), None, None),
        P(("groups", "pool"), None, None),
        P(("groups", "pool"), None, None),
        P(("groups", "pool"), None, None),
        P(("groups", "pool"), None, None),
        P(("groups", "pool"), None, None),
        P(("groups", "pool")),
        P(("groups", "pool")),
        P("groups"),
    )
    return jax.shard_map(
        body, mesh=mesh, in_specs=placed, out_specs=P(("groups", "pool"), None), check_vma=False
    )
```

profile of v0, /device:TPU:0, one launch (start us, length us, event | category | flops | bytes accessed | tf_op | source)
XLA Modules:
  0.0 259.2 jit_solution(17246240990628994279)
XLA Ops:
  0.0 10.5 %copy.31 = bf16[4,16,8192]{1,0,2:T(4,128)(2,1)} copy(bf16[4,16,8192]{2,1,0:T(8,128)(2,1)} %param.20) | data formatting | bytes 2097152 | tf_op args[6]
  10.5 11.2 %reshape.161 = bf16[16,2,16384]{2,1,0:T(2,128)(2,1)} reshape(bf16[8192,4,16]{2,1,0:T(4,128)(2,1)} %bitcast.80) | data formatting | bytes 2097152
  21.7 7.6 %all-to-all-start = ((bf16[16,2,16384]{2,1,0:T(2,128)(2,1)}), bf16[16,2,16384]{2,1,0:T(2,128)(2,1)}, u32[]{:S(2)}, u32[]{:S(2)}) async-start(bf16[16,2,16384]{2,1,0:T(2,128)(2,1)} %reshape.161), calls=%async_computation | async-start | bytes 2097152 | tf_op jit(solution)/shard_map/all_to_all | solution.py:108
  29.3 0.2 fusion.26
  29.7 34.9 %all-gather = bf16[16,2,8192]{2,1,0:T(2,128)(2,1)S(1)} all-gather(bf16[1,2,8192]{2,1,0:T(2,128)(2,1)S(1)} %fusion.31), channel_id=1, replica_groups=mesh['groups'=2,'pool'=16] {'pool'}, dimensions={0}, use_global_device_ids=true | all-gather | bytes 557056 | tf_op jit(solution)/shard_map/all_gather | solution.py:91
  64.6 0.2 reshape.145
  64.8 0.7 fusion.41
  66.8 0.2 dynamic-update-slice
  67.0 12.4 %all-reduce = s32[32]{0:T(128)S(1)} all-reduce(s32[32]{0:T(128)S(1)} %dynamic-update-slice), channel_id=1, replica_groups=mesh['groups'=2,'pool'=16] {'pool'}, use_global_device_ids=true, to_apply=%add | all-reduce | flops 32 | bytes 256
  79.4 0.2 select_reduce_fusion.2
  79.7 1.6 fusion.43
  81.3 30.0 %psum.7 = bf16[32,16]{0,1:T(8,128)(2,1)S(1)} all-reduce(f32[32,16]{0,1:T(8,128)S(1)} %select_reduce_fusion.1), channel_id=1, replica_groups=mesh['groups'=2,'pool'=16] {'pool'}, use_global_device_ids=true, to_apply=%region_3.4 | all-reduce | flops 512 | bytes 3072 | tf_op jit(solution)/shard_map/psum | solution.py:107
  111.5 2.6 %convolution_convert_fusion = bf16[32,128]{1,0:T(8,128)(2,1)} fusion(bf16[32,8192]{1,0:T(8,128)(2,1)S(1)} %reshape.145, bf16[8192,128]{1,0:T(8,128)(2,1)} %param.17), kind=kOutput, calls=%fused_computation.16 | convolution fusion | flops 67112960 | bytes 2629632 | tf_op jit(solution)/shard_map/dot_general | solution.py:122
  114.1 3.5 %all-to-all-start.2 = ((bf16[16,2,128]{2,1,0:T(2,128)(2,1)}), bf16[16,2,128]{2,1,0:T(2,128)(2,1)S(1)}, u32[]{:S(2)}, u32[]{:S(2)}) async-start(bf16[16,2,128]{2,1,0:T(2,128)(2,1)} %bitcast.11), calls=%async_computation.2 | async-start | bytes 16384 | tf_op jit(solution)/shard_map/all_to_all | solution.py:127
  117.6 8.9 %reshape.162 = bf16[8192,4,16]{2,1,0:T(4,128)(2,1)} reshape(bf16[16,2,16384]{2,1,0:T(2,128)(2,1)} %all-to-all-done) | data formatting | bytes 2097152
  126.6 11.9 %copy.40 = bf16[4,16,16,512]{3,1,0,2:T(8,128)(2,1)} copy(bf16[4,16,16,512]{1,0,3,2:T(4,128)(2,1)} %bitcast.79) | data formatting | bytes 2097152 | tf_op jit(solution)/shard_map/all_to_all | solution.py:108
  138.5 1.5 convolution_multiply_fusion
  140.0 4.9 %fusion.17 = bf16[32,512]{1,0:T(8,128)(2,1)S(1)} fusion(f32[32,512]{1,0:T(8,128)S(1)} %convolution_multiply_fusion, bf16[32,8192]{1,0:T(8,128)(2,1)S(1)} %reshape.145, bf16[8192,512]{1,0:T(8,128)(2,1)} %param.16), kind=kOutput, calls=%fused_computation.14 | convolution fusion | flops 268468224 | bytes 9011200 | tf_op jit(solution)/shard_map/dot_general | solution.py:119
  144.9 0.7 all_to_all.40
  145.6 6.0 %all-to-all-start.1 = ((bf16[16,2,512]{2,1,0:T(2,128)(2,1)}), bf16[16,2,512]{2,1,0:T(2,128)(2,1)S(1)}, u32[]{:S(2)}, u32[]{:S(2)}) async-start(bf16[16,2,512]{2,1,0:T(2,128)(2,1)} %all_to_all.40), calls=%async_computation.1 | async-start | bytes 65536 | tf_op jit(solution)/shard_map/all_to_all | solution.py:126
  151.6 6.6 %all-to-all-done.1 = bf16[16,2,512]{2,1,0:T(2,128)(2,1)S(1)} async-done(((bf16[16,2,512]{2,1,0:T(2,128)(2,1)}), bf16[16,2,512]{2,1,0:T(2,128)(2,1)S(1)}, u32[]{:S(2)}, u32[]{:S(2)}) %all-to-all-start.1) | async-done | bytes 32800 | tf_op jit(solution)/shard_map/all_to_all | solution.py:126
  158.4 0.7 fusion.42
  159.1 0.2 fusion.21
  159.4 0.5 copy-done.6
  159.8 0.5 fusion.18
  160.4 19.0 %all-gather.1 = bf16[16,2,8192]{2,1,0:T(2,128)(2,1)S(1)} all-gather(bf16[1,2,8192]{2,1,0:T(2,128)(2,1)S(1)} %reshape.146), channel_id=1, replica_groups=mesh['groups'=2,'pool'=16] {'pool'}, dimensions={0}, use_global_device_ids=true | all-gather | bytes 557056 | tf_op jit(solution)/shard_map/all_gather | solution.py:131
  179.4 0.2 reshape.147
  179.6 1.6 fusion.45
  181.3 5.0 %fusion.29 = f32[32,8192]{1,0:T(8,128)S(1)} fusion(bf16[512,8192]{1,0:T(8,128)(2,1)} %param.18, bf16[32,8192]{1,0:T(8,128)(2,1)S(1)} %reshape.147, s32[]{:T(128)S(6)} %select_n.45), kind=kOutput, calls=%fused_computation.32 | convolution fusion | flops 268435456 | bytes 9469956 | tf_op jit(solution)/shard_map/dot_general | solution.py:138
  186.3 0.3 fusion.1
  186.7 71.0 %all-reduce.3 = bf16[32,8192]{1,0:T(8,128)(2,1)} all-reduce(f32[32,8192]{1,0:T(8,128)S(1)} %fusion.1), channel_id=2, replica_groups=mesh['groups'=2,'pool'=16] {'pool'}, use_global_device_ids=true, to_apply=%region_7.8.clone | all-reduce | flops 262144 | bytes 1572864
  257.6 1.6 dynamic-slice_convert_fusion
  (38 shorter events, 0.6 us)
Async XLA Ops:
  0.0 158.4 %copy-start = (bf16[2,512,1024]{2,1,0:T(8,128)(2,1)S(1)}, bf16[2,512,1024]{2,1,0:T(8,128)(2,1)}, u32[]{:S(2)}) copy-start(bf16[2,512,1024]{2,1,0:T(8,128)(2,1)} %param.23) | copy-start | bytes 6291460
  21.7 7.6 %copy-start.2 = (bf16[2,8192]{1,0:T(2,128)(2,1)S(1)}, bf16[2,8192]{1,0:T(2,128)(2,1)}, u32[]{:S(2)}) copy-start(bf16[2,8192]{1,0:T(2,128)(2,1)} %param.14) | copy-start | bytes 98308
  21.7 7.8 %copy-start.3 = (f32[8192]{0:T(1024)S(1)}, f32[8192]{0:T(1024)}, u32[]{:S(2)}) copy-start(f32[8192]{0:T(1024)} %param.15) | copy-start | bytes 98308
  21.7 43.1 %copy-start.4 = (u32[32]{0:T(128)S(1)}, u32[32]{0:T(128)}, u32[]{:S(2)}) copy-start(u32[32]{0:T(128)} %constant.42) | copy-start | bytes 388
  21.7 45.1 %copy-start.7 = (s32[2]{0:T(128)S(1)}, s32[2]{0:T(128)}, u32[]{:S(2)}) copy-start(s32[2]{0:T(128)} %param.26) | copy-start | bytes 28
  21.7 57.7 %copy-start.8 = (s32[64]{0:T(128)S(1)}, s32[64]{0:T(128)}, u32[]{:S(2)}) copy-start(s32[64]{0:T(128)} %param.27) | copy-start | bytes 772
  21.7 92.4 %all-to-all-start = ((bf16[16,2,16384]{2,1,0:T(2,128)(2,1)}), bf16[16,2,16384]{2,1,0:T(2,128)(2,1)}, u32[]{:S(2)}, u32[]{:S(2)}) async-start(bf16[16,2,16384]{2,1,0:T(2,128)(2,1)} %reshape.161), calls=%async_computation | async-start | bytes 2097152 | tf_op jit(solution)/shard_map/all_to_all | solution.py:108
  29.3 82.0 %copy-start.5 = (s32[2]{0:T(128)S(1)}, s32[2]{0:T(128)}, u32[]{:S(2)}) copy-start(s32[2]{0:T(128)} %param.25) | copy-start | bytes 28
  114.1 31.4 %all-to-all-start.2 = ((bf16[16,2,128]{2,1,0:T(2,128)(2,1)}), bf16[16,2,128]{2,1,0:T(2,128)(2,1)S(1)}, u32[]{:S(2)}, u32[]{:S(2)}) async-start(bf16[16,2,128]{2,1,0:T(2,128)(2,1)} %bitcast.11), calls=%async_computation.2 | async-start | bytes 16384 | tf_op jit(solution)/shard_map/all_to_all | solution.py:127
  145.6 12.6 %all-to-all-start.1 = ((bf16[16,2,512]{2,1,0:T(2,128)(2,1)}), bf16[16,2,512]{2,1,0:T(2,128)(2,1)S(1)}, u32[]{:S(2)}, u32[]{:S(2)}) async-start(bf16[16,2,512]{2,1,0:T(2,128)(2,1)} %all_to_all.40), calls=%async_computation.1 | async-start | bytes 65536 | tf_op jit(solution)/shard_map/all_to_all | solution.py:126
  158.2 1.6 copy-start.6
  181.3 5.0 %copy-start.1 = (bf16[4,16,8192]{2,1,0:T(8,128)(2,1)S(1)}, bf16[4,16,8192]{2,1,0:T(8,128)(2,1)}, u32[]{:S(2)}) copy-start(bf16[4,16,8192]{2,1,0:T(8,128)(2,1)} %param.22) | copy-start | bytes 3145732
where the time goes:
time: 261 us; the launch traced here: 259 us
  blocking collectives  167 us (64%)
  local copies, waits for them, and re-layouts  46.7 us (18%)
  matrix products  19.1 us (7%)
  starting transfers between devices  17 us (7%)
  waiting for transfers between devices  6.6 us (3%)
    unnamed x2, blocking collectives  83.3 us
    all_gather x1, blocking collectives, body(): lax.all_gather(normalized_input, 'pool', axis=0, tiled=True)  34.9 us
    unnamed x28, local copies, waits for them, and re-layouts  32.5 us
    psum x1, blocking collectives, body(): shrunk_q = lax.psum(query_partial, 'pool').astype(jnp.bfloat16)  30 us
    all_gather x1, blocking collectives, body(): every_row = lax.all_gather(attention_output, 'pool', axis=0, tiled=True)  19 us
    all_to_all x1, local copies, waits for them, and re-layouts, body(): lax.all_to_all(query_up_factor, 'pool', split_axis=2, concat_axis=0, tile...  11.9 us
    all_to_all x1, starting transfers between devices, body(): lax.all_to_all(query_up_factor, 'pool', split_axis=2, concat_axis=0, tile...  7.58 us
    all_to_all x1, waiting for transfers between devices, body(): lax.all_to_all(query_cols, 'pool', split_axis=0, concat_axis=1, tiled=True)  6.59 us
  transfers between devices with their start and end apart: 3, of which 1 were waited for; matrix products, arithmetic and copies ran while one was open for 13% of the time, Pallas kernels for 0%

commit v1 on v0

--- a/solution.py
+++ b/solution.py
@@ -8,7 +8,6 @@
 KVH = 8
 HEAD_WIDTH = 128
 ADAPTER_RANK = 16
-ADAPTER_SLOTS = 4
 CACHE = 512
 DKV = 1024
 
@@ -63,11 +62,45 @@
     return mixture.reshape(local_rows, KVH * group_size * HEAD_WIDTH).astype(jnp.bfloat16)
 
 
-def owner_shrunk(every_row, output_down_factor, owner_mask):
-    output_partial = jnp.einsum(
-        "we,bey->wby", every_row, output_down_factor, preferred_element_type=jnp.float32
-    )
-    return jnp.sum(jnp.where(owner_mask[:, :, None], output_partial, 0.0), axis=1)
+def owner_shrunk(rows, down_factor, owner_mask):
+    partial = jnp.einsum("we,bey->wby", rows, down_factor, preferred_element_type=jnp.float32)
+    return jnp.sum(jnp.where(owner_mask[:, :, None], partial, 0.0), axis=1).astype(jnp.bfloat16)
+
+
+def pool_size():
+    return lax.axis_size("pool")
+
+
+def gather_rows(rows):
+    count = pool_size()
+    me = lax.axis_index("pool")
+    step = 4
+    while step < count:
+        other = lax.ppermute(rows, "pool", [(i, i ^ step) for i in range(count)])
+        upper = (me & step) != 0
+        first = jnp.where(upper, other, rows)
+        second = jnp.where(upper, rows, other)
+        rows = jnp.concatenate([first, second], axis=0)
+        step *= 2
+    fours = [[4 * k + j for j in range(4)] for k in range(count // 4)]
+    width = rows.shape[-1]
+    rows = lax.all_gather(rows, "pool", axis=0, axis_index_groups=fours)
+    rows = rows.reshape(4, count // 4, -1, width).transpose(1, 0, 2, 3)
+    return rows.reshape(-1, width)
+
+
+def scatter_sums(partial):
+    count = pool_size()
+    me = lax.axis_index("pool")
+    width = partial.shape[-1]
+    blocks = partial.reshape(count // 2, 2, -1, width)
+    odd = (me & 1) != 0
+    keep = jnp.where(odd, blocks[:, 1], blocks[:, 0])
+    give = jnp.where(odd, blocks[:, 0], blocks[:, 1])
+    keep = keep + lax.ppermute(give, "pool", [(i, i ^ 1) for i in range(count)])
+    same_core = [[2 * k + c for k in range(count // 2)] for c in range(2)]
+    parts = lax.all_to_all(keep, "pool", 0, 0, tiled=True, axis_index_groups=same_core)
+    return jnp.sum(parts, axis=0)
 
 
 def body(
@@ -86,35 +119,42 @@
     request_adapter,
     adapter_slot,
 ):
+    count = pool_size()
+    own_slots = query_down_factor.shape[0]
+    local_rows = hidden.shape[0]
+    slot_total = adapter_slot.shape[0]
+    col_width = query_weight.shape[1]
+
+    up_blocks = query_up_factor.reshape(own_slots, ADAPTER_RANK, count, col_width)
+    up_blocks = up_blocks.transpose(2, 0, 1, 3)
+    column_up_factor = lax.all_to_all(up_blocks, "pool", 0, 0, tiled=True)
+    column_up_factor = column_up_factor.reshape(slot_total * ADAPTER_RANK, col_width)
+
     normalized_input = norm_rows(hidden, gain)
-    gathered_rows, all_ids = (
-        lax.all_gather(normalized_input, "pool", axis=0, tiled=True),
-        lax.all_gather(request_adapter, "pool", axis=0, tiled=True),
-    )
+    slot_ids = lookup_slots(request_adapter, adapter_slot)
+    digits = jnp.stack([slot_ids // 32, slot_ids % 32], axis=1).astype(jnp.bfloat16)
+    sent = jnp.concatenate([normalized_input, jnp.pad(digits, ((0, 0), (0, 126)))], axis=1)
+    gathered = gather_rows(sent)
+    gathered_rows = gathered[:, :MODEL_WIDTH]
+    all_digits = gathered[:, MODEL_WIDTH : MODEL_WIDTH + 2].astype(jnp.int32)
+    slot_ids = all_digits[:, 0] * 32 + all_digits[:, 1]
     request_total = gathered_rows.shape[0]
-    slot_total = adapter_slot.shape[0]
-    slot_ids = lookup_slots(all_ids, adapter_slot)
+
     slot_table = slot_ids[:, None] == jnp.arange(slot_total, dtype=jnp.int32)[None, :]
-    first_slot = lax.axis_index("pool") * ADAPTER_SLOTS
+    first_slot = lax.axis_index("pool") * own_slots
     owner_mask = (
-        slot_ids[:, None] == first_slot + jnp.arange(ADAPTER_SLOTS, dtype=jnp.int32)[None, :]
+        slot_ids[:, None] == first_slot + jnp.arange(own_slots, dtype=jnp.int32)[None, :]
     )
     bf_zero = jnp.zeros((), jnp.bfloat16)
-    query_partial = jnp.einsum(
-        "vg,wgl->vwl", gathered_rows, query_down_factor, preferred_element_type=jnp.float32
-    )
-    query_partial = jnp.sum(jnp.where(owner_mask[:, :, None], query_partial, 0.0), axis=1)
-    shrunk_q = lax.psum(query_partial, "pool").astype(jnp.bfloat16)
-    column_up_factor = lax.all_to_all(
-        query_up_factor, "pool", split_axis=2, concat_axis=0, tiled=True
-    )
+
+    own_shrunk = owner_shrunk(gathered_rows, query_down_factor, owner_mask)
+    spread = jnp.broadcast_to(own_shrunk[None], (count,) + own_shrunk.shape)
+    shrunk_q = jnp.sum(
+        lax.all_to_all(spread, "pool", 0, 0, tiled=True).astype(jnp.float32), axis=0
+    ).astype(jnp.bfloat16)
     picked = jnp.where(slot_table[:, :, None], shrunk_q[:, None, :], bf_zero)
     picked = picked.reshape(request_total, slot_total * ADAPTER_RANK)
-    query_delta = jnp.dot(
-        picked,
-        column_up_factor.reshape(slot_total * ADAPTER_RANK, -1),
-        preferred_element_type=jnp.float32,
-    )
+    query_delta = jnp.dot(picked, column_up_factor, preferred_element_type=jnp.float32)
     query_cols = (
         jnp.dot(gathered_rows, query_weight, preferred_element_type=jnp.float32)
         + adapter_scale * query_delta
@@ -122,28 +162,24 @@
     keyval_cols = jnp.dot(
         gathered_rows, key_value_weight, preferred_element_type=jnp.float32
     ).astype(jnp.bfloat16)
-    query_rows, keyval_rows = (
-        lax.all_to_all(query_cols, "pool", split_axis=0, concat_axis=1, tiled=True),
-        lax.all_to_all(keyval_cols, "pool", split_axis=0, concat_axis=1, tiled=True),
-    )
+    both = jnp.concatenate([query_cols, keyval_cols], axis=1)
+    both = lax.all_to_all(both.reshape(count, local_rows, -1), "pool", 0, 0, tiled=True)
+    query_rows = both[:, :, :col_width].transpose(1, 0, 2).reshape(local_rows, -1)
+    keyval_rows = both[:, :, col_width:].transpose(1, 0, 2).reshape(local_rows, -1)
+
     attention_output = attend(query_rows, keyval_rows, key_cache, value_cache, lengths)
-    col_width = output_weight.shape[0]
-    every_row = lax.all_gather(attention_output, "pool", axis=0, tiled=True)
-    columns = lax.dynamic_slice_in_dim(every_row, lax.axis_index("pool") * col_width, col_width, 1)
-    output_shrunk = owner_shrunk(every_row, output_down_factor, owner_mask).astype(jnp.bfloat16)
+    every_row = gather_rows(attention_output)
+    out_width = output_weight.shape[0]
+    columns = lax.dynamic_slice_in_dim(every_row, lax.axis_index("pool") * out_width, out_width, 1)
+    output_shrunk = owner_shrunk(every_row, output_down_factor, owner_mask)
     lifted_rows = jnp.where(owner_mask[:, :, None], output_shrunk[:, None, :], bf_zero).reshape(
-        request_total, ADAPTER_SLOTS * ADAPTER_RANK
-    )
-    down_product = output_up_factor.reshape(ADAPTER_SLOTS * ADAPTER_RANK, MODEL_WIDTH)
-    base_product = jnp.dot(columns, output_weight, preferred_element_type=jnp.float32)
-    summed_rows = lax.psum_scatter(
-        base_product
-        + adapter_scale * jnp.dot(lifted_rows, down_product, preferred_element_type=jnp.float32),
-        "pool",
-        scatter_dimension=0,
-        tiled=True,
-    )
-    return summed_rows.astype(jnp.bfloat16)
+        request_total, own_slots * ADAPTER_RANK
+    )
+    up_rows = output_up_factor.reshape(own_slots * ADAPTER_RANK, MODEL_WIDTH)
+    partial = jnp.dot(
+        columns, output_weight, preferred_element_type=jnp.float32
+    ) + adapter_scale * jnp.dot(lifted_rows, up_rows, preferred_element_type=jnp.float32)
+    return scatter_sums(partial).astype(jnp.bfloat16)
 
 
 def solution(mesh):

time: 261 us -> 140 us (0.54)
  blocking collectives: 167 us -> 31.4 us
  waiting for transfers between devices: 6.6 us -> 43.9 us
  local copies, waits for them, and re-layouts: 46.7 us -> 14.9 us
  starting transfers between devices: 17 us -> 23.8 us
  other arithmetic: 0.94 us -> 5.68 us
    unnamed x2 -> x0, blocking collectives: 83.3 us -> none
    all_gather x2, blocking collectives: 53.9 us -> 13.8 us  [gather_rows(): rows = lax.all_gather(rows, 'pool', axis=0, axis_index_groups=fours)]
    psum x1 -> x0, blocking collectives: 30 us -> none  [body(): shrunk_q = lax.psum(query_partial, 'pool').astype(jnp.bfloat16)]
    unnamed x28 -> x15, local copies, waits for them, and re-layouts: 32.5 us -> 4.03 us
    all_to_all x3, waiting for transfers between devices: 6.6 us -> 30.9 us  [the longest x1 20.7 us: body(): column_up_factor = lax.all_to_all(up_blocks, 'pool', 0, 0, tiled=True)]
    all_to_all x0 -> x1, blocking collectives: none -> 17.7 us  [scatter_sums(): lax.all_to_all(keep, 'pool', 0, 0, tiled=True, axis_index_groups=same_core)]
    ppermute x0 -> x5, waiting for transfers between devices: none -> 13 us  [the longest x4 11.5 us: gather_rows(): other = lax.ppermute(rows, 'pool', [(i, i ^ step) for i in range(count)])]
    all_to_all x3 -> x0, local copies, waits for them, and re-layouts: 12.6 us -> none  [the longest x1 11.9 us: body(): lax.all_to_all(query_up_factor, 'pool', split_axis=2, concat_axis=0, tile...]
  transfers between devices with their start and end apart: 3 -> 8, of which waited for: 1 -> 7; matrix products, arithmetic and copies ran while one was open for 13% -> 6% of each run, Pallas kernels for 0% -> 0%
where the time goes in v1:
time: 140 us; the launch traced here: 139 us
  waiting for transfers between devices  43.9 us (31%)
  blocking collectives  31.4 us (22%)
  starting transfers between devices  23.8 us (17%)
  matrix products  19.5 us (14%)
  local copies, waits for them, and re-layouts  14.9 us (11%)
  other arithmetic  5.68 us (4%)
    all_to_all x1, waiting for transfers between devices, body(): column_up_factor = lax.all_to_all(up_blocks, 'pool', 0, 0, tiled=True)  20.7 us
    all_to_all x1, blocking collectives, scatter_sums(): lax.all_to_all(keep, 'pool', 0, 0, tiled=True, axis_index_groups=same_core)  17.7 us
    all_gather x2, blocking collectives, gather_rows(): rows = lax.all_gather(rows, 'pool', axis=0, axis_index_groups=fours)  13.8 us
    ppermute x4, waiting for transfers between devices, gather_rows(): other = lax.ppermute(rows, 'pool', [(i, i ^ step) for i in range(count)])  11.5 us
    all_to_all x1, starting transfers between devices, body(): lax.all_to_all(both.reshape(count, local_rows, -1), 'pool', 0, 0, tiled=T...  6.81 us
    all_to_all x1, waiting for transfers between devices, body(): lax.all_to_all(both.reshape(count, local_rows, -1), 'pool', 0, 0, tiled=T...  6.61 us
    ppermute x4, starting transfers between devices, gather_rows(): other = lax.ppermute(rows, 'pool', [(i, i ^ step) for i in range(count)])  6.51 us
    all_to_all x1, starting transfers between devices, body(): lax.all_to_all(spread, 'pool', 0, 0, tiled=True).astype(jnp.float32)  5.71 us
  transfers between devices with their start and end apart: 8, of which 7 were waited for; matrix products, arithmetic and copies ran while one was open for 6% of the time, Pallas kernels for 0%

profile of v1, /device:TPU:0, one launch (start us, length us, event | category | flops | bytes accessed | tf_op | source)
XLA Modules:
  0.0 139.5 jit_solution(1303478544370145247)
XLA Ops:
  0.0 1.0 fusion.49
  1.1 0.9 fusion.36
  3.0 3.1 %collective-permute-start = (bf16[2,8320]{1,0:T(2,128)(2,1)S(1)}, bf16[2,8320]{1,0:T(2,128)(2,1)S(1)}, u32[]{:S(2)}, u32[]{:S(2)}) collective-permute-start(bf16[2,8320]{1,0:T(2,128)(2,1)S(1)} %fusion.39), channel_id=1, source_target_pairs={{0,4},{1,5},{2,6},{3,7},{4,0},{5,1},{6,2},{7,3},{8,12},{9,13},{10,... | collective-permute-start | bytes 99848 | tf_op jit(solution)/shard_map/ppermute | solution.py:79
  6.1 2.6 %copy.72 = bf16[8,8,16,512]{3,2,1,0:T(8,128)(2,1)} copy(bf16[8,8,16,512]{3,1,2,0:T(8,128)(2,1)} %bitcast.133) | data formatting | bytes 2097152
  8.8 2.7 %collective-permute-start.1 = (bf16[4,8320]{1,0:T(4,128)(2,1)S(1)}, bf16[4,8320]{1,0:T(4,128)(2,1)S(1)}, u32[]{:S(2)}, u32[]{:S(2)}) collective-permute-start(bf16[4,8320]{1,0:T(4,128)(2,1)S(1)} %pad_maximum_fusion.2), channel_id=1, source_target_pairs={{0,8},{1,9},{2,10},{3,11},{4,12},{5,13},{6,14},{7,15},{8,0},{9,1},... | collective-permute-start | bytes 199688 | tf_op jit(solution)/shard_map/ppermute | solution.py:79
  11.5 2.6 %collective-permute-done.1 = bf16[4,8320]{1,0:T(4,128)(2,1)S(1)} collective-permute-done((bf16[4,8320]{1,0:T(4,128)(2,1)S(1)}, bf16[4,8320]{1,0:T(4,128)(2,1)S(1)}, u32[]{:S(2)}, u32[]{:S(2)}) %collective-permute-start.1) | collective-permute-done | bytes 66592 | tf_op jit(solution)/shard_map/ppermute | solution.py:79
  14.3 7.2 %all-gather = bf16[32,8320]{1,0:T(8,128)(2,1)S(1)} all-gather(bf16[8,8320]{1,0:T(8,128)(2,1)S(1)} %pad_maximum_fusion), channel_id=2, replica_groups={{0,1,2,3},{4,5,6,7},{8,9,10,11},{12,13,14,15},{16,17,18,19},{20,21,22,2..., dimensions={0}, use_global_device_ids=true | all-gather | bytes 665600 | tf_op jit(solution)/shard_map/all_gather | solution.py:87
  21.7 1.2 copy.102
  22.9 1.2 reshape.232
  24.3 1.6 %fusion.28 = f32[32,64]{0,1:S(1)} fusion(bf16[8192,64]{0,1:T(8,128)(2,1)} %bitcast.142, bf16[32,8320]{1,0:T(8,128)(2,1)S(1)} %reshape.232), kind=kOutput, calls=%fused_computation.26 | convolution fusion | flops 33554432 | bytes 1605632
  26.8 5.7 %all-to-all-start = ((bf16[16,2,256]{2,1,0:T(2,128)(2,1)}), bf16[16,2,256]{2,1,0:T(2,128)(2,1)S(1)}, u32[]{:S(2)}, u32[]{:S(2)}) async-start(bf16[16,2,256]{2,1,0:T(2,128)(2,1)} %reshape.258), calls=%async_computation | async-start | bytes 32768 | tf_op jit(solution)/shard_map/all_to_all | solution.py:153
  32.5 1.3 bitcast_bitcast_fusion
  33.8 1.6 %copy.57 = bf16[16,4,16,512]{3,2,1,0:T(8,128)(2,1)} copy(bf16[16,4,16,512]{3,0,2,1:T(8,128)(2,1)S(1)} %bitcast_bitcast_fusion) | data formatting | bytes 2097152 | tf_op jit(solution)/shard_map/transpose | solution.py:129
  35.4 3.6 %all-to-all-done = bf16[16,2,256]{2,1,0:T(2,128)(2,1)S(1)} async-done(((bf16[16,2,256]{2,1,0:T(2,128)(2,1)}), bf16[16,2,256]{2,1,0:T(2,128)(2,1)S(1)}, u32[]{:S(2)}, u32[]{:S(2)}) %all-to-all-start) | async-done | bytes 16416 | tf_op jit(solution)/shard_map/all_to_all | solution.py:153
  39.0 4.3 %all-to-all-start.1 = ((bf16[16,4,16,512]{3,2,1,0:T(8,128)(2,1)}), bf16[16,4,16,512]{3,2,1,0:T(8,128)(2,1)}, u32[]{:S(2)}, u32[]{:S(2)}) async-start(bf16[16,4,16,512]{3,2,1,0:T(8,128)(2,1)} %copy.57), calls=%async_computation.1 | async-start | bytes 2097152 | tf_op jit(solution)/shard_map/all_to_all | solution.py:130
  43.4 2.1 %convolution_convert_fusion = bf16[32,128]{1,0:T(8,128)(2,1)S(1)} fusion(bf16[8192,128]{1,0:T(8,128)(2,1)} %param.17, bf16[32,8320]{1,0:T(8,128)(2,1)S(1)} %reshape.232), kind=kOutput, calls=%fused_computation.17 | convolution fusion | flops 67112960 | bytes 2629632 | tf_op jit(solution)/shard_map/dot_general | solution.py:162
  45.6 20.7 %all-to-all-done.1 = bf16[16,4,16,512]{3,2,1,0:T(8,128)(2,1)} async-done(((bf16[16,4,16,512]{3,2,1,0:T(8,128)(2,1)}), bf16[16,4,16,512]{3,2,1,0:T(8,128)(2,1)}, u32[]{:S(2)}, u32[]{:S(2)}) %all-to-all-start.1) | async-done | bytes 1048608 | tf_op jit(solution)/shard_map/all_to_all | solution.py:130
  66.3 1.5 %convolution_multiply_fusion = f32[32,512]{1,0:T(8,128)S(1)} fusion(bf16[32,1024]{0,1:T(8,128)(2,1)S(1)} %bitcast.135, bf16[1024,512]{1,0:T(8,128)(2,1)} %bitcast.7), kind=kOutput, calls=%fused_computation.13 | convolution fusion | flops 33570816 | bytes 1179648 | tf_op jit(solution)/shard_map/dot_general | solution.py:157
  67.8 4.9 %fusion.17 = bf16[32,512]{1,0:T(8,128)(2,1)S(1)} fusion(f32[32,512]{1,0:T(8,128)S(1)} %convolution_multiply_fusion, bf16[8192,512]{1,0:T(8,128)(2,1)} %param.16, bf16[32,8320]{1,0:T(8,128)(2,1)S(1)} %reshape.232), kind=kOutput, calls=%fused_computation.14 | convolution fusion | flops 268468224 | bytes 9011200 | tf_op jit(solution)/shard_map/dot_general | solution.py:159
  73.4 6.8 %all-to-all-start.2 = ((bf16[16,2,640]{2,1,0:T(2,128)(2,1)}), bf16[16,2,640]{2,1,0:T(2,128)(2,1)S(1)}, u32[]{:S(2)}, u32[]{:S(2)}) async-start(bf16[16,2,640]{2,1,0:T(2,128)(2,1)} %reshape.235), calls=%async_computation.2 | async-start | bytes 81920 | tf_op jit(solution)/shard_map/all_to_all | solution.py:166
  80.3 6.6 %all-to-all-done.2 = bf16[16,2,640]{2,1,0:T(2,128)(2,1)S(1)} async-done(((bf16[16,2,640]{2,1,0:T(2,128)(2,1)}), bf16[16,2,640]{2,1,0:T(2,128)(2,1)S(1)}, u32[]{:S(2)}, u32[]{:S(2)}) %all-to-all-start.2) | async-done | bytes 40992 | tf_op jit(solution)/shard_map/all_to_all | solution.py:166
  89.6 3.6 %collective-permute-done.2 = bf16[2,8192]{1,0:T(2,128)(2,1)S(1)} collective-permute-done((bf16[2,8192]{1,0:T(2,128)(2,1)S(1)}, bf16[2,8192]{1,0:T(2,128)(2,1)S(1)}, u32[]{:S(2)}, u32[]{:S(2)}) %collective-permute-start.2) | collective-permute-done | bytes 32800 | tf_op jit(solution)/shard_map/ppermute | solution.py:79
  93.7 5.2 %collective-permute-done.3 = bf16[4,8192]{1,0:T(4,128)(2,1)S(1)} collective-permute-done((bf16[4,8192]{1,0:T(4,128)(2,1)S(1)}, bf16[4,8192]{1,0:T(4,128)(2,1)S(1)}, u32[]{:S(2)}, u32[]{:S(2)}) %collective-permute-start.3) | collective-permute-done | bytes 65568 | tf_op jit(solution)/shard_map/ppermute | solution.py:79
  99.2 6.5 %all-gather.1 = bf16[32,8192]{1,0:T(8,128)(2,1)S(1)} all-gather(bf16[8,8192]{1,0:T(8,128)(2,1)S(1)} %pad_maximum_fusion.1), channel_id=3, replica_groups={{0,1,2,3},{4,5,6,7},{8,9,10,11},{12,13,14,15},{16,17,18,19},{20,21,22,2..., dimensions={0}, use_global_device_ids=true | all-gather | bytes 655360 | tf_op jit(solution)/shard_map/all_gather | solution.py:87
  106.0 1.2 copy.61
  107.2 1.2 reshape.241
  108.5 1.6 %fusion.57 = f32[32,64]{0,1:S(1)} fusion(bf16[32,8192]{1,0:T(8,128)(2,1)S(1)} %reshape.241, bf16[8192,64]{0,1:T(8,128)(2,1)} %bitcast.134), kind=kOutput, calls=%fused_computation.102 | convolution fusion | flops 33554432 | bytes 1581056
  110.1 5.0 %fusion.40 = f32[32,8192]{1,0:T(8,128)S(1)} fusion(bf16[512,8192]{1,0:T(8,128)(2,1)} %param.18, bf16[32,8192]{1,0:T(8,128)(2,1)S(1)} %reshape.241, s32[]{:T(128)S(6)} %select_n.152), kind=kOutput, calls=%fused_computation.60 | convolution fusion | flops 268435456 | bytes 9469956 | tf_op jit(solution)/shard_map/dot_general | solution.py:179
  115.2 1.3 fusion.1
  116.5 1.8 %reshape.242 = f32[8,2,2,8192]{3,2,1,0:T(2,128)S(1)} reshape(f32[32,8192]{1,0:T(8,128)} %fusion.1) | data formatting | bytes 2097152 | tf_op jit(solution)/shard_map/reshape | solution.py:96
  119.0 1.6 %collective-permute-done.4 = f32[8,2,8192]{2,1,0:T(2,128)S(1)} collective-permute-done((f32[8,2,8192]{2,1,0:T(2,128)S(1)}, f32[8,2,8192]{2,1,0:T(2,128)S(1)}, u32[]{:S(2)}, u32[]{:S(2)}) %collective-permute-start.4) | collective-permute-done | bytes 524320 | tf_op jit(solution)/shard_map/ppermute | solution.py:100
  121.0 17.7 %all_to_all.20 = f32[8,2,8192]{2,1,0:T(2,128)S(1)} all-to-all(f32[8,2,8192]{2,1,0:T(2,128)S(1)} %fusion.26), channel_id=1, replica_groups={{0,2,4,6,8,10,12,14},{1,3,5,7,9,11,13,15},{16,18,20,22,24,26,28,30},{17..., dimensions={0} | all-to-all | bytes 1048576 | tf_op jit(solution)/shard_map/all_to_all | solution.py:102
  (60 shorter events, 9.0 us)
Async XLA Ops:
  0.0 87.2 %copy-start = (bf16[2,512,1024]{2,1,0:T(8,128)(2,1)S(1)}, bf16[2,512,1024]{2,1,0:T(8,128)(2,1)}, u32[]{:S(2)}) copy-start(bf16[2,512,1024]{2,1,0:T(8,128)(2,1)} %param.23) | copy-start | bytes 6291460
  3.0 5.7 %collective-permute-start = (bf16[2,8320]{1,0:T(2,128)(2,1)S(1)}, bf16[2,8320]{1,0:T(2,128)(2,1)S(1)}, u32[]{:S(2)}, u32[]{:S(2)}) collective-permute-start(bf16[2,8320]{1,0:T(2,128)(2,1)S(1)} %fusion.39), channel_id=1, source_target_pairs={{0,4},{1,5},{2,6},{3,7},{4,0},{5,1},{6,2},{7,3},{8,12},{9,13},{10,... | collective-permute-start | bytes 99848 | tf_op jit(solution)/shard_map/ppermute | solution.py:79
  8.8 5.2 %collective-permute-start.1 = (bf16[4,8320]{1,0:T(4,128)(2,1)S(1)}, bf16[4,8320]{1,0:T(4,128)(2,1)S(1)}, u32[]{:S(2)}, u32[]{:S(2)}) collective-permute-start(bf16[4,8320]{1,0:T(4,128)(2,1)S(1)} %pad_maximum_fusion.2), channel_id=1, source_target_pairs={{0,8},{1,9},{2,10},{3,11},{4,12},{5,13},{6,14},{7,15},{8,0},{9,1},... | collective-permute-start | bytes 199688 | tf_op jit(solution)/shard_map/ppermute | solution.py:79
  26.8 12.2 %all-to-all-start = ((bf16[16,2,256]{2,1,0:T(2,128)(2,1)}), bf16[16,2,256]{2,1,0:T(2,128)(2,1)S(1)}, u32[]{:S(2)}, u32[]{:S(2)}) async-start(bf16[16,2,256]{2,1,0:T(2,128)(2,1)} %reshape.258), calls=%async_computation | async-start | bytes 32768 | tf_op jit(solution)/shard_map/all_to_all | solution.py:153
  39.0 27.3 %all-to-all-start.1 = ((bf16[16,4,16,512]{3,2,1,0:T(8,128)(2,1)}), bf16[16,4,16,512]{3,2,1,0:T(8,128)(2,1)}, u32[]{:S(2)}, u32[]{:S(2)}) async-start(bf16[16,4,16,512]{3,2,1,0:T(8,128)(2,1)} %copy.57), calls=%async_computation.1 | async-start | bytes 2097152 | tf_op jit(solution)/shard_map/all_to_all | solution.py:130
  67.8 12.4 %copy-start.2 = (s32[2]{0:T(128)S(1)}, s32[2]{0:T(128)}, u32[]{:S(2)}) copy-start(s32[2]{0:T(128)} %param.25) | copy-start | bytes 28
  73.4 13.5 %all-to-all-start.2 = ((bf16[16,2,640]{2,1,0:T(2,128)(2,1)}), bf16[16,2,640]{2,1,0:T(2,128)(2,1)S(1)}, u32[]{:S(2)}, u32[]{:S(2)}) async-start(bf16[16,2,640]{2,1,0:T(2,128)(2,1)} %reshape.235), calls=%async_computation.2 | async-start | bytes 81920 | tf_op jit(solution)/shard_map/all_to_all | solution.py:166
  87.1 1.6 %copy-start.3 = (bf16[2,512,1024]{2,1,0:T(8,128)(2,1)S(1)}, bf16[2,512,1024]{2,1,0:T(8,128)(2,1)}, u32[]{:S(2)}) copy-start(bf16[2,512,1024]{2,1,0:T(8,128)(2,1)} %param.24) | copy-start | bytes 6291460
  89.2 4.0 %collective-permute-start.2 = (bf16[2,8192]{1,0:T(2,128)(2,1)S(1)}, bf16[2,8192]{1,0:T(2,128)(2,1)S(1)}, u32[]{:S(2)}, u32[]{:S(2)}) collective-permute-start(bf16[2,8192]{1,0:T(2,128)(2,1)S(1)} %bitcast.140), channel_id=1, source_target_pairs={{0,4},{1,5},{2,6},{3,7},{4,0},{5,1},{6,2},{7,3},{8,12},{9,13},{10,... | collective-permute-start | bytes 98312 | tf_op jit(solution)/shard_map/ppermute | solution.py:79
  93.3 5.7 %collective-permute-start.3 = (bf16[4,8192]{1,0:T(4,128)(2,1)S(1)}, bf16[4,8192]{1,0:T(4,128)(2,1)S(1)}, u32[]{:S(2)}, u32[]{:S(2)}) collective-permute-start(bf16[4,8192]{1,0:T(4,128)(2,1)S(1)} %pad_maximum_fusion.3), channel_id=1, source_target_pairs={{0,8},{1,9},{2,10},{3,11},{4,12},{5,13},{6,14},{7,15},{8,0},{9,1},... | collective-permute-start | bytes 196616 | tf_op jit(solution)/shard_map/ppermute | solution.py:79
  110.1 5.0 %copy-start.1 = (bf16[4,16,8192]{2,1,0:T(8,128)(2,1)S(1)}, bf16[4,16,8192]{2,1,0:T(8,128)(2,1)}, u32[]{:S(2)}) copy-start(bf16[4,16,8192]{2,1,0:T(8,128)(2,1)} %param.22) | copy-start | bytes 3145732
  118.6 2.0 %collective-permute-start.4 = (f32[8,2,8192]{2,1,0:T(2,128)S(1)}, f32[8,2,8192]{2,1,0:T(2,128)S(1)}, u32[]{:S(2)}, u32[]{:S(2)}) collective-permute-start(f32[8,2,8192]{2,1,0:T(2,128)S(1)} %fusion.24), channel_id=1, source_target_pairs={{0,1},{1,0},{2,3},{3,2},{4,5},{5,4},{6,7},{7,6},{8,9},{9,8},{10,11... | collective-permute-start | bytes 1572872 | tf_op jit(solution)/shard_map/ppermute | solution.py:100

commit v2 on v1

--- a/solution.py
+++ b/solution.py
@@ -71,33 +71,68 @@
     return lax.axis_size("pool")
 
 
+def exchange_quads(rows, step):
+    count = pool_size()
+    me = lax.axis_index("pool")
+    parts = [rows] + [
+        lax.ppermute(rows, "pool", [(i, i ^ (k * step)) for i in range(count)]) for k in (1, 2, 3)
+    ]
+    low = (me & step) != 0
+    high = (me & (2 * step)) != 0
+    swapped = [
+        jnp.where(low, parts[1], parts[0]),
+        jnp.where(low, parts[0], parts[1]),
+        jnp.where(low, parts[3], parts[2]),
+        jnp.where(low, parts[2], parts[3]),
+    ]
+    return jnp.concatenate(
+        [
+            jnp.where(high, swapped[2], swapped[0]),
+            jnp.where(high, swapped[3], swapped[1]),
+            jnp.where(high, swapped[0], swapped[2]),
+            jnp.where(high, swapped[1], swapped[3]),
+        ],
+        axis=0,
+    )
+
+
+def exchange_pair(rows, step):
+    count = pool_size()
+    upper = (lax.axis_index("pool") & step) != 0
+    other = lax.ppermute(rows, "pool", [(i, i ^ step) for i in range(count)])
+    return jnp.concatenate([jnp.where(upper, other, rows), jnp.where(upper, rows, other)], axis=0)
+
+
 def gather_rows(rows):
     count = pool_size()
-    me = lax.axis_index("pool")
     step = 4
     while step < count:
-        other = lax.ppermute(rows, "pool", [(i, i ^ step) for i in range(count)])
-        upper = (me & step) != 0
-        first = jnp.where(upper, other, rows)
-        second = jnp.where(upper, rows, other)
-        rows = jnp.concatenate([first, second], axis=0)
-        step *= 2
+        if step * 4 <= count:
+            rows = exchange_quads(rows, step)
+            step *= 4
+        else:
+            rows = exchange_pair(rows, step)
+            step *= 2
     fours = [[4 * k + j for j in range(4)] for k in range(count // 4)]
-    width = rows.shape[-1]
-    rows = lax.all_gather(rows, "pool", axis=0, axis_index_groups=fours)
-    rows = rows.reshape(4, count // 4, -1, width).transpose(1, 0, 2, 3)
-    return rows.reshape(-1, width)
+    return lax.all_gather(rows, "pool", axis=0, axis_index_groups=fours, tiled=True)
+
+
+def pool_blocks(rows):
+    count = pool_size()
+    blocks = rows.reshape(4, count // 4, rows.shape[0] // count, rows.shape[1])
+    return blocks.transpose(1, 0, 2, 3).reshape(count, -1, rows.shape[1])
 
 
 def scatter_sums(partial):
     count = pool_size()
     me = lax.axis_index("pool")
     width = partial.shape[-1]
-    blocks = partial.reshape(count // 2, 2, -1, width)
+    blocks = partial.reshape(2, 2, count // 4, -1, width)
     odd = (me & 1) != 0
     keep = jnp.where(odd, blocks[:, 1], blocks[:, 0])
     give = jnp.where(odd, blocks[:, 0], blocks[:, 1])
     keep = keep + lax.ppermute(give, "pool", [(i, i ^ 1) for i in range(count)])
+    keep = keep.transpose(1, 0, 2, 3).reshape(count // 2, -1, width)
     same_core = [[2 * k + c for k in range(count // 2)] for c in range(2)]
     parts = lax.all_to_all(keep, "pool", 0, 0, tiled=True, axis_index_groups=same_core)
     return jnp.sum(parts, axis=0)
@@ -148,22 +183,24 @@
     bf_zero = jnp.zeros((), jnp.bfloat16)
 
     own_shrunk = owner_shrunk(gathered_rows, query_down_factor, owner_mask)
+    own_shrunk, column_up_factor = lax.optimization_barrier((own_shrunk, column_up_factor))
     spread = jnp.broadcast_to(own_shrunk[None], (count,) + own_shrunk.shape)
     shrunk_q = jnp.sum(
         lax.all_to_all(spread, "pool", 0, 0, tiled=True).astype(jnp.float32), axis=0
     ).astype(jnp.bfloat16)
+    query_base = jnp.dot(gathered_rows, query_weight, preferred_element_type=jnp.float32)
+    keyval_cols = jnp.dot(
+        gathered_rows, key_value_weight, preferred_element_type=jnp.float32
+    ).astype(jnp.bfloat16)
+    query_base, keyval_cols, shrunk_q = lax.optimization_barrier(
+        (query_base, keyval_cols, shrunk_q)
+    )
     picked = jnp.where(slot_table[:, :, None], shrunk_q[:, None, :], bf_zero)
     picked = picked.reshape(request_total, slot_total * ADAPTER_RANK)
     query_delta = jnp.dot(picked, column_up_factor, preferred_element_type=jnp.float32)
-    query_cols = (
-        jnp.dot(gathered_rows, query_weight, preferred_element_type=jnp.float32)
-        + adapter_scale * query_delta
-    ).astype(jnp.bfloat16)
-    keyval_cols = jnp.dot(
-        gathered_rows, key_value_weight, preferred_element_type=jnp.float32
-    ).astype(jnp.bfloat16)
-    both = jnp.concatenate([query_cols, keyval_cols], axis=1)
-    both = lax.all_to_all(both.reshape(count, local_rows, -1), "pool", 0, 0, tiled=True)
+    query_cols = (query_base + adapter_scale * query_delta).astype(jnp.bfloat16)
+    both = pool_blocks(jnp.concatenate([query_cols, keyval_cols], axis=1))
+    both = lax.all_to_all(both, "pool", 0, 0, tiled=True)
     query_rows = both[:, :, :col_width].transpose(1, 0, 2).reshape(local_rows, -1)
     keyval_rows = both[:, :, col_width:].transpose(1, 0, 2).reshape(local_rows, -1)
 

time: 140 us -> 114 us (0.81)
  waiting for transfers between devices: 43.9 us -> 17.8 us
  blocking collectives: 31.4 us -> 39.5 us
  local copies, waits for them, and re-layouts: 14.9 us -> 7.34 us
  matrix products: 19.5 us -> 15.5 us
  starting transfers between devices: 23.8 us -> 27.1 us
    all_to_all x1, waiting for transfers between devices: 20.7 us -> 1.28 us  [body(): column_up_factor = lax.all_to_all(up_blocks, 'pool', 0, 0, tiled=True)]
    ppermute x4 -> x6, waiting for transfers between devices: 11.5 us -> 1.9 us  [exchange_quads(): lax.ppermute(rows, 'pool', [(i, i ^ k * step) for i in range(count)])]
    all_gather x2, blocking collectives: 13.8 us -> 20.5 us  [gather_rows(): lax.all_gather(rows, 'pool', axis=0, axis_index_groups=fours, tiled=True)]
    reshape x7 -> x3, local copies, waits for them, and re-layouts: 6.68 us -> 2.51 us  [the longest x1 1.84 us: scatter_sums(): blocks = partial.reshape(2, 2, count // 4, -1, width)]
    ppermute x4 -> x6, starting transfers between devices: 6.51 us -> 10.2 us  [exchange_quads(): lax.ppermute(rows, 'pool', [(i, i ^ k * step) for i in range(count)])]
    all_to_all x1, starting transfers between devices: 6.81 us -> 3.5 us  [body(): both = lax.all_to_all(both, 'pool', 0, 0, tiled=True)]
    all_to_all x1, waiting for transfers between devices: 3.59 us -> 6.48 us  [body(): lax.all_to_all(spread, 'pool', 0, 0, tiled=True).astype(jnp.float32)]
    all_to_all x1, starting transfers between devices: 4.34 us -> 6.08 us  [body(): column_up_factor = lax.all_to_all(up_blocks, 'pool', 0, 0, tiled=True)]
  transfers between devices with their start and end apart: 8 -> 10, of which waited for: 7 -> 6; matrix products, arithmetic and copies ran while one was open for 6% -> 10% of each run, Pallas kernels for 0% -> 0%
where the time goes in v2:
time: 114 us; the launch traced here: 113 us
  blocking collectives  39.5 us (35%)
  starting transfers between devices  27.1 us (24%)
  waiting for transfers between devices  17.8 us (16%)
  matrix products  15.5 us (14%)
  local copies, waits for them, and re-layouts  7.34 us (6%)
  other arithmetic  5.71 us (5%)
    all_gather x2, blocking collectives, gather_rows(): lax.all_gather(rows, 'pool', axis=0, axis_index_groups=fours, tiled=True)  20.5 us
    all_to_all x1, blocking collectives, scatter_sums(): lax.all_to_all(keep, 'pool', 0, 0, tiled=True, axis_index_groups=same_core)  19.1 us
    ppermute x6, starting transfers between devices, exchange_quads(): lax.ppermute(rows, 'pool', [(i, i ^ k * step) for i in range(count)])  10.2 us
    all_to_all x1, starting transfers between devices, body(): lax.all_to_all(spread, 'pool', 0, 0, tiled=True).astype(jnp.float32)  6.9 us
    all_to_all x1, waiting for transfers between devices, body(): both = lax.all_to_all(both, 'pool', 0, 0, tiled=True)  6.58 us
    all_to_all x1, waiting for transfers between devices, body(): lax.all_to_all(spread, 'pool', 0, 0, tiled=True).astype(jnp.float32)  6.48 us
    all_to_all x1, starting transfers between devices, body(): column_up_factor = lax.all_to_all(up_blocks, 'pool', 0, 0, tiled=True)  6.08 us
    dot_general x1, matrix products, body(): jnp.dot(columns, output_weight, preferred_element_type=jnp.float32)  5.02 us
  transfers between devices with their start and end apart: 10, of which 6 were waited for; matrix products, arithmetic and copies ran while one was open for 10% of the time, Pallas kernels for 0%

profile of v2, /device:TPU:0, one launch (start us, length us, event | category | flops | bytes accessed | tf_op | source)
XLA Modules:
  0.0 113.3 jit_solution(10955632071955814947)
XLA Ops:
  0.0 1.0 fusion.47
  1.1 0.9 fusion.35
  2.1 0.9 fusion.37
  3.1 5.1 %collective-permute-start = (bf16[2,8320]{1,0:T(2,128)(2,1)S(1)}, bf16[2,8320]{1,0:T(2,128)(2,1)S(1)}, u32[]{:S(2)}, u32[]{:S(2)}) collective-permute-start(bf16[2,8320]{1,0:T(2,128)(2,1)S(1)} %pad_maximum_fusion.3), channel_id=1, source_target_pairs={{0,12},{1,13},{2,14},{3,15},{4,8},{5,9},{6,10},{7,11},{8,4},{9,5},... | collective-permute-start | bytes 99848 | tf_op jit(solution)/shard_map/ppermute | solution.py:78
  8.2 0.6 collective-permute-start.2
  8.8 1.6 %copy.74 = bf16[8,8,16,512]{3,2,1,0:T(8,128)(2,1)S(1)} copy(bf16[8,8,16,512]{3,1,2,0:T(8,128)(2,1)} %bitcast.107) | data formatting | bytes 2097152
  10.5 1.6 %copy.61 = bf16[16,4,16,512]{3,2,1,0:T(8,128)(2,1)} copy(bf16[16,4,16,512]{3,0,2,1:T(8,128)(2,1)S(1)} %bitcast_bitcast_fusion) | data formatting | bytes 2097152 | tf_op jit(solution)/shard_map/transpose | solution.py:164
  12.1 6.1 %all-to-all-start = ((bf16[16,4,16,512]{3,2,1,0:T(8,128)(2,1)}), bf16[16,4,16,512]{3,2,1,0:T(8,128)(2,1)S(1)}, u32[]{:S(2)}, u32[]{:S(2)}) async-start(bf16[16,4,16,512]{3,2,1,0:T(8,128)(2,1)} %copy.61), calls=%async_computation | async-start | bytes 2097152 | tf_op jit(solution)/shard_map/all_to_all | solution.py:165
  18.5 14.0 %all_gather.6 = bf16[32,8320]{1,0:T(8,128)(2,1)S(1)} all-gather(bf16[8,8320]{1,0:T(8,128)(2,1)S(1)} %pad_maximum_fusion), channel_id=1, replica_groups={{0,1,2,3},{4,5,6,7},{8,9,10,11},{12,13,14,15},{16,17,18,19},{20,21,22,2..., dimensions={0}, use_global_device_ids=true | all-gather | bytes 665600 | tf_op jit(solution)/shard_map/all_gather | solution.py:117
  32.8 1.6 %fusion.25 = f32[32,64]{0,1:S(1)} fusion(bf16[8192,64]{0,1:T(8,128)(2,1)} %bitcast.118, bf16[32,8320]{1,0:T(8,128)(2,1)S(1)} %all_gather.6), kind=kOutput, calls=%fused_computation.21 | convolution fusion | flops 33554432 | bytes 1605632
  34.9 4.9 %fusion.28 = f32[32,512]{1,0:T(8,128)S(1)} fusion(bf16[8192,512]{1,0:T(8,128)(2,1)} %param.16, bf16[32,8320]{1,0:T(8,128)(2,1)S(1)} %all_gather.6), kind=kOutput, calls=%fused_computation.24 | convolution fusion | flops 268435456 | bytes 8978432 | tf_op jit(solution)/shard_map/dot_general | solution.py:191
  39.8 1.3 %all-to-all-done = bf16[16,4,16,512]{3,2,1,0:T(8,128)(2,1)S(1)} async-done(((bf16[16,4,16,512]{3,2,1,0:T(8,128)(2,1)}), bf16[16,4,16,512]{3,2,1,0:T(8,128)(2,1)S(1)}, u32[]{:S(2)}, u32[]{:S(2)}) %all-to-all-start) | async-done | bytes 1048608 | tf_op jit(solution)/shard_map/all_to_all | solution.py:165
  41.1 0.7 reshape.236
  41.8 6.9 %all-to-all-start.1 = ((bf16[16,2,256]{2,1,0:T(2,128)(2,1)}), bf16[16,2,256]{2,1,0:T(2,128)(2,1)S(1)}, u32[]{:S(2)}, u32[]{:S(2)}) async-start(bf16[16,2,256]{2,1,0:T(2,128)(2,1)} %reshape.236), calls=%async_computation.1 | async-start | bytes 32768 | tf_op jit(solution)/shard_map/all_to_all | solution.py:189
  48.7 6.5 %all-to-all-done.1 = bf16[16,2,256]{2,1,0:T(2,128)(2,1)S(1)} async-done(((bf16[16,2,256]{2,1,0:T(2,128)(2,1)}), bf16[16,2,256]{2,1,0:T(2,128)(2,1)S(1)}, u32[]{:S(2)}, u32[]{:S(2)}) %all-to-all-start.1) | async-done | bytes 16416 | tf_op jit(solution)/shard_map/all_to_all | solution.py:189
  55.8 0.6 copy.62
  56.4 3.5 %all-to-all-start.2 = ((bf16[16,2,640]{2,1,0:T(2,128)(2,1)}), bf16[16,2,640]{2,1,0:T(2,128)(2,1)S(1)}, u32[]{:S(2)}, u32[]{:S(2)}) async-start(bf16[16,2,640]{2,1,0:T(2,128)(2,1)} %bitcast.8), calls=%async_computation.2 | async-start | bytes 81920 | tf_op jit(solution)/shard_map/all_to_all | solution.py:203
  60.0 6.6 %all-to-all-done.2 = bf16[16,2,640]{2,1,0:T(2,128)(2,1)S(1)} async-done(((bf16[16,2,640]{2,1,0:T(2,128)(2,1)}), bf16[16,2,640]{2,1,0:T(2,128)(2,1)S(1)}, u32[]{:S(2)}, u32[]{:S(2)}) %all-to-all-start.2) | async-done | bytes 40992 | tf_op jit(solution)/shard_map/all_to_all | solution.py:203
  66.9 0.7 fusion.57
  68.3 0.5 fusion.22
  68.8 0.5 collective-permute-start.3
  69.3 1.3 %collective-permute-start.4 = (bf16[2,8192]{1,0:T(2,128)(2,1)S(1)}, bf16[2,8192]{1,0:T(2,128)(2,1)S(1)}, u32[]{:S(2)}, u32[]{:S(2)}) collective-permute-start(bf16[2,8192]{1,0:T(2,128)(2,1)S(1)} %bitcast.115), channel_id=1, source_target_pairs={{0,8},{1,9},{2,10},{3,11},{4,12},{5,13},{6,14},{7,15},{8,0},{9,1},... | collective-permute-start | bytes 98312 | tf_op jit(solution)/shard_map/ppermute | solution.py:78
  70.7 2.6 %collective-permute-start.5 = (bf16[2,8192]{1,0:T(2,128)(2,1)S(1)}, bf16[2,8192]{1,0:T(2,128)(2,1)S(1)}, u32[]{:S(2)}, u32[]{:S(2)}) collective-permute-start(bf16[2,8192]{1,0:T(2,128)(2,1)S(1)} %bitcast.116), channel_id=1, source_target_pairs={{0,4},{1,5},{2,6},{3,7},{4,0},{5,1},{6,2},{7,3},{8,12},{9,13},{10,... | collective-permute-start | bytes 98312 | tf_op jit(solution)/shard_map/ppermute | solution.py:78
  73.3 1.3 %collective-permute-done.3 = bf16[2,8192]{1,0:T(2,128)(2,1)S(1)} collective-permute-done((bf16[2,8192]{1,0:T(2,128)(2,1)S(1)}, bf16[2,8192]{1,0:T(2,128)(2,1)S(1)}, u32[]{:S(2)}, u32[]{:S(2)}) %collective-permute-start.3) | collective-permute-done | bytes 32800 | tf_op jit(solution)/shard_map/ppermute | solution.py:78
  74.6 0.6 collective-permute-done.5
  75.5 6.5 %all_gather.7 = bf16[32,8192]{1,0:T(8,128)(2,1)S(1)} all-gather(bf16[8,8192]{1,0:T(8,128)(2,1)S(1)} %pad_maximum_fusion.1), channel_id=1, replica_groups={{0,1,2,3},{4,5,6,7},{8,9,10,11},{12,13,14,15},{16,17,18,19},{20,21,22,2..., dimensions={0}, use_global_device_ids=true | all-gather | bytes 655360 | tf_op jit(solution)/shard_map/all_gather | solution.py:117
  82.5 5.0 %fusion.38 = f32[32,8192]{1,0:T(8,128)S(1)} fusion(bf16[512,8192]{1,0:T(8,128)(2,1)} %param.18, bf16[32,8192]{1,0:T(8,128)(2,1)S(1)} %all_gather.7, s32[]{:T(128)S(6)} %select_n.182), kind=kOutput, calls=%fused_computation.62 | convolution fusion | flops 268435456 | bytes 9469956 | tf_op jit(solution)/shard_map/dot_general | solution.py:216
  87.5 1.3 %fusion.1 = f32[32,8192]{1,0:T(8,128)} fusion(f32[32,8192]{1,0:T(8,128)S(1)} %fusion.38, bf16[4,16,8192]{2,1,0:T(8,128)(2,1)S(1)} %copy-done.3, pred[32,4]{0,1:T(4,128)(4,1)S(1)} %broadcast_compare_fusion, bf16[32,16]{0,1:T(8,128)(2,1)S(1)} %select_reduce_fusion), kind=kOutput, calls=%fused_computation.2 | convolution fusion | flops 34080768 | bytes 3146880 | tf_op jit(solution)/shard_map/dot_general | solution.py:218
  88.8 1.8 %reshape.223 = f32[2,2,4,2,8192]{4,3,2,1,0:T(2,128)S(1)} reshape(f32[32,8192]{1,0:T(8,128)} %fusion.1) | data formatting | bytes 2097152 | tf_op jit(solution)/shard_map/reshape | solution.py:130
  91.5 1.6 %collective-permute-done.6 = f32[2,4,2,8192]{3,2,0,1:T(2,128)S(1)} collective-permute-done((f32[2,4,2,8192]{3,2,0,1:T(2,128)S(1)}, f32[2,4,2,8192]{3,2,0,1:T(2,128)S(1)}, u32[]{:S(2)}, u32[]{:S(2)}) %collective-permute-start.6) | collective-permute-done | bytes 524320 | tf_op jit(solution)/shard_map/ppermute | solution.py:134
  93.4 19.1 %all_to_all.20 = f32[8,2,8192]{2,1,0:T(2,128)S(1)} all-to-all(f32[8,2,8192]{2,1,0:T(2,128)S(1)} %bitcast.106), channel_id=1, replica_groups={{0,2,4,6,8,10,12,14},{1,3,5,7,9,11,13,15},{16,18,20,22,24,26,28,30},{17..., dimensions={0} | all-to-all | bytes 1048576 | tf_op jit(solution)/shard_map/all_to_all | solution.py:137
  112.5 0.8 reduce_sum.75
  (60 shorter events, 4.8 us)
Async XLA Ops:
  0.0 66.9 %copy-start = (bf16[2,512,1024]{2,1,0:T(8,128)(2,1)S(1)}, bf16[2,512,1024]{2,1,0:T(8,128)(2,1)}, u32[]{:S(2)}) copy-start(bf16[2,512,1024]{2,1,0:T(8,128)(2,1)} %param.23) | copy-start | bytes 6291460
  3.1 15.1 %collective-permute-start = (bf16[2,8320]{1,0:T(2,128)(2,1)S(1)}, bf16[2,8320]{1,0:T(2,128)(2,1)S(1)}, u32[]{:S(2)}, u32[]{:S(2)}) collective-permute-start(bf16[2,8320]{1,0:T(2,128)(2,1)S(1)} %pad_maximum_fusion.3), channel_id=1, source_target_pairs={{0,12},{1,13},{2,14},{3,15},{4,8},{5,9},{6,10},{7,11},{8,4},{9,5},... | collective-permute-start | bytes 99848 | tf_op jit(solution)/shard_map/ppermute | solution.py:78
  8.2 10.0 %collective-permute-start.1 = (bf16[2,8320]{1,0:T(2,128)(2,1)S(1)}, bf16[2,8320]{1,0:T(2,128)(2,1)S(1)}, u32[]{:S(2)}, u32[]{:S(2)}) collective-permute-start(bf16[2,8320]{1,0:T(2,128)(2,1)S(1)} %pad_maximum_fusion.3), channel_id=1, source_target_pairs={{0,8},{1,9},{2,10},{3,11},{4,12},{5,13},{6,14},{7,15},{8,0},{9,1},... | collective-permute-start | bytes 99848 | tf_op jit(solution)/shard_map/ppermute | solution.py:78
  8.2 10.0 %collective-permute-start.2 = (bf16[2,8320]{1,0:T(2,128)(2,1)S(1)}, bf16[2,8320]{1,0:T(2,128)(2,1)S(1)}, u32[]{:S(2)}, u32[]{:S(2)}) collective-permute-start(bf16[2,8320]{1,0:T(2,128)(2,1)S(1)} %pad_maximum_fusion.3), channel_id=1, source_target_pairs={{0,4},{1,5},{2,6},{3,7},{4,0},{5,1},{6,2},{7,3},{8,12},{9,13},{10,... | collective-permute-start | bytes 99848 | tf_op jit(solution)/shard_map/ppermute | solution.py:78
  12.1 29.0 %all-to-all-start = ((bf16[16,4,16,512]{3,2,1,0:T(8,128)(2,1)}), bf16[16,4,16,512]{3,2,1,0:T(8,128)(2,1)S(1)}, u32[]{:S(2)}, u32[]{:S(2)}) async-start(bf16[16,4,16,512]{3,2,1,0:T(8,128)(2,1)} %copy.61), calls=%async_computation | async-start | bytes 2097152 | tf_op jit(solution)/shard_map/all_to_all | solution.py:165
  18.2 16.3 %copy-start.1 = (bf16[8192,128]{1,0:T(8,128)(2,1)S(1)}, bf16[8192,128]{1,0:T(8,128)(2,1)}, u32[]{:S(2)}) copy-start(bf16[8192,128]{1,0:T(8,128)(2,1)} %param.17) | copy-start | bytes 6291460
  39.8 20.1 %copy-start.4 = (s32[2]{0:T(128)S(1)}, s32[2]{0:T(128)}, u32[]{:S(2)}) copy-start(s32[2]{0:T(128)} %param.25) | copy-start | bytes 28
  41.8 13.4 %all-to-all-start.1 = ((bf16[16,2,256]{2,1,0:T(2,128)(2,1)}), bf16[16,2,256]{2,1,0:T(2,128)(2,1)S(1)}, u32[]{:S(2)}, u32[]{:S(2)}) async-start(bf16[16,2,256]{2,1,0:T(2,128)(2,1)} %reshape.236), calls=%async_computation.1 | async-start | bytes 32768 | tf_op jit(solution)/shard_map/all_to_all | solution.py:189
  56.4 10.2 %all-to-all-start.2 = ((bf16[16,2,640]{2,1,0:T(2,128)(2,1)}), bf16[16,2,640]{2,1,0:T(2,128)(2,1)S(1)}, u32[]{:S(2)}, u32[]{:S(2)}) async-start(bf16[16,2,640]{2,1,0:T(2,128)(2,1)} %bitcast.8), calls=%async_computation.2 | async-start | bytes 81920 | tf_op jit(solution)/shard_map/all_to_all | solution.py:203
  66.7 1.6 %copy-start.5 = (bf16[2,512,1024]{2,1,0:T(8,128)(2,1)S(1)}, bf16[2,512,1024]{2,1,0:T(8,128)(2,1)}, u32[]{:S(2)}) copy-start(bf16[2,512,1024]{2,1,0:T(8,128)(2,1)} %param.24) | copy-start | bytes 6291460
  68.3 13.7 %copy-start.2 = (bf16[4,8192,16]{1,2,0:T(8,128)(2,1)S(1)}, bf16[4,8192,16]{1,2,0:T(8,128)(2,1)}, u32[]{:S(2)}) copy-start(bf16[4,8192,16]{1,2,0:T(8,128)(2,1)} %param.21) | copy-start | bytes 3145732
  68.8 5.8 %collective-permute-start.3 = (bf16[2,8192]{1,0:T(2,128)(2,1)S(1)}, bf16[2,8192]{1,0:T(2,128)(2,1)S(1)}, u32[]{:S(2)}, u32[]{:S(2)}) collective-permute-start(bf16[2,8192]{1,0:T(2,128)(2,1)S(1)} %bitcast.114), channel_id=1, source_target_pairs={{0,12},{1,13},{2,14},{3,15},{4,8},{5,9},{6,10},{7,11},{8,4},{9,5},... | collective-permute-start | bytes 98312 | tf_op jit(solution)/shard_map/ppermute | solution.py:78
  69.3 5.3 %collective-permute-start.4 = (bf16[2,8192]{1,0:T(2,128)(2,1)S(1)}, bf16[2,8192]{1,0:T(2,128)(2,1)S(1)}, u32[]{:S(2)}, u32[]{:S(2)}) collective-permute-start(bf16[2,8192]{1,0:T(2,128)(2,1)S(1)} %bitcast.115), channel_id=1, source_target_pairs={{0,8},{1,9},{2,10},{3,11},{4,12},{5,13},{6,14},{7,15},{8,0},{9,1},... | collective-permute-start | bytes 98312 | tf_op jit(solution)/shard_map/ppermute | solution.py:78
  70.7 4.5 %collective-permute-start.5 = (bf16[2,8192]{1,0:T(2,128)(2,1)S(1)}, bf16[2,8192]{1,0:T(2,128)(2,1)S(1)}, u32[]{:S(2)}, u32[]{:S(2)}) collective-permute-start(bf16[2,8192]{1,0:T(2,128)(2,1)S(1)} %bitcast.116), channel_id=1, source_target_pairs={{0,4},{1,5},{2,6},{3,7},{4,0},{5,1},{6,2},{7,3},{8,12},{9,13},{10,... | collective-permute-start | bytes 98312 | tf_op jit(solution)/shard_map/ppermute | solution.py:78
  82.5 5.0 %copy-start.3 = (bf16[4,16,8192]{2,1,0:T(8,128)(2,1)S(1)}, bf16[4,16,8192]{2,1,0:T(8,128)(2,1)}, u32[]{:S(2)}) copy-start(bf16[4,16,8192]{2,1,0:T(8,128)(2,1)} %param.22) | copy-start | bytes 3145732
  91.1 2.0 %collective-permute-start.6 = (f32[2,4,2,8192]{3,2,0,1:T(2,128)S(1)}, f32[2,4,2,8192]{3,2,0,1:T(2,128)S(1)}, u32[]{:S(2)}, u32[]{:S(2)}) collective-permute-start(f32[2,4,2,8192]{3,2,0,1:T(2,128)S(1)} %select_bitcast_fusion), channel_id=1, source_target_pairs={{0,1},{1,0},{2,3},{3,2},{4,5},{5,4},{6,7},{7,6},{8,9},{9,8},{10,11... | collective-permute-start | bytes 1572872 | tf_op jit(solution)/shard_map/ppermute | solution.py:134

commit v3 on v2

--- a/solution.py
+++ b/solution.py
@@ -117,25 +117,35 @@
     return lax.all_gather(rows, "pool", axis=0, axis_index_groups=fours, tiled=True)
 
 
-def pool_blocks(rows):
-    count = pool_size()
-    blocks = rows.reshape(4, count // 4, rows.shape[0] // count, rows.shape[1])
-    return blocks.transpose(1, 0, 2, 3).reshape(count, -1, rows.shape[1])
-
-
-def scatter_sums(partial):
-    count = pool_size()
-    me = lax.axis_index("pool")
+def core_halves(partial):
+    count = pool_size()
     width = partial.shape[-1]
     blocks = partial.reshape(2, 2, count // 4, -1, width)
-    odd = (me & 1) != 0
+    odd = (lax.axis_index("pool") & 1) != 0
     keep = jnp.where(odd, blocks[:, 1], blocks[:, 0])
     give = jnp.where(odd, blocks[:, 0], blocks[:, 1])
-    keep = keep + lax.ppermute(give, "pool", [(i, i ^ 1) for i in range(count)])
-    keep = keep.transpose(1, 0, 2, 3).reshape(count // 2, -1, width)
+    return (
+        keep.transpose(1, 0, 2, 3).reshape(count // 2, -1, width),
+        give.transpose(1, 0, 2, 3).reshape(count // 2, -1, width),
+    )
+
+
+def swap_cores(block):
+    count = pool_size()
+    return lax.ppermute(block, "pool", [(i, i ^ 1) for i in range(count)])
+
+
+def exchange_chips(blocks):
+    count = pool_size()
     same_core = [[2 * k + c for k in range(count // 2)] for c in range(2)]
-    parts = lax.all_to_all(keep, "pool", 0, 0, tiled=True, axis_index_groups=same_core)
-    return jnp.sum(parts, axis=0)
+    return lax.all_to_all(blocks, "pool", 0, 0, tiled=True, axis_index_groups=same_core)
+
+
+def pair_columns(kept, received):
+    odd = (lax.axis_index("pool") & 1) != 0
+    return jnp.concatenate(
+        [jnp.where(odd, received, kept), jnp.where(odd, kept, received)], axis=-1
+    )
 
 
 def body(
@@ -157,13 +167,7 @@
     count = pool_size()
     own_slots = query_down_factor.shape[0]
     local_rows = hidden.shape[0]
-    slot_total = adapter_slot.shape[0]
     col_width = query_weight.shape[1]
-
-    up_blocks = query_up_factor.reshape(own_slots, ADAPTER_RANK, count, col_width)
-    up_blocks = up_blocks.transpose(2, 0, 1, 3)
-    column_up_factor = lax.all_to_all(up_blocks, "pool", 0, 0, tiled=True)
-    column_up_factor = column_up_factor.reshape(slot_total * ADAPTER_RANK, col_width)
 
     normalized_input = norm_rows(hidden, gain)
     slot_ids = lookup_slots(request_adapter, adapter_slot)
@@ -175,34 +179,44 @@
     slot_ids = all_digits[:, 0] * 32 + all_digits[:, 1]
     request_total = gathered_rows.shape[0]
 
-    slot_table = slot_ids[:, None] == jnp.arange(slot_total, dtype=jnp.int32)[None, :]
     first_slot = lax.axis_index("pool") * own_slots
     owner_mask = (
         slot_ids[:, None] == first_slot + jnp.arange(own_slots, dtype=jnp.int32)[None, :]
     )
     bf_zero = jnp.zeros((), jnp.bfloat16)
 
-    own_shrunk = owner_shrunk(gathered_rows, query_down_factor, owner_mask)
-    own_shrunk, column_up_factor = lax.optimization_barrier((own_shrunk, column_up_factor))
-    spread = jnp.broadcast_to(own_shrunk[None], (count,) + own_shrunk.shape)
-    shrunk_q = jnp.sum(
-        lax.all_to_all(spread, "pool", 0, 0, tiled=True).astype(jnp.float32), axis=0
-    ).astype(jnp.bfloat16)
-    query_base = jnp.dot(gathered_rows, query_weight, preferred_element_type=jnp.float32)
-    keyval_cols = jnp.dot(
-        gathered_rows, key_value_weight, preferred_element_type=jnp.float32
-    ).astype(jnp.bfloat16)
-    query_base, keyval_cols, shrunk_q = lax.optimization_barrier(
-        (query_base, keyval_cols, shrunk_q)
-    )
-    picked = jnp.where(slot_table[:, :, None], shrunk_q[:, None, :], bf_zero)
-    picked = picked.reshape(request_total, slot_total * ADAPTER_RANK)
-    query_delta = jnp.dot(picked, column_up_factor, preferred_element_type=jnp.float32)
-    query_cols = (query_base + adapter_scale * query_delta).astype(jnp.bfloat16)
-    both = pool_blocks(jnp.concatenate([query_cols, keyval_cols], axis=1))
-    both = lax.all_to_all(both, "pool", 0, 0, tiled=True)
-    query_rows = both[:, :, :col_width].transpose(1, 0, 2).reshape(local_rows, -1)
-    keyval_rows = both[:, :, col_width:].transpose(1, 0, 2).reshape(local_rows, -1)
+    query_shrunk = owner_shrunk(gathered_rows, query_down_factor, owner_mask)
+    lifted_rows = jnp.where(owner_mask[:, :, None], query_shrunk[:, None, :], bf_zero).reshape(
+        request_total, own_slots * ADAPTER_RANK
+    )
+    query_delta = adapter_scale * jnp.dot(
+        lifted_rows,
+        query_up_factor.reshape(own_slots * ADAPTER_RANK, -1),
+        preferred_element_type=jnp.float32,
+    )
+    kept_delta, given_delta = core_halves(query_delta)
+    received_delta = swap_cores(given_delta)
+    base = jnp.concatenate(
+        [
+            jnp.dot(gathered_rows, query_weight, preferred_element_type=jnp.float32),
+            jnp.dot(gathered_rows, key_value_weight, preferred_element_type=jnp.float32),
+        ],
+        axis=1,
+    )
+    kept_base, given_base = core_halves(base)
+    received_base = swap_cores(given_base)
+    pair_query = pair_columns(kept_base[:, :, :col_width], received_base[:, :, :col_width])
+    pair_keyval = pair_columns(kept_base[:, :, col_width:], received_base[:, :, col_width:])
+    pair_delta = kept_delta + received_delta
+    first_column = (lax.axis_index("pool") // 2) * (2 * col_width)
+    there = lax.dynamic_slice_in_dim(pair_delta, first_column, 2 * col_width, 2)
+    pair_delta = lax.dynamic_update_slice_in_dim(pair_delta, there + pair_query, first_column, 2)
+    arrived = exchange_chips(jnp.concatenate([pair_delta, pair_keyval], axis=2))
+    query_width = pair_delta.shape[2]
+    query_rows = jnp.sum(arrived[:, :, :query_width], axis=0).astype(jnp.bfloat16)
+    keyval_rows = arrived[:, :, query_width:].astype(jnp.bfloat16)
+    keyval_rows = keyval_rows.reshape(count // 2, local_rows, 2, -1)
+    keyval_rows = keyval_rows.transpose(1, 0, 2, 3).reshape(local_rows, -1)
 
     attention_output = attend(query_rows, keyval_rows, key_cache, value_cache, lengths)
     every_row = gather_rows(attention_output)
@@ -216,7 +230,9 @@
     partial = jnp.dot(
         columns, output_weight, preferred_element_type=jnp.float32
     ) + adapter_scale * jnp.dot(lifted_rows, up_rows, preferred_element_type=jnp.float32)
-    return scatter_sums(partial).astype(jnp.bfloat16)
+    kept, given = core_halves(partial)
+    arrived = exchange_chips(kept + swap_cores(given))
+    return jnp.sum(arrived, axis=0).astype(jnp.bfloat16)
 
 
 def solution(mesh):

time: 114 us -> 107 us (0.939)
  starting transfers between devices: 27.1 us -> 14.7 us
  waiting for transfers between devices: 17.8 us -> 27.4 us
  blocking collectives: 39.5 us -> 33.1 us
  other arithmetic: 5.71 us -> 8.78 us
  local copies, waits for them, and re-layouts: 7.34 us -> 5.41 us
  matrix products: 15.5 us -> 17.1 us
    all_to_all x3 -> x1, starting transfers between devices: 16.5 us -> 3.54 us  [exchange_chips(): lax.all_to_all(blocks, 'pool', 0, 0, tiled=True, axis_index_groups=same_c...]
    ppermute x6, waiting for transfers between devices: 1.9 us -> 9.03 us  [exchange_quads(): lax.ppermute(rows, 'pool', [(i, i ^ k * step) for i in range(count)])]
    all_gather x2, blocking collectives: 20.5 us -> 14.4 us  [gather_rows(): lax.all_gather(rows, 'pool', axis=0, axis_index_groups=fours, tiled=True)]
    unnamed x18 -> x14, local copies, waits for them, and re-layouts: 2.93 us -> 0.41 us
    transpose x4 -> x0, local copies, waits for them, and re-layouts: 1.67 us -> none  [the longest x2 1.64 us: body(): up_blocks = up_blocks.transpose(2, 0, 1, 3)]
    dot_general x1, matrix products: 0.46 us -> 2.05 us  [body(): jnp.dot(gathered_rows, key_value_weight, preferred_element_type=jnp.float32)]
    ppermute x1 -> x3, waiting for transfers between devices: 1.56 us -> 2.94 us  [swap_cores(): return lax.ppermute(block, 'pool', [(i, i ^ 1) for i in range(count)])]
    slice x1 -> x4, local copies, waits for them, and re-layouts: 0.09 us -> 1.38 us  [the longest x2 1.36 us: core_halves(): keep = jnp.where(odd, blocks[:, 1], blocks[:, 0])]
  transfers between devices with their start and end apart: 10 -> 10, of which waited for: 6 -> 7; matrix products, arithmetic and copies ran while one was open for 10% -> 0% of each run, Pallas kernels for 0% -> 0%
where the time goes in v3:
time: 107 us
  blocking collectives  33.1 us (31%)
  waiting for transfers between devices  27.4 us (26%)
  matrix products  17.1 us (16%)
  starting transfers between devices  14.7 us (14%)
  other arithmetic  8.78 us (8%)
  local copies, waits for them, and re-layouts  5.41 us (5%)
    all_to_all x1, blocking collectives, exchange_chips(): lax.all_to_all(blocks, 'pool', 0, 0, tiled=True, axis_index_groups=same_c...  18.7 us
    all_to_all x1, waiting for transfers between devices, exchange_chips(): lax.all_to_all(blocks, 'pool', 0, 0, tiled=True, axis_index_groups=same_c...  15.5 us
    all_gather x2, blocking collectives, gather_rows(): lax.all_gather(rows, 'pool', axis=0, axis_index_groups=fours, tiled=True)  14.4 us
    ppermute x6, starting transfers between devices, exchange_quads(): lax.ppermute(rows, 'pool', [(i, i ^ k * step) for i in range(count)])  10.1 us
    ppermute x6, waiting for transfers between devices, exchange_quads(): lax.ppermute(rows, 'pool', [(i, i ^ k * step) for i in range(count)])  9.03 us
    dot_general x1, matrix products, body(): jnp.dot(columns, output_weight, preferred_element_type=jnp.float32)  5.02 us
    dot_general x1, matrix products, body(): jnp.dot(gathered_rows, query_weight, preferred_element_type=jnp.float32)  4.9 us
    all_to_all x1, starting transfers between devices, exchange_chips(): lax.all_to_all(blocks, 'pool', 0, 0, tiled=True, axis_index_groups=same_c...  3.54 us
  transfers between devices with their start and end apart: 10, of which 7 were waited for; matrix products, arithmetic and copies ran while one was open for 0% of the time, Pallas kernels for 0%

profile of v3, /device:TPU:0, one launch (start us, length us, event | category | flops | bytes accessed | tf_op | source)
XLA Modules:
  0.0 106.8 jit_solution(7089458873428014117)
XLA Ops:
  0.0 1.0 fusion.57
  1.1 0.9 fusion.35
  2.1 0.9 fusion.37
  3.1 3.1 %collective-permute-start.2 = (bf16[2,8320]{1,0:T(2,128)(2,1)S(1)}, bf16[2,8320]{1,0:T(2,128)(2,1)S(1)}, u32[]{:S(2)}, u32[]{:S(2)}) collective-permute-start(bf16[2,8320]{1,0:T(2,128)(2,1)S(1)} %pad_maximum_fusion.4), channel_id=1, source_target_pairs={{0,4},{1,5},{2,6},{3,7},{4,0},{5,1},{6,2},{7,3},{8,12},{9,13},{10,... | collective-permute-start | bytes 99848 | tf_op jit(solution)/shard_map/ppermute | solution.py:78
  6.2 2.6 %collective-permute-start.1 = (bf16[2,8320]{1,0:T(2,128)(2,1)S(1)}, bf16[2,8320]{1,0:T(2,128)(2,1)S(1)}, u32[]{:S(2)}, u32[]{:S(2)}) collective-permute-start(bf16[2,8320]{1,0:T(2,128)(2,1)S(1)} %pad_maximum_fusion.4), channel_id=1, source_target_pairs={{0,8},{1,9},{2,10},{3,11},{4,12},{5,13},{6,14},{7,15},{8,0},{9,1},... | collective-permute-start | bytes 99848 | tf_op jit(solution)/shard_map/ppermute | solution.py:78
  8.8 2.8 %collective-permute-done.1 = bf16[2,8320]{1,0:T(2,128)(2,1)S(1)} collective-permute-done((bf16[2,8320]{1,0:T(2,128)(2,1)S(1)}, bf16[2,8320]{1,0:T(2,128)(2,1)S(1)}, u32[]{:S(2)}, u32[]{:S(2)}) %collective-permute-start.1) | collective-permute-done | bytes 33312 | tf_op jit(solution)/shard_map/ppermute | solution.py:78
  11.6 2.9 %collective-permute-done = bf16[2,8320]{1,0:T(2,128)(2,1)S(1)} collective-permute-done((bf16[2,8320]{1,0:T(2,128)(2,1)S(1)}, bf16[2,8320]{1,0:T(2,128)(2,1)S(1)}, u32[]{:S(2)}, u32[]{:S(2)}) %collective-permute-start) | collective-permute-done | bytes 33312 | tf_op jit(solution)/shard_map/ppermute | solution.py:78
  14.8 7.2 %all_gather.6 = bf16[32,8320]{1,0:T(8,128)(2,1)S(1)} all-gather(bf16[8,8320]{1,0:T(8,128)(2,1)S(1)} %pad_maximum_fusion.1), channel_id=1, replica_groups={{0,1,2,3},{4,5,6,7},{8,9,10,11},{12,13,14,15},{16,17,18,19},{20,21,22,2..., dimensions={0}, use_global_device_ids=true | all-gather | bytes 665600 | tf_op jit(solution)/shard_map/all_gather | solution.py:117
  22.0 2.1 %fusion.24 = f32[32,128]{1,0:T(8,128)S(1)} fusion(bf16[8192,128]{1,0:T(8,128)(2,1)} %param.17, bf16[32,8320]{1,0:T(8,128)(2,1)S(1)} %all_gather.6), kind=kOutput, calls=%fused_computation.24 | convolution fusion | flops 67108864 | bytes 2637824 | tf_op jit(solution)/shard_map/dot_general | solution.py:202
  24.7 4.9 %fusion.26 = f32[32,512]{1,0:T(8,128)S(1)} fusion(bf16[8192,512]{1,0:T(8,128)(2,1)} %param.16, bf16[32,8320]{1,0:T(8,128)(2,1)S(1)} %all_gather.6), kind=kOutput, calls=%fused_computation.26 | convolution fusion | flops 268435456 | bytes 8978432 | tf_op jit(solution)/shard_map/dot_general | solution.py:201
  29.8 1.6 %fusion.2 = f32[32,8192]{1,0:T(8,128)S(1)} fusion(bf16[4,16,8192]{2,1,0:T(8,128)(2,1)} %param.20, pred[32,4]{0,1:T(4,128)(4,1)S(1)} %broadcast_compare_fusion, bf16[32,16]{0,1:T(8,128)(2,1)S(1)} %select_reduce_fusion.1), kind=kOutput, calls=%fused_computation.4 | convolution fusion | flops 33818624 | bytes 2098304 | tf_op jit(solution)/shard_map/dot_general | solution.py:192
  31.4 1.6 %reshape.214 = f32[2,2,4,2,8192]{4,3,2,1,0:T(2,128)} reshape(f32[32,8192]{1,0:T(8,128)S(1)} %fusion.2) | data formatting | bytes 2097152 | tf_op jit(solution)/shard_map/reshape | solution.py:123
  33.0 1.3 %fusion.68 = (f32[2,1,4,2,8192]{4,3,2,1,0:T(2,128)S(1)}, f32[2,1,4,2,8192]{4,3,2,1,0:T(2,128)S(1)}) fusion(f32[2,2,4,2,8192]{4,3,2,1,0:T(2,128)} %reshape.214), kind=kLoop, calls=%fused_computation.126 | loop fusion | bytes 2097152 | tf_op jit(solution)/shard_map/slice | solution.py:125
  35.4 1.3 %collective-permute-done.4 = f32[8,2,640]{2,1,0:T(2,128)S(1)} collective-permute-done((f32[8,2,640]{2,1,0:T(2,128)S(1)}, f32[8,2,640]{2,1,0:T(2,128)S(1)}, u32[]{:S(2)}, u32[]{:S(2)}) %collective-permute-start.4) | collective-permute-done | bytes 40992 | tf_op jit(solution)/shard_map/ppermute | solution.py:135
  36.8 1.3 %bitcast_add_fusion.1 = f32[8,2,8192]{2,1,0:T(2,128)S(1)} fusion(f32[8,2,8192]{2,1,0:T(2,128)} %collective-permute-done.3, f32[2,1,4,2,8192]{4,3,0,2,1:T(2,128)S(1)} %get-tuple-element.9), kind=kLoop, calls=%fused_computation.19 | loop fusion | flops 131072 | bytes 1572864 | tf_op jit(solution)/shard_map/add | solution.py:210
  38.2 1.0 pad_maximum_fusion
  39.2 3.5 %all-to-all-start = ((f32[8,2,8448]{2,1,0:T(2,128)}), f32[8,2,8448]{2,1,0:T(2,128)S(1)}, u32[]{:S(2)}, u32[]{:S(2)}) async-start(f32[8,2,8448]{2,1,0:T(2,128)} %pad_maximum_fusion), calls=%async_computation | async-start | bytes 1081344 | tf_op jit(solution)/shard_map/all_to_all | solution.py:141
  42.8 15.5 %all-to-all-done = f32[8,2,8448]{2,1,0:T(2,128)S(1)} async-done(((f32[8,2,8448]{2,1,0:T(2,128)}), f32[8,2,8448]{2,1,0:T(2,128)S(1)}, u32[]{:S(2)}, u32[]{:S(2)}) %all-to-all-start) | async-done | bytes 540704 | tf_op jit(solution)/shard_map/all_to_all | solution.py:141
  58.7 0.7 fusion.70
  60.0 0.5 fusion.21
  60.5 0.7 collective-permute-start.7
  61.2 1.4 %collective-permute-start.6 = (bf16[2,8192]{1,0:T(2,128)(2,1)S(1)}, bf16[2,8192]{1,0:T(2,128)(2,1)S(1)}, u32[]{:S(2)}, u32[]{:S(2)}) collective-permute-start(bf16[2,8192]{1,0:T(2,128)(2,1)S(1)} %bitcast.134), channel_id=1, source_target_pairs={{0,8},{1,9},{2,10},{3,11},{4,12},{5,13},{6,14},{7,15},{8,0},{9,1},... | collective-permute-start | bytes 98312 | tf_op jit(solution)/shard_map/ppermute | solution.py:78
  62.6 2.4 %collective-permute-start.5 = (bf16[2,8192]{1,0:T(2,128)(2,1)S(1)}, bf16[2,8192]{1,0:T(2,128)(2,1)S(1)}, u32[]{:S(2)}, u32[]{:S(2)}) collective-permute-start(bf16[2,8192]{1,0:T(2,128)(2,1)S(1)} %bitcast.135), channel_id=1, source_target_pairs={{0,12},{1,13},{2,14},{3,15},{4,8},{5,9},{6,10},{7,11},{8,4},{9,5},... | collective-permute-start | bytes 98312 | tf_op jit(solution)/shard_map/ppermute | solution.py:78
  65.0 1.0 collective-permute-done.6
  66.0 2.3 %collective-permute-done.5 = bf16[2,8192]{1,0:T(2,128)(2,1)S(1)} collective-permute-done((bf16[2,8192]{1,0:T(2,128)(2,1)S(1)}, bf16[2,8192]{1,0:T(2,128)(2,1)S(1)}, u32[]{:S(2)}, u32[]{:S(2)}) %collective-permute-start.5) | collective-permute-done | bytes 32800 | tf_op jit(solution)/shard_map/ppermute | solution.py:78
  68.6 7.1 %all_gather.7 = bf16[32,8192]{1,0:T(8,128)(2,1)S(1)} all-gather(bf16[8,8192]{1,0:T(8,128)(2,1)S(1)} %pad_maximum_fusion.2), channel_id=1, replica_groups={{0,1,2,3},{4,5,6,7},{8,9,10,11},{12,13,14,15},{16,17,18,19},{20,21,22,2..., dimensions={0}, use_global_device_ids=true | all-gather | bytes 655360 | tf_op jit(solution)/shard_map/all_gather | solution.py:117
  76.3 5.0 %fusion.42 = f32[32,8192]{1,0:T(8,128)S(1)} fusion(bf16[512,8192]{1,0:T(8,128)(2,1)} %param.18, bf16[32,8192]{1,0:T(8,128)(2,1)S(1)} %all_gather.7, s32[]{:T(128)S(6)} %select_n.257), kind=kOutput, calls=%fused_computation.71 | convolution fusion | flops 268435456 | bytes 9469956 | tf_op jit(solution)/shard_map/dot_general | solution.py:230
  81.3 1.3 %fusion.1 = f32[32,8192]{1,0:T(8,128)} fusion(f32[32,8192]{1,0:T(8,128)S(1)} %fusion.42, bf16[4,16,8192]{2,1,0:T(8,128)(2,1)S(1)} %copy-done.2, pred[32,4]{0,1:T(4,128)(4,1)S(1)} %broadcast_compare_fusion, bf16[32,16]{0,1:T(8,128)(2,1)S(1)} %select_reduce_fusion), kind=kOutput, calls=%fused_computation.2 | convolution fusion | flops 34080768 | bytes 3146880 | tf_op jit(solution)/shard_map/dot_general | solution.py:232
  82.6 1.8 %reshape.225 = f32[2,2,4,2,8192]{4,3,2,1,0:T(2,128)S(1)} reshape(f32[32,8192]{1,0:T(8,128)} %fusion.1) | data formatting | bytes 2097152 | tf_op jit(solution)/shard_map/reshape | solution.py:123
  85.4 1.6 %collective-permute-done.8 = f32[8,2,8192]{2,1,0:T(2,128)S(1)} collective-permute-done((f32[8,2,8192]{2,1,0:T(2,128)S(1)}, f32[8,2,8192]{2,1,0:T(2,128)S(1)}, u32[]{:S(2)}, u32[]{:S(2)}) %collective-permute-start.8) | collective-permute-done | bytes 524320 | tf_op jit(solution)/shard_map/ppermute | solution.py:135
  87.3 18.7 %all_to_all.10 = f32[8,2,8192]{2,1,0:T(2,128)S(1)} all-to-all(f32[8,2,8192]{2,1,0:T(2,128)S(1)} %bitcast_add_fusion), channel_id=1, replica_groups={{0,2,4,6,8,10,12,14},{1,3,5,7,9,11,13,15},{16,18,20,22,24,26,28,30},{17..., dimensions={0} | all-to-all | bytes 1048576 | tf_op jit(solution)/shard_map/all_to_all | solution.py:141
  106.0 0.8 reduce_sum.72
  (61 shorter events, 5.6 us)
Async XLA Ops:
  0.0 58.7 %copy-start = (bf16[2,512,1024]{2,1,0:T(8,128)(2,1)S(1)}, bf16[2,512,1024]{2,1,0:T(8,128)(2,1)}, u32[]{:S(2)}) copy-start(bf16[2,512,1024]{2,1,0:T(8,128)(2,1)} %param.23) | copy-start | bytes 6291460
  3.1 5.7 %collective-permute-start.2 = (bf16[2,8320]{1,0:T(2,128)(2,1)S(1)}, bf16[2,8320]{1,0:T(2,128)(2,1)S(1)}, u32[]{:S(2)}, u32[]{:S(2)}) collective-permute-start(bf16[2,8320]{1,0:T(2,128)(2,1)S(1)} %pad_maximum_fusion.4), channel_id=1, source_target_pairs={{0,4},{1,5},{2,6},{3,7},{4,0},{5,1},{6,2},{7,3},{8,12},{9,13},{10,... | collective-permute-start | bytes 99848 | tf_op jit(solution)/shard_map/ppermute | solution.py:78
  6.2 5.4 %collective-permute-start.1 = (bf16[2,8320]{1,0:T(2,128)(2,1)S(1)}, bf16[2,8320]{1,0:T(2,128)(2,1)S(1)}, u32[]{:S(2)}, u32[]{:S(2)}) collective-permute-start(bf16[2,8320]{1,0:T(2,128)(2,1)S(1)} %pad_maximum_fusion.4), channel_id=1, source_target_pairs={{0,8},{1,9},{2,10},{3,11},{4,12},{5,13},{6,14},{7,15},{8,0},{9,1},... | collective-permute-start | bytes 99848 | tf_op jit(solution)/shard_map/ppermute | solution.py:78
  8.7 5.7 %collective-permute-start = (bf16[2,8320]{1,0:T(2,128)(2,1)S(1)}, bf16[2,8320]{1,0:T(2,128)(2,1)S(1)}, u32[]{:S(2)}, u32[]{:S(2)}) collective-permute-start(bf16[2,8320]{1,0:T(2,128)(2,1)S(1)} %pad_maximum_fusion.4), channel_id=1, source_target_pairs={{0,12},{1,13},{2,14},{3,15},{4,8},{5,9},{6,10},{7,11},{8,4},{9,5},... | collective-permute-start | bytes 99848 | tf_op jit(solution)/shard_map/ppermute | solution.py:78
  8.8 15.5 %copy-start.5 = (bf16[4,8192,16]{1,2,0:T(8,128)(2,1)S(1)}, bf16[4,8192,16]{1,2,0:T(8,128)(2,1)}, u32[]{:S(2)}) copy-start(bf16[4,8192,16]{1,2,0:T(8,128)(2,1)} %param.19) | copy-start | bytes 3145732
  34.7 2.1 %collective-permute-start.3 = (f32[8,2,8192]{2,1,0:T(2,128)S(1)}, f32[8,2,8192]{2,1,0:T(2,128)}, u32[]{:S(2)}, u32[]{:S(2)}) collective-permute-start(f32[8,2,8192]{2,1,0:T(2,128)S(1)} %bitcast.122), channel_id=1, source_target_pairs={{0,1},{1,0},{2,3},{3,2},{4,5},{5,4},{6,7},{7,6},{8,9},{9,8},{10,11... | collective-permute-start | bytes 1572872 | tf_op jit(solution)/shard_map/ppermute | solution.py:135
  35.1 7.6 %copy-start.3 = (s32[2]{0:T(128)S(1)}, s32[2]{0:T(128)}, u32[]{:S(2)}) copy-start(s32[2]{0:T(128)} %param.25) | copy-start | bytes 28
  35.1 1.6 %collective-permute-start.4 = (f32[8,2,640]{2,1,0:T(2,128)S(1)}, f32[8,2,640]{2,1,0:T(2,128)S(1)}, u32[]{:S(2)}, u32[]{:S(2)}) collective-permute-start(f32[8,2,640]{2,1,0:T(2,128)S(1)} %bitcast.129), channel_id=1, source_target_pairs={{0,1},{1,0},{2,3},{3,2},{4,5},{5,4},{6,7},{7,6},{8,9},{9,8},{10,11... | collective-permute-start | bytes 122888 | tf_op jit(solution)/shard_map/ppermute | solution.py:135
  39.2 19.1 %all-to-all-start = ((f32[8,2,8448]{2,1,0:T(2,128)}), f32[8,2,8448]{2,1,0:T(2,128)S(1)}, u32[]{:S(2)}, u32[]{:S(2)}) async-start(f32[8,2,8448]{2,1,0:T(2,128)} %pad_maximum_fusion), calls=%async_computation | async-start | bytes 1081344 | tf_op jit(solution)/shard_map/all_to_all | solution.py:141
  58.4 1.6 %copy-start.4 = (bf16[2,512,1024]{2,1,0:T(8,128)(2,1)S(1)}, bf16[2,512,1024]{2,1,0:T(8,128)(2,1)}, u32[]{:S(2)}) copy-start(bf16[2,512,1024]{2,1,0:T(8,128)(2,1)} %param.24) | copy-start | bytes 6291460
  60.0 15.8 %copy-start.1 = (bf16[4,8192,16]{1,2,0:T(8,128)(2,1)S(1)}, bf16[4,8192,16]{1,2,0:T(8,128)(2,1)}, u32[]{:S(2)}) copy-start(bf16[4,8192,16]{1,2,0:T(8,128)(2,1)} %param.21) | copy-start | bytes 3145732
  60.5 4.5 %collective-permute-start.7 = (bf16[2,8192]{1,0:T(2,128)(2,1)S(1)}, bf16[2,8192]{1,0:T(2,128)(2,1)S(1)}, u32[]{:S(2)}, u32[]{:S(2)}) collective-permute-start(bf16[2,8192]{1,0:T(2,128)(2,1)S(1)} %bitcast.133), channel_id=1, source_target_pairs={{0,4},{1,5},{2,6},{3,7},{4,0},{5,1},{6,2},{7,3},{8,12},{9,13},{10,... | collective-permute-start | bytes 98312 | tf_op jit(solution)/shard_map/ppermute | solution.py:78
  61.2 4.8 %collective-permute-start.6 = (bf16[2,8192]{1,0:T(2,128)(2,1)S(1)}, bf16[2,8192]{1,0:T(2,128)(2,1)S(1)}, u32[]{:S(2)}, u32[]{:S(2)}) collective-permute-start(bf16[2,8192]{1,0:T(2,128)(2,1)S(1)} %bitcast.134), channel_id=1, source_target_pairs={{0,8},{1,9},{2,10},{3,11},{4,12},{5,13},{6,14},{7,15},{8,0},{9,1},... | collective-permute-start | bytes 98312 | tf_op jit(solution)/shard_map/ppermute | solution.py:78
  62.6 5.7 %collective-permute-start.5 = (bf16[2,8192]{1,0:T(2,128)(2,1)S(1)}, bf16[2,8192]{1,0:T(2,128)(2,1)S(1)}, u32[]{:S(2)}, u32[]{:S(2)}) collective-permute-start(bf16[2,8192]{1,0:T(2,128)(2,1)S(1)} %bitcast.135), channel_id=1, source_target_pairs={{0,12},{1,13},{2,14},{3,15},{4,8},{5,9},{6,10},{7,11},{8,4},{9,5},... | collective-permute-start | bytes 98312 | tf_op jit(solution)/shard_map/ppermute | solution.py:78
  76.2 5.0 %copy-start.2 = (bf16[4,16,8192]{2,1,0:T(8,128)(2,1)S(1)}, bf16[4,16,8192]{2,1,0:T(8,128)(2,1)}, u32[]{:S(2)}) copy-start(bf16[4,16,8192]{2,1,0:T(8,128)(2,1)} %param.22) | copy-start | bytes 3145732
  85.0 2.0 %collective-permute-start.8 = (f32[8,2,8192]{2,1,0:T(2,128)S(1)}, f32[8,2,8192]{2,1,0:T(2,128)S(1)}, u32[]{:S(2)}, u32[]{:S(2)}) collective-permute-start(f32[8,2,8192]{2,1,0:T(2,128)S(1)} %bitcast.123), channel_id=1, source_target_pairs={{0,1},{1,0},{2,3},{3,2},{4,5},{5,4},{6,7},{7,6},{8,9},{9,8},{10,11... | collective-permute-start | bytes 1572872 | tf_op jit(solution)/shard_map/ppermute | solution.py:135

commit v4 on v3

--- a/solution.py
+++ b/solution.py
@@ -1,6 +1,8 @@
 import jax
 import jax.numpy as jnp
 from jax import lax
+from jax.experimental import pallas as pl
+from jax.experimental.pallas import tpu as pltpu
 from jax.sharding import PartitionSpec as P
 
 MODEL_WIDTH = 8192
@@ -148,6 +150,203 @@
     )
 
 
+CHUNKS = 8
+LANES = 128
+KERNEL_VMEM = 52 * 1024 * 1024
+
+
+def whole_block(shape):
+    return pl.BlockSpec(shape, lambda: (0,) * len(shape))
+
+
+def own_lift(rows_ref, down_ref, marks_ref, first_slot):
+    ranks = down_ref.shape[0]
+    width = down_ref.shape[1]
+    step = width // CHUNKS
+    total = None
+    for k in range(CHUNKS):
+        part = lax.dot_general(
+            rows_ref[:, k * step : (k + 1) * step],
+            down_ref[:, k * step : (k + 1) * step],
+            (((1,), (1,)), ((), ())),
+            preferred_element_type=jnp.float32,
+        )
+        total = part if total is None else total + part
+    marks = marks_ref[...].astype(jnp.float32)
+    slots = (marks[:, 0:1] * 32.0 + marks[:, 1:2]).astype(jnp.int32)
+    place = lax.broadcasted_iota(jnp.int32, total.shape, 1) // ADAPTER_RANK + first_slot
+    return jnp.where(slots == place, total, 0.0).astype(jnp.bfloat16)
+
+
+def split_store(values, odd, kept_ref, given_ref, first, add):
+    width = values.shape[1]
+    size = values.shape[0] // 4
+    local = kept_ref.shape[1]
+    spot = pl.ds(first, width)
+    for y in range(2):
+        even_rows = values[2 * y * size : (2 * y + 1) * size]
+        odd_rows = values[(2 * y + 1) * size : (2 * y + 2) * size]
+        kept = jnp.where(odd, odd_rows, even_rows)
+        given = jnp.where(odd, even_rows, odd_rows)
+        for z in range(size // local):
+            k = 2 * z + y
+            kept_piece = kept[z * local : (z + 1) * local]
+            given_piece = given[z * local : (z + 1) * local]
+            if add:
+                kept_piece = kept_piece + kept_ref[k, :, spot]
+                given_piece = given_piece + given_ref[k, :, spot]
+            kept_ref[k, :, spot] = kept_piece
+            given_ref[k, :, spot] = given_piece
+
+
+def query_kernel(
+    where_ref, rows_ref, marks_ref, query_hbm, keyval_hbm, down_hbm, up_hbm,
+    kept_ref, given_ref, query_vmem, keyval_vmem, down_vmem, up_vmem, sems,
+):
+    me = where_ref[0]
+    odd = (me % 2) == 1
+    width = down_vmem.shape[1]
+    step = width // CHUNKS
+    down_copy = pltpu.make_async_copy(down_hbm, down_vmem, sems.at[CHUNKS])
+    up_copy = pltpu.make_async_copy(up_hbm, up_vmem, sems.at[CHUNKS + 1])
+    keyval_copy = pltpu.make_async_copy(keyval_hbm, keyval_vmem, sems.at[CHUNKS + 2])
+    query_copies = [
+        pltpu.make_async_copy(
+            query_hbm.at[pl.ds(k * step, step)], query_vmem.at[pl.ds(k * step, step)], sems.at[k]
+        )
+        for k in range(CHUNKS)
+    ]
+    down_copy.start()
+    up_copy.start()
+    for copy in query_copies:
+        copy.start()
+    keyval_copy.start()
+    down_copy.wait()
+    lifted = own_lift(rows_ref, down_vmem, marks_ref, where_ref[1])
+    up_copy.wait()
+    for k in range(CHUNKS):
+        spot = slice(k * step, (k + 1) * step)
+        delta = adapter_scale * jnp.dot(
+            lifted, up_vmem[:, spot], preferred_element_type=jnp.float32
+        )
+        split_store(delta, odd, kept_ref, given_ref, k * step, False)
+    query = None
+    for k in range(CHUNKS):
+        spot = slice(k * step, (k + 1) * step)
+        query_copies[k].wait()
+        part = jnp.dot(rows_ref[:, spot], query_vmem[spot], preferred_element_type=jnp.float32)
+        query = part if query is None else query + part
+    columns = query.shape[1]
+    split_store(
+        query, odd, kept_ref, given_ref, pl.multiple_of(me * columns, LANES), True
+    )
+    keyval_copy.wait()
+    keyval = None
+    for k in range(CHUNKS):
+        spot = slice(k * step, (k + 1) * step)
+        part = jnp.dot(rows_ref[:, spot], keyval_vmem[spot], preferred_element_type=jnp.float32)
+        keyval = part if keyval is None else keyval + part
+    none = jnp.zeros_like(keyval)
+    both = jnp.concatenate([jnp.where(odd, none, keyval), jnp.where(odd, keyval, none)], axis=1)
+    split_store(both, odd, kept_ref, given_ref, width, False)
+
+
+def query_halves(where, gathered, query_weight, key_value_weight, down, up, count, local_rows):
+    rows = gathered.shape[0]
+    width, columns = query_weight.shape
+    keyval_columns = key_value_weight.shape[1]
+    ranks = down.shape[0]
+    sent = jax.ShapeDtypeStruct(
+        (count // 2, local_rows, width + 2 * keyval_columns), jnp.float32
+    )
+    return pl.pallas_call(
+        query_kernel,
+        in_specs=[
+            pl.BlockSpec(memory_space=pltpu.SMEM),
+            whole_block((rows, width)),
+            whole_block((rows, LANES)),
+        ]
+        + [pl.BlockSpec(memory_space=pl.ANY)] * 4,
+        out_specs=[whole_block(sent.shape)] * 2,
+        out_shape=[sent, sent],
+        scratch_shapes=[
+            pltpu.VMEM((width, columns), jnp.bfloat16),
+            pltpu.VMEM((width, keyval_columns), jnp.bfloat16),
+            pltpu.VMEM((ranks, width), jnp.bfloat16),
+            pltpu.VMEM((ranks, width), jnp.bfloat16),
+            pltpu.SemaphoreType.DMA((CHUNKS + 3,)),
+        ],
+        compiler_params=pltpu.CompilerParams(vmem_limit_bytes=KERNEL_VMEM),
+        name="query_halves",
+    )(where, gathered[:, :width], gathered[:, width:], query_weight, key_value_weight, down, up)
+
+
+def output_kernel(
+    where_ref, rows_ref, marks_ref, output_hbm, down_hbm, up_hbm,
+    kept_ref, given_ref, output_vmem, down_vmem, up_vmem, sems,
+):
+    me = where_ref[0]
+    odd = (me % 2) == 1
+    depth, width = output_vmem.shape
+    step = width // CHUNKS
+    down_copy = pltpu.make_async_copy(down_hbm, down_vmem, sems.at[CHUNKS])
+    up_copy = pltpu.make_async_copy(up_hbm, up_vmem, sems.at[CHUNKS + 1])
+    output_copies = [
+        pltpu.make_async_copy(
+            output_hbm.at[:, pl.ds(k * step, step)],
+            output_vmem.at[:, pl.ds(k * step, step)],
+            sems.at[k],
+        )
+        for k in range(CHUNKS)
+    ]
+    down_copy.start()
+    up_copy.start()
+    for copy in output_copies:
+        copy.start()
+    down_copy.wait()
+    lifted = own_lift(rows_ref, down_vmem, marks_ref, where_ref[1])
+    columns = rows_ref[:, pl.ds(pl.multiple_of(me * depth, LANES), depth)]
+    up_copy.wait()
+    for k in range(CHUNKS):
+        spot = slice(k * step, (k + 1) * step)
+        output_copies[k].wait()
+        part = jnp.dot(columns, output_vmem[:, spot], preferred_element_type=jnp.float32)
+        part = part + adapter_scale * jnp.dot(
+            lifted, up_vmem[:, spot], preferred_element_type=jnp.float32
+        )
+        split_store(part, odd, kept_ref, given_ref, k * step, False)
+
+
+def output_halves(where, every_row, gathered, output_weight, down, up, count, local_rows):
+    rows = every_row.shape[0]
+    depth, width = output_weight.shape
+    ranks = down.shape[0]
+    sent = jax.ShapeDtypeStruct((count // 2, local_rows, width), jnp.float32)
+    return pl.pallas_call(
+        output_kernel,
+        in_specs=[
+            pl.BlockSpec(memory_space=pltpu.SMEM),
+            whole_block((rows, width)),
+            whole_block((rows, LANES)),
+        ]
+        + [pl.BlockSpec(memory_space=pl.ANY)] * 3,
+        out_specs=[whole_block(sent.shape)] * 2,
+        out_shape=[sent, sent],
+        scratch_shapes=[
+            pltpu.VMEM((depth, width), jnp.bfloat16),
+            pltpu.VMEM((ranks, width), jnp.bfloat16),
+            pltpu.VMEM((ranks, width), jnp.bfloat16),
+            pltpu.SemaphoreType.DMA((CHUNKS + 2,)),
+        ],
+        compiler_params=pltpu.CompilerParams(vmem_limit_bytes=KERNEL_VMEM),
+        name="output_halves",
+    )(where, every_row, gathered[:, width:], output_weight, down, up)
+
+
+def by_rank(factor):
+    return factor.transpose(0, 2, 1).reshape(-1, factor.shape[1])
+
+
 def body(
     hidden,
     gain,
@@ -185,34 +384,50 @@
     )
     bf_zero = jnp.zeros((), jnp.bfloat16)
 
-    query_shrunk = owner_shrunk(gathered_rows, query_down_factor, owner_mask)
-    lifted_rows = jnp.where(owner_mask[:, :, None], query_shrunk[:, None, :], bf_zero).reshape(
-        request_total, own_slots * ADAPTER_RANK
-    )
-    query_delta = adapter_scale * jnp.dot(
-        lifted_rows,
-        query_up_factor.reshape(own_slots * ADAPTER_RANK, -1),
-        preferred_element_type=jnp.float32,
-    )
-    kept_delta, given_delta = core_halves(query_delta)
-    received_delta = swap_cores(given_delta)
-    base = jnp.concatenate(
-        [
-            jnp.dot(gathered_rows, query_weight, preferred_element_type=jnp.float32),
-            jnp.dot(gathered_rows, key_value_weight, preferred_element_type=jnp.float32),
-        ],
-        axis=1,
-    )
-    kept_base, given_base = core_halves(base)
-    received_base = swap_cores(given_base)
-    pair_query = pair_columns(kept_base[:, :, :col_width], received_base[:, :, :col_width])
-    pair_keyval = pair_columns(kept_base[:, :, col_width:], received_base[:, :, col_width:])
-    pair_delta = kept_delta + received_delta
-    first_column = (lax.axis_index("pool") // 2) * (2 * col_width)
-    there = lax.dynamic_slice_in_dim(pair_delta, first_column, 2 * col_width, 2)
-    pair_delta = lax.dynamic_update_slice_in_dim(pair_delta, there + pair_query, first_column, 2)
-    arrived = exchange_chips(jnp.concatenate([pair_delta, pair_keyval], axis=2))
-    query_width = pair_delta.shape[2]
+    aligned = col_width % LANES == 0 and key_value_weight.shape[1] % LANES == 0
+    query_width = MODEL_WIDTH
+    if aligned:
+        where = jnp.stack([lax.axis_index("pool"), first_slot]).astype(jnp.int32)
+        kept, given = query_halves(
+            where,
+            gathered,
+            query_weight,
+            key_value_weight,
+            by_rank(query_down_factor),
+            query_up_factor.reshape(own_slots * ADAPTER_RANK, -1),
+            count,
+            local_rows,
+        )
+        leaving = kept + swap_cores(given)
+    else:
+        query_shrunk = owner_shrunk(gathered_rows, query_down_factor, owner_mask)
+        lifted_rows = jnp.where(owner_mask[:, :, None], query_shrunk[:, None, :], bf_zero).reshape(
+            request_total, own_slots * ADAPTER_RANK
+        )
+        query_delta = adapter_scale * jnp.dot(
+            lifted_rows,
+            query_up_factor.reshape(own_slots * ADAPTER_RANK, -1),
+            preferred_element_type=jnp.float32,
+        )
+        kept_delta, given_delta = core_halves(query_delta)
+        received_delta = swap_cores(given_delta)
+        base = jnp.concatenate(
+            [
+                jnp.dot(gathered_rows, query_weight, preferred_element_type=jnp.float32),
+                jnp.dot(gathered_rows, key_value_weight, preferred_element_type=jnp.float32),
+            ],
+            axis=1,
+        )
+        kept_base, given_base = core_halves(base)
+        received_base = swap_cores(given_base)
+        pair_query = pair_columns(kept_base[:, :, :col_width], received_base[:, :, :col_width])
+        pair_keyval = pair_columns(kept_base[:, :, col_width:], received_base[:, :, col_width:])
+        pair_delta = kept_delta + received_delta
+        first_column = (lax.axis_index("pool") // 2) * (2 * col_width)
+        there = lax.dynamic_slice_in_dim(pair_delta, first_column, 2 * col_width, 2)
+        pair_delta = lax.dynamic_update_slice_in_dim(pair_delta, there + pair_query, first_column, 2)
+        leaving = jnp.concatenate([pair_delta, pair_keyval], axis=2)
+    arrived = exchange_chips(leaving)
     query_rows = jnp.sum(arrived[:, :, :query_width], axis=0).astype(jnp.bfloat16)
     keyval_rows = arrived[:, :, query_width:].astype(jnp.bfloat16)
     keyval_rows = keyval_rows.reshape(count // 2, local_rows, 2, -1)
@@ -220,17 +435,29 @@
 
     attention_output = attend(query_rows, keyval_rows, key_cache, value_cache, lengths)
     every_row = gather_rows(attention_output)
-    out_width = output_weight.shape[0]
-    columns = lax.dynamic_slice_in_dim(every_row, lax.axis_index("pool") * out_width, out_width, 1)
-    output_shrunk = owner_shrunk(every_row, output_down_factor, owner_mask)
-    lifted_rows = jnp.where(owner_mask[:, :, None], output_shrunk[:, None, :], bf_zero).reshape(
-        request_total, own_slots * ADAPTER_RANK
-    )
-    up_rows = output_up_factor.reshape(own_slots * ADAPTER_RANK, MODEL_WIDTH)
-    partial = jnp.dot(
-        columns, output_weight, preferred_element_type=jnp.float32
-    ) + adapter_scale * jnp.dot(lifted_rows, up_rows, preferred_element_type=jnp.float32)
-    kept, given = core_halves(partial)
+    if aligned:
+        kept, given = output_halves(
+            where,
+            every_row,
+            gathered,
+            output_weight,
+            by_rank(output_down_factor),
+            output_up_factor.reshape(own_slots * ADAPTER_RANK, -1),
+            count,
+            local_rows,
+        )
+    else:
+        out_width = output_weight.shape[0]
+        columns = lax.dynamic_slice_in_dim(every_row, lax.axis_index("pool") * out_width, out_width, 1)
+        output_shrunk = owner_shrunk(every_row, output_down_factor, owner_mask)
+        lifted_rows = jnp.where(owner_mask[:, :, None], output_shrunk[:, None, :], bf_zero).reshape(
+            request_total, own_slots * ADAPTER_RANK
+        )
+        up_rows = output_up_factor.reshape(own_slots * ADAPTER_RANK, MODEL_WIDTH)
+        partial = jnp.dot(
+            columns, output_weight, preferred_element_type=jnp.float32
+        ) + adapter_scale * jnp.dot(lifted_rows, up_rows, preferred_element_type=jnp.float32)
+        kept, given = core_halves(partial)
     arrived = exchange_chips(kept + swap_cores(given))
     return jnp.sum(arrived, axis=0).astype(jnp.bfloat16)
 

time: 107 us -> 92.5 us (0.86)
  matrix products: 17.1 us -> 1.37 us
  Pallas kernels: 0 us -> 11.5 us
  local copies, waits for them, and re-layouts: 5.41 us -> 0.57 us
  other arithmetic: 8.78 us -> 6.22 us
  waiting for transfers between devices: 27.4 us -> 24.9 us
    dot_general x5 -> x0, matrix products: 14.8 us -> none  [the longest x1 5.02 us: body(): jnp.dot(columns, output_weight, preferred_element_type=jnp.float32)]
    pallas_call x0 -> x2, Pallas kernels: none -> 11.5 us  [the longest x1 6.12 us: query_halves(): pl.pallas_call(query_kernel, in_specs=[pl.BlockSpec(memory_space=pltpu.SM...]
    reshape x3 -> x0, local copies, waits for them, and re-layouts: 3.47 us -> none  [core_halves(): blocks = partial.reshape(2, 2, count // 4, -1, width)]
    ppermute x6, waiting for transfers between devices: 9.03 us -> 6.28 us  [exchange_quads(): lax.ppermute(rows, 'pool', [(i, i ^ k * step) for i in range(count)])]
    slice x3 -> x2, local copies, waits for them, and re-layouts: 1.37 us -> 0.04 us  [the longest x1 0.03 us: query_halves(): gathered[:, :width]]
    ppermute x3 -> x2, waiting for transfers between devices: 2.94 us -> 3.15 us  [swap_cores(): return lax.ppermute(block, 'pool', [(i, i ^ 1) for i in range(count)])]
  transfers between devices with their start and end apart: 10 -> 9, of which waited for: 7 -> 8; matrix products, arithmetic and copies ran while one was open for 0% -> 0% of each run, Pallas kernels for 0% -> 0%
where the time goes in v4:
time: 92.5 us; the launch traced here: 92.1 us
  blocking collectives  32.8 us (35%)
  waiting for transfers between devices  24.9 us (27%)
  starting transfers between devices  14.6 us (16%)
  Pallas kernels  11.5 us (12%)
  other arithmetic  6.22 us (7%)
  matrix products  1.37 us (1%)
    all_to_all x1, blocking collectives, exchange_chips(): lax.all_to_all(blocks, 'pool', 0, 0, tiled=True, axis_index_groups=same_c...  18.4 us
    all_to_all x1, waiting for transfers between devices, exchange_chips(): lax.all_to_all(blocks, 'pool', 0, 0, tiled=True, axis_index_groups=same_c...  15.5 us
    all_gather x2, blocking collectives, gather_rows(): lax.all_gather(rows, 'pool', axis=0, axis_index_groups=fours, tiled=True)  14.4 us
    ppermute x6, starting transfers between devices, exchange_quads(): lax.ppermute(rows, 'pool', [(i, i ^ k * step) for i in range(count)])  10.2 us
    ppermute x6, waiting for transfers between devices, exchange_quads(): lax.ppermute(rows, 'pool', [(i, i ^ k * step) for i in range(count)])  6.28 us
    pallas_call x1, Pallas kernels, query_halves(): pl.pallas_call(query_kernel, in_specs=[pl.BlockSpec(memory_space=pltpu.SM...  6.12 us
    pallas_call x1, Pallas kernels, output_halves(): pl.pallas_call(output_kernel, in_specs=[pl.BlockSpec(memory_space=pltpu.S...  5.33 us
    all_to_all x1, starting transfers between devices, exchange_chips(): lax.all_to_all(blocks, 'pool', 0, 0, tiled=True, axis_index_groups=same_c...  3.54 us
  transfers between devices with their start and end apart: 9, of which 8 were waited for; matrix products, arithmetic and copies ran while one was open for 0% of the time, Pallas kernels for 0%

profile of v4, /device:TPU:0, one launch (start us, length us, event | category | flops | bytes accessed | tf_op | source)
XLA Modules:
  0.0 92.1 jit_solution(7977088282912624443)
XLA Ops:
  0.0 1.0 %fusion.36 = s32[2]{0:T(128)S(1)} fusion(s32[64]{0:T(128)} %param.27, s32[2]{0:T(128)} %param.26), kind=kLoop, calls=%fused_computation.66 | loop fusion | flops 382 | bytes 272 | tf_op jit(solution)/shard_map/reduce_sum | solution.py:30
  1.1 0.9 %fusion.26 = f32[2]{0:T(128)S(1)} fusion(bf16[2,8192]{1,0:T(2,128)(2,1)} %param.14), kind=kLoop, calls=%fused_computation.31 | loop fusion | flops 49150 | bytes 32776 | tf_op jit(solution)/shard_map/reduce_sum | solution.py:23
  2.1 0.9 fusion.28
  3.1 5.1 %collective-permute-start = (bf16[2,8320]{1,0:T(2,128)(2,1)S(1)}, bf16[2,8320]{1,0:T(2,128)(2,1)S(1)}, u32[]{:S(2)}, u32[]{:S(2)}) collective-permute-start(bf16[2,8320]{1,0:T(2,128)(2,1)S(1)} %pad_maximum_fusion.2), channel_id=1, source_target_pairs={{0,12},{1,13},{2,14},{3,15},{4,8},{5,9},{6,10},{7,11},{8,4},{9,5},... | collective-permute-start | bytes 99848 | tf_op jit(solution)/shard_map/ppermute | solution.py:80
  8.2 0.6 collective-permute-start.2
  8.9 1.2 %collective-permute-done = bf16[2,8320]{1,0:T(2,128)(2,1)S(1)} collective-permute-done((bf16[2,8320]{1,0:T(2,128)(2,1)S(1)}, bf16[2,8320]{1,0:T(2,128)(2,1)S(1)}, u32[]{:S(2)}, u32[]{:S(2)}) %collective-permute-start) | collective-permute-done | bytes 33312 | tf_op jit(solution)/shard_map/ppermute | solution.py:80
  10.1 2.9 %collective-permute-done.1 = bf16[2,8320]{1,0:T(2,128)(2,1)S(1)} collective-permute-done((bf16[2,8320]{1,0:T(2,128)(2,1)S(1)}, bf16[2,8320]{1,0:T(2,128)(2,1)S(1)}, u32[]{:S(2)}, u32[]{:S(2)}) %collective-permute-start.1) | collective-permute-done | bytes 33312 | tf_op jit(solution)/shard_map/ppermute | solution.py:80
  13.2 0.2 pad_maximum_fusion
  13.3 7.2 %all_gather.6 = bf16[32,8320]{1,0:T(8,128)(2,1)S(1)} all-gather(bf16[8,8320]{1,0:T(8,128)(2,1)S(1)} %pad_maximum_fusion), channel_id=1, replica_groups={{0,1,2,3},{4,5,6,7},{8,9,10,11},{12,13,14,15},{16,17,18,19},{20,21,22,2..., dimensions={0}, use_global_device_ids=true | all-gather | bytes 665600 | tf_op jit(solution)/shard_map/all_gather | solution.py:119
  20.6 6.1 %query_halves.1 = (f32[8,2,8448]{2,1,0:T(2,128)S(1)}, f32[8,2,8448]{2,1,0:T(2,128)S(1)}) custom-call(s32[2]{0:T(128)S(1)} %pad_add_fusion.where_ref, bf16[32,8192]{1,0:T(8,128)(2,1)S(1)} %slice.26.rows_ref, bf16[32,128]{1,0:T(8,128)(2,1)S(1)} %slice.27.marks_ref, bf16[8192,512]{1,0:T(8,128)(2,1)} %query_hbm.1, bf16[8192,128]{1,0:T(8,128)(2,1)} %keyval_hbm.1, ...), custom_call_target="tpu_custom_call" | custom-call | tf_op jit(solution)/shard_map/query_halves/pallas_call | solution.py:262
  26.8 0.4 collective-permute-start.3
  27.2 1.6 %collective-permute-done.3 = f32[8,2,8448]{2,1,0:T(2,128)S(1)} collective-permute-done((f32[8,2,8448]{2,1,0:T(2,128)S(1)}, f32[8,2,8448]{2,1,0:T(2,128)S(1)}, u32[]{:S(2)}, u32[]{:S(2)}) %collective-permute-start.3) | collective-permute-done | bytes 540704 | tf_op jit(solution)/shard_map/ppermute | solution.py:137
  28.8 1.1 %add.45 = f32[8,2,8448]{2,1,0:T(2,128)} add(f32[8,2,8448]{2,1,0:T(2,128)S(1)} %get-tuple-element.9, f32[8,2,8448]{2,1,0:T(2,128)S(1)} %collective-permute-done.3) | non-fusion elementwise | flops 135168 | bytes 1622016 | tf_op jit(solution)/shard_map/add | solution.py:401
  29.8 3.5 %all-to-all-start = ((f32[8,2,8448]{2,1,0:T(2,128)}), f32[8,2,8448]{2,1,0:T(2,128)S(1)}, u32[]{:S(2)}, u32[]{:S(2)}) async-start(f32[8,2,8448]{2,1,0:T(2,128)} %add.45), calls=%async_computation | async-start | bytes 1081344 | tf_op jit(solution)/shard_map/all_to_all | solution.py:143
  33.5 15.5 %all-to-all-done = f32[8,2,8448]{2,1,0:T(2,128)S(1)} async-done(((f32[8,2,8448]{2,1,0:T(2,128)}), f32[8,2,8448]{2,1,0:T(2,128)S(1)}, u32[]{:S(2)}, u32[]{:S(2)}) %all-to-all-start) | async-done | bytes 540704 | tf_op jit(solution)/shard_map/all_to_all | solution.py:143
  49.3 0.7 fusion.43
  50.0 0.2 fusion.21
  50.3 0.3 copy-done.2
  50.6 0.5 fusion.18
  51.2 1.5 %collective-permute-start.4 = (bf16[2,8192]{1,0:T(2,128)(2,1)S(1)}, bf16[2,8192]{1,0:T(2,128)(2,1)S(1)}, u32[]{:S(2)}, u32[]{:S(2)}) collective-permute-start(bf16[2,8192]{1,0:T(2,128)(2,1)S(1)} %bitcast.81), channel_id=1, source_target_pairs={{0,12},{1,13},{2,14},{3,15},{4,8},{5,9},{6,10},{7,11},{8,4},{9,5},... | collective-permute-start | bytes 98312 | tf_op jit(solution)/shard_map/ppermute | solution.py:80
  52.6 0.7 collective-permute-start.5
  53.4 2.3 %collective-permute-start.6 = (bf16[2,8192]{1,0:T(2,128)(2,1)S(1)}, bf16[2,8192]{1,0:T(2,128)(2,1)S(1)}, u32[]{:S(2)}, u32[]{:S(2)}) collective-permute-start(bf16[2,8192]{1,0:T(2,128)(2,1)S(1)} %bitcast.83), channel_id=1, source_target_pairs={{0,4},{1,5},{2,6},{3,7},{4,0},{5,1},{6,2},{7,3},{8,12},{9,13},{10,... | collective-permute-start | bytes 98312 | tf_op jit(solution)/shard_map/ppermute | solution.py:80
  55.6 1.3 %collective-permute-done.4 = bf16[2,8192]{1,0:T(2,128)(2,1)S(1)} collective-permute-done((bf16[2,8192]{1,0:T(2,128)(2,1)S(1)}, bf16[2,8192]{1,0:T(2,128)(2,1)S(1)}, u32[]{:S(2)}, u32[]{:S(2)}) %collective-permute-start.4) | collective-permute-done | bytes 32800 | tf_op jit(solution)/shard_map/ppermute | solution.py:80
  56.9 0.7 collective-permute-done.5
  57.9 0.2 pad_maximum_fusion.1
  58.1 7.2 %all_gather.7.rows_ref = bf16[32,8192]{1,0:T(8,128)(2,1)S(1)} all-gather(bf16[8,8192]{1,0:T(8,128)(2,1)S(1)} %pad_maximum_fusion.1), channel_id=1, replica_groups={{0,1,2,3},{4,5,6,7},{8,9,10,11},{12,13,14,15},{16,17,18,19},{20,21,22,2..., dimensions={0}, use_global_device_ids=true | all-gather | bytes 655360 | tf_op jit(solution)/shard_map/all_gather | solution.py:119
  65.3 5.3 %output_halves.1 = (f32[8,2,8192]{2,1,0:T(2,128)S(1)}, f32[8,2,8192]{2,1,0:T(2,128)S(1)}) custom-call(s32[2]{0:T(128)S(1)} %pad_add_fusion.where_ref, bf16[32,8192]{1,0:T(8,128)(2,1)S(1)} %all_gather.7.rows_ref, bf16[32,128]{1,0:T(8,128)(2,1)S(1)} %slice.27.marks_ref, bf16[512,8192]{1,0:T(8,128)(2,1)} %output_hbm.1, bf16[64,8192]{1,0:T(8,128)(2,1)} %bitcast.75, ...), custom_call_target="tpu_custom_call" | custom-call | tf_op jit(solution)/shard_map/output_halves/pallas_call | solution.py:325
  70.6 0.4 collective-permute-start.7
  71.0 1.6 %collective-permute-done.7 = f32[8,2,8192]{2,1,0:T(2,128)S(1)} collective-permute-done((f32[8,2,8192]{2,1,0:T(2,128)S(1)}, f32[8,2,8192]{2,1,0:T(2,128)S(1)}, u32[]{:S(2)}, u32[]{:S(2)}) %collective-permute-start.7) | collective-permute-done | bytes 524320 | tf_op jit(solution)/shard_map/ppermute | solution.py:137
  72.6 0.3 add.48
  72.9 18.4 %all_to_all.10 = f32[8,2,8192]{2,1,0:T(2,128)S(1)} all-to-all(f32[8,2,8192]{2,1,0:T(2,128)S(1)} %add.48), channel_id=1, replica_groups={{0,2,4,6,8,10,12,14},{1,3,5,7,9,11,13,15},{16,18,20,22,24,26,28,30},{17..., dimensions={0} | all-to-all | bytes 1048576 | tf_op jit(solution)/shard_map/all_to_all | solution.py:143
  91.3 0.8 reduce_sum.52
  (31 shorter events, 1.2 us)
Async XLA Ops:
  0.0 49.3 %copy-start = (bf16[2,512,1024]{2,1,0:T(8,128)(2,1)S(1)}, bf16[2,512,1024]{2,1,0:T(8,128)(2,1)}, u32[]{:S(2)}) copy-start(bf16[2,512,1024]{2,1,0:T(8,128)(2,1)} %param.23) | copy-start | bytes 6291460
  3.1 7.0 %collective-permute-start = (bf16[2,8320]{1,0:T(2,128)(2,1)S(1)}, bf16[2,8320]{1,0:T(2,128)(2,1)S(1)}, u32[]{:S(2)}, u32[]{:S(2)}) collective-permute-start(bf16[2,8320]{1,0:T(2,128)(2,1)S(1)} %pad_maximum_fusion.2), channel_id=1, source_target_pairs={{0,12},{1,13},{2,14},{3,15},{4,8},{5,9},{6,10},{7,11},{8,4},{9,5},... | collective-permute-start | bytes 99848 | tf_op jit(solution)/shard_map/ppermute | solution.py:80
  8.2 4.8 %collective-permute-start.1 = (bf16[2,8320]{1,0:T(2,128)(2,1)S(1)}, bf16[2,8320]{1,0:T(2,128)(2,1)S(1)}, u32[]{:S(2)}, u32[]{:S(2)}) collective-permute-start(bf16[2,8320]{1,0:T(2,128)(2,1)S(1)} %pad_maximum_fusion.2), channel_id=1, source_target_pairs={{0,8},{1,9},{2,10},{3,11},{4,12},{5,13},{6,14},{7,15},{8,0},{9,1},... | collective-permute-start | bytes 99848 | tf_op jit(solution)/shard_map/ppermute | solution.py:80
  8.2 4.8 %collective-permute-start.2 = (bf16[2,8320]{1,0:T(2,128)(2,1)S(1)}, bf16[2,8320]{1,0:T(2,128)(2,1)S(1)}, u32[]{:S(2)}, u32[]{:S(2)}) collective-permute-start(bf16[2,8320]{1,0:T(2,128)(2,1)S(1)} %pad_maximum_fusion.2), channel_id=1, source_target_pairs={{0,4},{1,5},{2,6},{3,7},{4,0},{5,1},{6,2},{7,3},{8,12},{9,13},{10,... | collective-permute-start | bytes 99848 | tf_op jit(solution)/shard_map/ppermute | solution.py:80
  26.7 6.6 %copy-start.1 = (s32[2]{0:T(128)S(1)}, s32[2]{0:T(128)}, u32[]{:S(2)}) copy-start(s32[2]{0:T(128)} %param.25) | copy-start | bytes 28
  26.8 2.0 %collective-permute-start.3 = (f32[8,2,8448]{2,1,0:T(2,128)S(1)}, f32[8,2,8448]{2,1,0:T(2,128)S(1)}, u32[]{:S(2)}, u32[]{:S(2)}) collective-permute-start(f32[8,2,8448]{2,1,0:T(2,128)S(1)} %get-tuple-element.10), channel_id=1, source_target_pairs={{0,1},{1,0},{2,3},{3,2},{4,5},{5,4},{6,7},{7,6},{8,9},{9,8},{10,11... | collective-permute-start | bytes 1622024 | tf_op jit(solution)/shard_map/ppermute | solution.py:137
  29.8 19.1 %all-to-all-start = ((f32[8,2,8448]{2,1,0:T(2,128)}), f32[8,2,8448]{2,1,0:T(2,128)S(1)}, u32[]{:S(2)}, u32[]{:S(2)}) async-start(f32[8,2,8448]{2,1,0:T(2,128)} %add.45), calls=%async_computation | async-start | bytes 1081344 | tf_op jit(solution)/shard_map/all_to_all | solution.py:143
  49.0 1.6 %copy-start.2 = (bf16[2,512,1024]{2,1,0:T(8,128)(2,1)S(1)}, bf16[2,512,1024]{2,1,0:T(8,128)(2,1)}, u32[]{:S(2)}) copy-start(bf16[2,512,1024]{2,1,0:T(8,128)(2,1)} %param.24) | copy-start | bytes 6291460
  51.2 5.8 %collective-permute-start.4 = (bf16[2,8192]{1,0:T(2,128)(2,1)S(1)}, bf16[2,8192]{1,0:T(2,128)(2,1)S(1)}, u32[]{:S(2)}, u32[]{:S(2)}) collective-permute-start(bf16[2,8192]{1,0:T(2,128)(2,1)S(1)} %bitcast.81), channel_id=1, source_target_pairs={{0,12},{1,13},{2,14},{3,15},{4,8},{5,9},{6,10},{7,11},{8,4},{9,5},... | collective-permute-start | bytes 98312 | tf_op jit(solution)/shard_map/ppermute | solution.py:80
  52.6 5.0 %collective-permute-start.5 = (bf16[2,8192]{1,0:T(2,128)(2,1)S(1)}, bf16[2,8192]{1,0:T(2,128)(2,1)S(1)}, u32[]{:S(2)}, u32[]{:S(2)}) collective-permute-start(bf16[2,8192]{1,0:T(2,128)(2,1)S(1)} %bitcast.82), channel_id=1, source_target_pairs={{0,8},{1,9},{2,10},{3,11},{4,12},{5,13},{6,14},{7,15},{8,0},{9,1},... | collective-permute-start | bytes 98312 | tf_op jit(solution)/shard_map/ppermute | solution.py:80
  53.4 4.4 %collective-permute-start.6 = (bf16[2,8192]{1,0:T(2,128)(2,1)S(1)}, bf16[2,8192]{1,0:T(2,128)(2,1)S(1)}, u32[]{:S(2)}, u32[]{:S(2)}) collective-permute-start(bf16[2,8192]{1,0:T(2,128)(2,1)S(1)} %bitcast.83), channel_id=1, source_target_pairs={{0,4},{1,5},{2,6},{3,7},{4,0},{5,1},{6,2},{7,3},{8,12},{9,13},{10,... | collective-permute-start | bytes 98312 | tf_op jit(solution)/shard_map/ppermute | solution.py:80
  70.6 2.0 %collective-permute-start.7 = (f32[8,2,8192]{2,1,0:T(2,128)S(1)}, f32[8,2,8192]{2,1,0:T(2,128)S(1)}, u32[]{:S(2)}, u32[]{:S(2)}) collective-permute-start(f32[8,2,8192]{2,1,0:T(2,128)S(1)} %get-tuple-element.12), channel_id=1, source_target_pairs={{0,1},{1,0},{2,3},{3,2},{4,5},{5,4},{6,7},{7,6},{8,9},{9,8},{10,11... | collective-permute-start | bytes 1572872 | tf_op jit(solution)/shard_map/ppermute | solution.py:137

commit v5 on v4

--- a/solution.py
+++ b/solution.py
@@ -105,9 +105,10 @@
     return jnp.concatenate([jnp.where(upper, other, rows), jnp.where(upper, rows, other)], axis=0)
 
 
-def gather_rows(rows):
+def gather_rows(rows, beside=None):
     count = pool_size()
     step = 4
+    held = None if beside is None else beside(rows)
     while step < count:
         if step * 4 <= count:
             rows = exchange_quads(rows, step)
@@ -115,8 +116,11 @@
         else:
             rows = exchange_pair(rows, step)
             step *= 2
+    if held is not None:
+        rows, held = lax.optimization_barrier((rows, held))
     fours = [[4 * k + j for j in range(4)] for k in range(count // 4)]
-    return lax.all_gather(rows, "pool", axis=0, axis_index_groups=fours, tiled=True)
+    rows = lax.all_gather(rows, "pool", axis=0, axis_index_groups=fours, tiled=True)
+    return rows if beside is None else (rows, held)
 
 
 def core_halves(partial):
@@ -152,7 +156,10 @@
 
 CHUNKS = 8
 LANES = 128
-KERNEL_VMEM = 52 * 1024 * 1024
+KERNEL_VMEM = 24 * 1024 * 1024
+QUERY_BRING_VMEM = 40 * 1024 * 1024
+OUTPUT_VMEM = 44 * 1024 * 1024
+NORM_VMEM = 8 * 1024 * 1024
 
 
 def whole_block(shape):
@@ -200,30 +207,14 @@
 
 
 def query_kernel(
-    where_ref, rows_ref, marks_ref, query_hbm, keyval_hbm, down_hbm, up_hbm,
-    kept_ref, given_ref, query_vmem, keyval_vmem, down_vmem, up_vmem, sems,
+    where_ref, rows_ref, marks_ref, query_vmem, keyval_vmem, down_vmem, up_vmem,
+    kept_ref, given_ref,
 ):
     me = where_ref[0]
     odd = (me % 2) == 1
     width = down_vmem.shape[1]
     step = width // CHUNKS
-    down_copy = pltpu.make_async_copy(down_hbm, down_vmem, sems.at[CHUNKS])
-    up_copy = pltpu.make_async_copy(up_hbm, up_vmem, sems.at[CHUNKS + 1])
-    keyval_copy = pltpu.make_async_copy(keyval_hbm, keyval_vmem, sems.at[CHUNKS + 2])
-    query_copies = [
-        pltpu.make_async_copy(
-            query_hbm.at[pl.ds(k * step, step)], query_vmem.at[pl.ds(k * step, step)], sems.at[k]
-        )
-        for k in range(CHUNKS)
-    ]
-    down_copy.start()
-    up_copy.start()
-    for copy in query_copies:
-        copy.start()
-    keyval_copy.start()
-    down_copy.wait()
     lifted = own_lift(rows_ref, down_vmem, marks_ref, where_ref[1])
-    up_copy.wait()
     for k in range(CHUNKS):
         spot = slice(k * step, (k + 1) * step)
         delta = adapter_scale * jnp.dot(
@@ -233,14 +224,12 @@
     query = None
     for k in range(CHUNKS):
         spot = slice(k * step, (k + 1) * step)
-        query_copies[k].wait()
         part = jnp.dot(rows_ref[:, spot], query_vmem[spot], preferred_element_type=jnp.float32)
         query = part if query is None else query + part
     columns = query.shape[1]
     split_store(
         query, odd, kept_ref, given_ref, pl.multiple_of(me * columns, LANES), True
     )
-    keyval_copy.wait()
     keyval = None
     for k in range(CHUNKS):
         spot = slice(k * step, (k + 1) * step)
@@ -266,58 +255,52 @@
             whole_block((rows, width)),
             whole_block((rows, LANES)),
         ]
-        + [pl.BlockSpec(memory_space=pl.ANY)] * 4,
+        + [pl.BlockSpec(memory_space=pltpu.VMEM)] * 4,
         out_specs=[whole_block(sent.shape)] * 2,
         out_shape=[sent, sent],
-        scratch_shapes=[
-            pltpu.VMEM((width, columns), jnp.bfloat16),
-            pltpu.VMEM((width, keyval_columns), jnp.bfloat16),
-            pltpu.VMEM((ranks, width), jnp.bfloat16),
-            pltpu.VMEM((ranks, width), jnp.bfloat16),
-            pltpu.SemaphoreType.DMA((CHUNKS + 3,)),
-        ],
         compiler_params=pltpu.CompilerParams(vmem_limit_bytes=KERNEL_VMEM),
         name="query_halves",
     )(where, gathered[:, :width], gathered[:, width:], query_weight, key_value_weight, down, up)
 
 
 def output_kernel(
-    where_ref, rows_ref, marks_ref, output_hbm, down_hbm, up_hbm,
-    kept_ref, given_ref, output_vmem, down_vmem, up_vmem, sems,
+    where_ref, rows_ref, marks_ref, near_vmem, output_hbm, down_vmem, up_vmem,
+    kept_ref, given_ref, late_vmem, sems,
 ):
     me = where_ref[0]
     odd = (me % 2) == 1
-    depth, width = output_vmem.shape
+    depth, width = output_hbm.shape
+    near = near_vmem.shape[1]
     step = width // CHUNKS
-    down_copy = pltpu.make_async_copy(down_hbm, down_vmem, sems.at[CHUNKS])
-    up_copy = pltpu.make_async_copy(up_hbm, up_vmem, sems.at[CHUNKS + 1])
-    output_copies = [
+    late = [
         pltpu.make_async_copy(
             output_hbm.at[:, pl.ds(k * step, step)],
-            output_vmem.at[:, pl.ds(k * step, step)],
-            sems.at[k],
-        )
-        for k in range(CHUNKS)
+            late_vmem.at[:, pl.ds(k * step - near, step)],
+            sems.at[k - near // step],
+        )
+        for k in range(near // step, CHUNKS)
     ]
-    down_copy.start()
-    up_copy.start()
-    for copy in output_copies:
+    for copy in late:
         copy.start()
-    down_copy.wait()
     lifted = own_lift(rows_ref, down_vmem, marks_ref, where_ref[1])
     columns = rows_ref[:, pl.ds(pl.multiple_of(me * depth, LANES), depth)]
-    up_copy.wait()
     for k in range(CHUNKS):
         spot = slice(k * step, (k + 1) * step)
-        output_copies[k].wait()
-        part = jnp.dot(columns, output_vmem[:, spot], preferred_element_type=jnp.float32)
+        if k * step < near:
+            weight = near_vmem[:, spot]
+        else:
+            late[k - near // step].wait()
+            weight = late_vmem[:, k * step - near : (k + 1) * step - near]
+        part = jnp.dot(columns, weight, preferred_element_type=jnp.float32)
         part = part + adapter_scale * jnp.dot(
             lifted, up_vmem[:, spot], preferred_element_type=jnp.float32
         )
         split_store(part, odd, kept_ref, given_ref, k * step, False)
 
 
-def output_halves(where, every_row, gathered, output_weight, down, up, count, local_rows):
+def output_halves(
+    where, every_row, gathered, output_near, output_weight, down, up, count, local_rows
+):
     rows = every_row.shape[0]
     depth, width = output_weight.shape
     ranks = down.shape[0]
@@ -329,18 +312,88 @@
             whole_block((rows, width)),
             whole_block((rows, LANES)),
         ]
-        + [pl.BlockSpec(memory_space=pl.ANY)] * 3,
+        + [
+            pl.BlockSpec(memory_space=pltpu.VMEM),
+            pl.BlockSpec(memory_space=pl.ANY),
+            pl.BlockSpec(memory_space=pltpu.VMEM),
+            pl.BlockSpec(memory_space=pltpu.VMEM),
+        ],
         out_specs=[whole_block(sent.shape)] * 2,
         out_shape=[sent, sent],
         scratch_shapes=[
-            pltpu.VMEM((depth, width), jnp.bfloat16),
-            pltpu.VMEM((ranks, width), jnp.bfloat16),
-            pltpu.VMEM((ranks, width), jnp.bfloat16),
-            pltpu.SemaphoreType.DMA((CHUNKS + 2,)),
+            pltpu.VMEM((depth, width - output_near.shape[1]), jnp.bfloat16),
+            pltpu.SemaphoreType.DMA((CHUNKS,)),
         ],
-        compiler_params=pltpu.CompilerParams(vmem_limit_bytes=KERNEL_VMEM),
+        compiler_params=pltpu.CompilerParams(vmem_limit_bytes=OUTPUT_VMEM),
         name="output_halves",
-    )(where, every_row, gathered[:, width:], output_weight, down, up)
+    )(where, every_row, gathered[:, width:], output_near, output_weight, down, up)
+
+
+def bring_kernel(where_ref, source, target, sems):
+    step = source.shape[0] // 4
+    copies = []
+    for k in range(4):
+        spot = pl.ds(k * step, step)
+        copies.append(
+            pltpu.make_async_copy(
+                source.at[spot, pl.ds(0, target.shape[1])], target.at[spot], sems.at[k]
+            )
+        )
+    for copy in copies:
+        copy.start()
+    for copy in copies:
+        copy.wait()
+
+
+def bring(where, weight, columns, vmem):
+    rows = weight.shape[0]
+    return pl.pallas_call(
+        bring_kernel,
+        in_specs=[
+            pl.BlockSpec(memory_space=pltpu.SMEM),
+            pl.BlockSpec(memory_space=pl.ANY),
+        ],
+        out_specs=pl.BlockSpec(memory_space=pltpu.VMEM),
+        out_shape=jax.ShapeDtypeStruct((rows, columns), weight.dtype),
+        scratch_shapes=[pltpu.SemaphoreType.DMA((4,))],
+        compiler_params=pltpu.CompilerParams(vmem_limit_bytes=vmem),
+        cost_estimate=pl.CostEstimate(
+            flops=0, bytes_accessed=4 * rows * columns, transcendentals=0
+        ),
+        name="bring",
+    )(where, weight)
+
+
+def norm_kernel(hidden_ref, gain_ref, adapter_ref, slot_ref, sent_ref):
+    rows, width = hidden_ref.shape
+    values = hidden_ref[...].astype(jnp.float32)
+    factor = lax.rsqrt(jnp.mean(values * values, axis=-1, keepdims=True) + norm_eps)
+    sent_ref[:, :width] = (values * factor * gain_ref[...]).astype(jnp.bfloat16)
+    row = lax.broadcasted_iota(jnp.int32, (rows, LANES), 0)
+    lane = lax.broadcasted_iota(jnp.int32, (rows, LANES), 1)
+    marks = jnp.zeros((rows, LANES), jnp.int32)
+    for r in range(rows):
+        slot = slot_ref[adapter_ref[r]]
+        digit = jnp.where(lane == 0, slot // 32, jnp.where(lane == 1, slot % 32, 0))
+        marks = jnp.where(row == r, digit, marks)
+    sent_ref[:, width:] = marks.astype(jnp.float32).astype(jnp.bfloat16)
+
+
+def norm_and_marks(hidden, gain, request_adapter, adapter_slot):
+    rows, width = hidden.shape
+    return pl.pallas_call(
+        norm_kernel,
+        in_specs=[
+            whole_block(hidden.shape),
+            whole_block((1, width)),
+            pl.BlockSpec(memory_space=pltpu.SMEM),
+            pl.BlockSpec(memory_space=pltpu.SMEM),
+        ],
+        out_specs=whole_block((rows, width + LANES)),
+        out_shape=jax.ShapeDtypeStruct((rows, width + LANES), jnp.bfloat16),
+        compiler_params=pltpu.CompilerParams(vmem_limit_bytes=NORM_VMEM),
+        name="norm_and_marks",
+    )(hidden, gain.reshape(1, width), request_adapter, adapter_slot)
 
 
 def by_rank(factor):
@@ -368,30 +421,41 @@
     local_rows = hidden.shape[0]
     col_width = query_weight.shape[1]
 
-    normalized_input = norm_rows(hidden, gain)
-    slot_ids = lookup_slots(request_adapter, adapter_slot)
-    digits = jnp.stack([slot_ids // 32, slot_ids % 32], axis=1).astype(jnp.bfloat16)
-    sent = jnp.concatenate([normalized_input, jnp.pad(digits, ((0, 0), (0, 126)))], axis=1)
-    gathered = gather_rows(sent)
+    aligned = col_width % LANES == 0 and key_value_weight.shape[1] % LANES == 0
+    if aligned:
+        sent = norm_and_marks(hidden, gain, request_adapter, adapter_slot)
+    else:
+        normalized_input = norm_rows(hidden, gain)
+        slot_ids = lookup_slots(request_adapter, adapter_slot)
+        digits = jnp.stack([slot_ids // 32, slot_ids % 32], axis=1).astype(jnp.bfloat16)
+        sent = jnp.concatenate([normalized_input, jnp.pad(digits, ((0, 0), (0, 126)))], axis=1)
+    first_slot = lax.axis_index("pool") * own_slots
+    where = jnp.stack([lax.axis_index("pool"), first_slot]).astype(jnp.int32)
+    if aligned:
+
+        def bring_query(rows):
+            now, _ = lax.optimization_barrier((where, rows))
+            return bring(now, query_weight, col_width, QUERY_BRING_VMEM)
+
+        gathered, query_near = gather_rows(sent, bring_query)
+    else:
+        gathered = gather_rows(sent)
     gathered_rows = gathered[:, :MODEL_WIDTH]
     all_digits = gathered[:, MODEL_WIDTH : MODEL_WIDTH + 2].astype(jnp.int32)
     slot_ids = all_digits[:, 0] * 32 + all_digits[:, 1]
     request_total = gathered_rows.shape[0]
 
-    first_slot = lax.axis_index("pool") * own_slots
     owner_mask = (
         slot_ids[:, None] == first_slot + jnp.arange(own_slots, dtype=jnp.int32)[None, :]
     )
     bf_zero = jnp.zeros((), jnp.bfloat16)
 
-    aligned = col_width % LANES == 0 and key_value_weight.shape[1] % LANES == 0
     query_width = MODEL_WIDTH
     if aligned:
-        where = jnp.stack([lax.axis_index("pool"), first_slot]).astype(jnp.int32)
         kept, given = query_halves(
             where,
             gathered,
-            query_weight,
+            query_near,
             key_value_weight,
             by_rank(query_down_factor),
             query_up_factor.reshape(own_slots * ADAPTER_RANK, -1),
@@ -428,18 +492,28 @@
         pair_delta = lax.dynamic_update_slice_in_dim(pair_delta, there + pair_query, first_column, 2)
         leaving = jnp.concatenate([pair_delta, pair_keyval], axis=2)
     arrived = exchange_chips(leaving)
+    arrived, lengths = lax.optimization_barrier((arrived, lengths))
     query_rows = jnp.sum(arrived[:, :, :query_width], axis=0).astype(jnp.bfloat16)
     keyval_rows = arrived[:, :, query_width:].astype(jnp.bfloat16)
     keyval_rows = keyval_rows.reshape(count // 2, local_rows, 2, -1)
     keyval_rows = keyval_rows.transpose(1, 0, 2, 3).reshape(local_rows, -1)
 
     attention_output = attend(query_rows, keyval_rows, key_cache, value_cache, lengths)
-    every_row = gather_rows(attention_output)
+    if aligned:
+
+        def bring_output(rows):
+            now, _ = lax.optimization_barrier((where, rows))
+            return bring(now, output_weight, output_weight.shape[1] // 2, OUTPUT_VMEM)
+
+        every_row, output_near = gather_rows(attention_output, bring_output)
+    else:
+        every_row = gather_rows(attention_output)
     if aligned:
         kept, given = output_halves(
             where,
             every_row,
             gathered,
+            output_near,
             output_weight,
             by_rank(output_down_factor),
             output_up_factor.reshape(own_slots * ADAPTER_RANK, -1),

time: 92.5 us -> 91.8 us (level)
  blocking collectives: 32.8 us -> 52.8 us
  waiting for transfers between devices: 24.9 us -> 5.21 us
  other arithmetic: 6.22 us -> 2.46 us
  starting transfers between devices: 14.6 us -> 11 us
  Pallas kernels: 11.5 us -> 14.8 us
  local copies, waits for them, and re-layouts: 0.57 us -> 3.61 us
    all_to_all x1 -> x2, blocking collectives: 18.4 us -> 39.1 us  [exchange_chips(): lax.all_to_all(blocks, 'pool', 0, 0, tiled=True, axis_index_groups=same_c...]
    all_to_all x1 -> x0, waiting for transfers between devices: 15.5 us -> none  [exchange_chips(): lax.all_to_all(blocks, 'pool', 0, 0, tiled=True, axis_index_groups=same_c...]
    pallas_call x0 -> x3, Pallas kernels: none -> 7.59 us  [the longest x2 6.87 us: bring(): pl.pallas_call(bring_kernel, in_specs=[pl.BlockSpec(memory_space=pltpu.SM...]
    ppermute x6, waiting for transfers between devices: 6.28 us -> 2.06 us  [exchange_quads(): lax.ppermute(rows, 'pool', [(i, i ^ k * step) for i in range(count)])]
    all_to_all x1 -> x0, starting transfers between devices: 3.54 us -> none  [exchange_chips(): lax.all_to_all(blocks, 'pool', 0, 0, tiled=True, axis_index_groups=same_c...]
    unnamed x8 -> x26, local copies, waits for them, and re-layouts: 0.38 us -> 3.52 us
    pallas_call x1, Pallas kernels: 6.12 us -> 3.18 us  [query_halves(): pl.pallas_call(query_kernel, in_specs=[pl.BlockSpec(memory_space=pltpu.SM...]
    reduce_sum x2 -> x0, other arithmetic: 1.94 us -> none  [the longest x1 1 us: lookup_slots(): return jnp.sum(jnp.where(matches, adapter_slot[None, :], 0), axis=1)]
  transfers between devices with their start and end apart: 9 -> 8, of which waited for: 8 -> 4; matrix products, arithmetic and copies ran while one was open for 0% -> 0% of each run, Pallas kernels for 0% -> 8%
where the time goes in v5:
time: 91.8 us; the launch traced here: 91.5 us
  blocking collectives  52.8 us (58%)
  Pallas kernels  14.8 us (16%)
  starting transfers between devices  11 us (12%)
  waiting for transfers between devices  5.21 us (6%)
  local copies, waits for them, and re-layouts  3.61 us (4%)
  other arithmetic  2.46 us (3%)
  matrix products  1.37 us (1%)
    all_to_all x2, blocking collectives, exchange_chips(): lax.all_to_all(blocks, 'pool', 0, 0, tiled=True, axis_index_groups=same_c...  39.1 us
    all_gather x2, blocking collectives, gather_rows(): lax.all_gather(rows, 'pool', axis=0, axis_index_groups=fours, tiled=True)  13.8 us
    ppermute x6, starting transfers between devices, exchange_quads(): lax.ppermute(rows, 'pool', [(i, i ^ k * step) for i in range(count)])  10.1 us
    pallas_call x2, Pallas kernels, bring(): pl.pallas_call(bring_kernel, in_specs=[pl.BlockSpec(memory_space=pltpu.SM...  6.87 us
    pallas_call x1, Pallas kernels, output_halves(): pl.pallas_call(output_kernel, in_specs=[pl.BlockSpec(memory_space=pltpu.S...  4.07 us
    unnamed x26, local copies, waits for them, and re-layouts  3.52 us
    pallas_call x1, Pallas kernels, query_halves(): pl.pallas_call(query_kernel, in_specs=[pl.BlockSpec(memory_space=pltpu.SM...  3.18 us
    ppermute x2, waiting for transfers between devices, swap_cores(): return lax.ppermute(block, 'pool', [(i, i ^ 1) for i in range(count)])  3.15 us
  transfers between devices with their start and end apart: 8, of which 4 were waited for; matrix products, arithmetic and copies ran while one was open for 0% of the time, Pallas kernels for 8%

profile of v5, /device:TPU:0, one launch (start us, length us, event | category | flops | bytes accessed | tf_op | source)
XLA Modules:
  0.0 91.5 jit_solution(15175578507064151466)
XLA Ops:
  0.0 0.9 copy-done.6
  0.9 0.8 copy-done.7
  1.7 0.7 copy-done.8
  2.3 0.7 copy-done.9
  3.0 0.7 norm_and_marks.1
  3.7 3.1 %collective-permute-start.2 = (bf16[2,8320]{1,0:T(2,128)(2,1)S(1)}, bf16[2,8320]{1,0:T(2,128)(2,1)S(1)}, u32[]{:S(2)}, u32[]{:S(2)}) collective-permute-start(bf16[2,8320]{1,0:T(2,128)(2,1)S(1)} %norm_and_marks.1), channel_id=1, source_target_pairs={{0,4},{1,5},{2,6},{3,7},{4,0},{5,1},{6,2},{7,3},{8,12},{9,13},{10,... | collective-permute-start | bytes 99848 | tf_op jit(solution)/shard_map/ppermute | solution.py:80
  6.8 2.6 %collective-permute-start.1 = (bf16[2,8320]{1,0:T(2,128)(2,1)S(1)}, bf16[2,8320]{1,0:T(2,128)(2,1)S(1)}, u32[]{:S(2)}, u32[]{:S(2)}) collective-permute-start(bf16[2,8320]{1,0:T(2,128)(2,1)S(1)} %norm_and_marks.1), channel_id=1, source_target_pairs={{0,8},{1,9},{2,10},{3,11},{4,12},{5,13},{6,14},{7,15},{8,0},{9,1},... | collective-permute-start | bytes 99848 | tf_op jit(solution)/shard_map/ppermute | solution.py:80
  9.5 4.1 %bring.2.query_vmem = bf16[8192,512]{1,0:T(8,128)(2,1)S(1)} custom-call(s32[2]{0:T(128)S(1)} %pad_add_fusion.where_ref, bf16[8192,512]{1,0:T(8,128)(2,1)} %source.2), custom_call_target="tpu_custom_call" | custom-call | bytes 16777216 | tf_op jit(solution)/shard_map/bring/pallas_call | solution.py:350
  13.6 1.5 %collective-permute-done = bf16[2,8320]{1,0:T(2,128)(2,1)S(1)} collective-permute-done((bf16[2,8320]{1,0:T(2,128)(2,1)S(1)}, bf16[2,8320]{1,0:T(2,128)(2,1)S(1)}, u32[]{:S(2)}, u32[]{:S(2)}) %collective-permute-start) | collective-permute-done | bytes 33312 | tf_op jit(solution)/shard_map/ppermute | solution.py:80
  15.3 0.2 pad_maximum_fusion
  15.4 7.2 %all_gather.6 = bf16[32,8320]{1,0:T(8,128)(2,1)S(1)} all-gather(bf16[8,8320]{1,0:T(8,128)(2,1)S(1)} %pad_maximum_fusion), channel_id=1, replica_groups={{0,1,2,3},{4,5,6,7},{8,9,10,11},{12,13,14,15},{16,17,18,19},{20,21,22,2..., dimensions={0}, use_global_device_ids=true | all-gather | bytes 665600 | tf_op jit(solution)/shard_map/all_gather | solution.py:122
  22.7 3.2 %query_halves.1 = (f32[8,2,8448]{2,1,0:T(2,128)S(1)}, f32[8,2,8448]{2,1,0:T(2,128)S(1)}) custom-call(s32[2]{0:T(128)S(1)} %pad_add_fusion.where_ref, bf16[32,8192]{1,0:T(8,128)(2,1)S(1)} %slice.26.rows_ref, bf16[32,128]{1,0:T(8,128)(2,1)S(1)} %slice.27.marks_ref, bf16[8192,512]{1,0:T(8,128)(2,1)S(1)} %bring.2.query_vmem, bf16[8192,128]{1,0:T(8,128)(2,1)S(1)} %copy-done.1, ...), custom_call_target="tpu_custom_call" | custom-call | tf_op jit(solution)/shard_map/query_halves/pallas_call | solution.py:251
  25.9 0.4 collective-permute-start.3
  26.4 1.6 %collective-permute-done.3 = f32[8,2,8448]{2,1,0:T(2,128)S(1)} collective-permute-done((f32[8,2,8448]{2,1,0:T(2,128)S(1)}, f32[8,2,8448]{2,1,0:T(2,128)S(1)}, u32[]{:S(2)}, u32[]{:S(2)}) %collective-permute-start.3) | collective-permute-done | bytes 540704 | tf_op jit(solution)/shard_map/ppermute | solution.py:141
  27.9 0.3 add.12
  28.2 20.0 %all_to_all.10 = f32[8,2,8448]{2,1,0:T(2,128)S(1)} all-to-all(f32[8,2,8448]{2,1,0:T(2,128)S(1)} %add.12), channel_id=1, replica_groups={{0,2,4,6,8,10,12,14},{1,3,5,7,9,11,13,15},{16,18,20,22,24,26,28,30},{17..., dimensions={0} | all-to-all | bytes 1081344 | tf_op jit(solution)/shard_map/all_to_all | solution.py:147
  48.7 0.7 fusion.34
  49.4 0.2 fusion.21
  49.7 0.5 copy-done.11
  50.1 0.5 fusion.18
  50.7 0.7 collective-permute-start.6
  51.4 1.4 %collective-permute-start.5 = (bf16[2,8192]{1,0:T(2,128)(2,1)S(1)}, bf16[2,8192]{1,0:T(2,128)(2,1)S(1)}, u32[]{:S(2)}, u32[]{:S(2)}) collective-permute-start(bf16[2,8192]{1,0:T(2,128)(2,1)S(1)} %bitcast.83), channel_id=1, source_target_pairs={{0,8},{1,9},{2,10},{3,11},{4,12},{5,13},{6,14},{7,15},{8,0},{9,1},... | collective-permute-start | bytes 98312 | tf_op jit(solution)/shard_map/ppermute | solution.py:80
  52.8 2.4 %collective-permute-start.4 = (bf16[2,8192]{1,0:T(2,128)(2,1)S(1)}, bf16[2,8192]{1,0:T(2,128)(2,1)S(1)}, u32[]{:S(2)}, u32[]{:S(2)}) collective-permute-start(bf16[2,8192]{1,0:T(2,128)(2,1)S(1)} %bitcast.84), channel_id=1, source_target_pairs={{0,12},{1,13},{2,14},{3,15},{4,8},{5,9},{6,10},{7,11},{8,4},{9,5},... | collective-permute-start | bytes 98312 | tf_op jit(solution)/shard_map/ppermute | solution.py:80
  55.1 2.7 %bring.3.near_vmem = bf16[512,4096]{1,0:T(8,128)(2,1)S(1)} custom-call(s32[2]{0:T(128)S(1)} %pad_add_fusion.where_ref, bf16[512,8192]{1,0:T(8,128)(2,1)} %output_hbm.1), custom_call_target="tpu_custom_call" | custom-call | bytes 8388608 | tf_op jit(solution)/shard_map/bring/pallas_call | solution.py:350
  57.9 0.6 collective-permute-done.4
  58.8 6.5 %all_gather.7.rows_ref = bf16[32,8192]{1,0:T(8,128)(2,1)S(1)} all-gather(bf16[8,8192]{1,0:T(8,128)(2,1)S(1)} %pad_maximum_fusion.1), channel_id=1, replica_groups={{0,1,2,3},{4,5,6,7},{8,9,10,11},{12,13,14,15},{16,17,18,19},{20,21,22,2..., dimensions={0}, use_global_device_ids=true | all-gather | bytes 655360 | tf_op jit(solution)/shard_map/all_gather | solution.py:122
  65.3 4.1 %output_halves.1 = (f32[8,2,8192]{2,1,0:T(2,128)S(1)}, f32[8,2,8192]{2,1,0:T(2,128)S(1)}) custom-call(s32[2]{0:T(128)S(1)} %pad_add_fusion.where_ref, bf16[32,8192]{1,0:T(8,128)(2,1)S(1)} %all_gather.7.rows_ref, bf16[32,128]{1,0:T(8,128)(2,1)S(1)} %slice.27.marks_ref, bf16[512,4096]{1,0:T(8,128)(2,1)S(1)} %bring.3.near_vmem, bf16[512,8192]{1,0:T(8,128)(2,1)} %output_hbm.1, ...), custom_call_target="tpu_custom_call" | custom-call | tf_op jit(solution)/shard_map/output_halves/pallas_call | solution.py:308
  69.4 0.4 collective-permute-start.7
  69.8 1.6 %collective-permute-done.7 = f32[8,2,8192]{2,1,0:T(2,128)S(1)} collective-permute-done((f32[8,2,8192]{2,1,0:T(2,128)S(1)}, f32[8,2,8192]{2,1,0:T(2,128)S(1)}, u32[]{:S(2)}, u32[]{:S(2)}) %collective-permute-start.7) | collective-permute-done | bytes 524320 | tf_op jit(solution)/shard_map/ppermute | solution.py:141
  71.4 0.3 add.15
  71.6 19.1 %all_to_all.11 = f32[8,2,8192]{2,1,0:T(2,128)S(1)} all-to-all(f32[8,2,8192]{2,1,0:T(2,128)S(1)} %add.15), channel_id=1, replica_groups={{0,2,4,6,8,10,12,14},{1,3,5,7,9,11,13,15},{16,18,20,22,24,26,28,30},{17..., dimensions={0} | all-to-all | bytes 1048576 | tf_op jit(solution)/shard_map/all_to_all | solution.py:147
  90.7 0.8 reduce_sum.29
  (43 shorter events, 1.1 us)
Async XLA Ops:
  0.0 48.7 %copy-start = (bf16[2,512,1024]{2,1,0:T(8,128)(2,1)S(1)}, bf16[2,512,1024]{2,1,0:T(8,128)(2,1)}, u32[]{:S(2)}) copy-start(bf16[2,512,1024]{2,1,0:T(8,128)(2,1)} %param.23) | copy-start | bytes 6291460
  0.0 0.9 copy-start.6
  0.9 0.8 copy-start.7
  1.7 0.7 copy-start.8
  2.3 0.7 copy-start.9
  3.7 9.9 %collective-permute-start.2 = (bf16[2,8320]{1,0:T(2,128)(2,1)S(1)}, bf16[2,8320]{1,0:T(2,128)(2,1)S(1)}, u32[]{:S(2)}, u32[]{:S(2)}) collective-permute-start(bf16[2,8320]{1,0:T(2,128)(2,1)S(1)} %norm_and_marks.1), channel_id=1, source_target_pairs={{0,4},{1,5},{2,6},{3,7},{4,0},{5,1},{6,2},{7,3},{8,12},{9,13},{10,... | collective-permute-start | bytes 99848 | tf_op jit(solution)/shard_map/ppermute | solution.py:80
  6.8 6.8 %collective-permute-start.1 = (bf16[2,8320]{1,0:T(2,128)(2,1)S(1)}, bf16[2,8320]{1,0:T(2,128)(2,1)S(1)}, u32[]{:S(2)}, u32[]{:S(2)}) collective-permute-start(bf16[2,8320]{1,0:T(2,128)(2,1)S(1)} %norm_and_marks.1), channel_id=1, source_target_pairs={{0,8},{1,9},{2,10},{3,11},{4,12},{5,13},{6,14},{7,15},{8,0},{9,1},... | collective-permute-start | bytes 99848 | tf_op jit(solution)/shard_map/ppermute | solution.py:80
  9.4 5.7 %collective-permute-start = (bf16[2,8320]{1,0:T(2,128)(2,1)S(1)}, bf16[2,8320]{1,0:T(2,128)(2,1)S(1)}, u32[]{:S(2)}, u32[]{:S(2)}) collective-permute-start(bf16[2,8320]{1,0:T(2,128)(2,1)S(1)} %norm_and_marks.1), channel_id=1, source_target_pairs={{0,12},{1,13},{2,14},{3,15},{4,8},{5,9},{6,10},{7,11},{8,4},{9,5},... | collective-permute-start | bytes 99848 | tf_op jit(solution)/shard_map/ppermute | solution.py:80
  9.5 13.2 %copy-start.2 = (bf16[4,8192,16]{1,2,0:T(8,128)(2,1)S(1)}, bf16[4,8192,16]{1,2,0:T(8,128)(2,1)}, u32[]{:S(2)}) copy-start(bf16[4,8192,16]{1,2,0:T(8,128)(2,1)} %param.19) | copy-start | bytes 3145732
  9.5 13.2 %copy-start.3 = (bf16[4,16,8192]{2,1,0:T(8,128)(2,1)S(1)}, bf16[4,16,8192]{2,1,0:T(8,128)(2,1)}, u32[]{:S(2)}) copy-start(bf16[4,16,8192]{2,1,0:T(8,128)(2,1)} %param.20) | copy-start | bytes 3145732
  13.6 9.1 %copy-start.1 = (bf16[8192,128]{1,0:T(8,128)(2,1)S(1)}, bf16[8192,128]{1,0:T(8,128)(2,1)}, u32[]{:S(2)}) copy-start(bf16[8192,128]{1,0:T(8,128)(2,1)} %keyval_vmem.1) | copy-start | bytes 6291460
  25.9 22.4 %copy-start.10 = (s32[2]{0:T(128)S(1)}, s32[2]{0:T(128)}, u32[]{:S(2)}) copy-start(s32[2]{0:T(128)} %param.25) | copy-start | bytes 28
  25.9 2.0 %collective-permute-start.3 = (f32[8,2,8448]{2,1,0:T(2,128)S(1)}, f32[8,2,8448]{2,1,0:T(2,128)S(1)}, u32[]{:S(2)}, u32[]{:S(2)}) collective-permute-start(f32[8,2,8448]{2,1,0:T(2,128)S(1)} %get-tuple-element.21), channel_id=1, source_target_pairs={{0,1},{1,0},{2,3},{3,2},{4,5},{5,4},{6,7},{7,6},{8,9},{9,8},{10,11... | collective-permute-start | bytes 1622024 | tf_op jit(solution)/shard_map/ppermute | solution.py:141
  48.5 1.6 %copy-start.11 = (bf16[2,512,1024]{2,1,0:T(8,128)(2,1)S(1)}, bf16[2,512,1024]{2,1,0:T(8,128)(2,1)}, u32[]{:S(2)}) copy-start(bf16[2,512,1024]{2,1,0:T(8,128)(2,1)} %param.24) | copy-start | bytes 6291460
  50.7 14.7 %copy-start.4 = (bf16[4,8192,16]{1,2,0:T(8,128)(2,1)S(1)}, bf16[4,8192,16]{1,2,0:T(8,128)(2,1)}, u32[]{:S(2)}) copy-start(bf16[4,8192,16]{1,2,0:T(8,128)(2,1)} %param.21) | copy-start | bytes 3145732
  50.7 14.6 %copy-start.5 = (bf16[4,16,8192]{2,1,0:T(8,128)(2,1)S(1)}, bf16[4,16,8192]{2,1,0:T(8,128)(2,1)}, u32[]{:S(2)}) copy-start(bf16[4,16,8192]{2,1,0:T(8,128)(2,1)} %param.22) | copy-start | bytes 3145732
  50.7 7.2 %collective-permute-start.6 = (bf16[2,8192]{1,0:T(2,128)(2,1)S(1)}, bf16[2,8192]{1,0:T(2,128)(2,1)S(1)}, u32[]{:S(2)}, u32[]{:S(2)}) collective-permute-start(bf16[2,8192]{1,0:T(2,128)(2,1)S(1)} %bitcast.82), channel_id=1, source_target_pairs={{0,4},{1,5},{2,6},{3,7},{4,0},{5,1},{6,2},{7,3},{8,12},{9,13},{10,... | collective-permute-start | bytes 98312 | tf_op jit(solution)/shard_map/ppermute | solution.py:80
  51.4 6.5 %collective-permute-start.5 = (bf16[2,8192]{1,0:T(2,128)(2,1)S(1)}, bf16[2,8192]{1,0:T(2,128)(2,1)S(1)}, u32[]{:S(2)}, u32[]{:S(2)}) collective-permute-start(bf16[2,8192]{1,0:T(2,128)(2,1)S(1)} %bitcast.83), channel_id=1, source_target_pairs={{0,8},{1,9},{2,10},{3,11},{4,12},{5,13},{6,14},{7,15},{8,0},{9,1},... | collective-permute-start | bytes 98312 | tf_op jit(solution)/shard_map/ppermute | solution.py:80
  52.8 5.7 %collective-permute-start.4 = (bf16[2,8192]{1,0:T(2,128)(2,1)S(1)}, bf16[2,8192]{1,0:T(2,128)(2,1)S(1)}, u32[]{:S(2)}, u32[]{:S(2)}) collective-permute-start(bf16[2,8192]{1,0:T(2,128)(2,1)S(1)} %bitcast.84), channel_id=1, source_target_pairs={{0,12},{1,13},{2,14},{3,15},{4,8},{5,9},{6,10},{7,11},{8,4},{9,5},... | collective-permute-start | bytes 98312 | tf_op jit(solution)/shard_map/ppermute | solution.py:80
  69.4 2.0 %collective-permute-start.7 = (f32[8,2,8192]{2,1,0:T(2,128)S(1)}, f32[8,2,8192]{2,1,0:T(2,128)S(1)}, u32[]{:S(2)}, u32[]{:S(2)}) collective-permute-start(f32[8,2,8192]{2,1,0:T(2,128)S(1)} %get-tuple-element.28), channel_id=1, source_target_pairs={{0,1},{1,0},{2,3},{3,2},{4,5},{5,4},{6,7},{7,6},{8,9},{9,8},{10,11... | collective-permute-start | bytes 1572872 | tf_op jit(solution)/shard_map/ppermute | solution.py:141

commit v6 on v4

--- a/solution.py
+++ b/solution.py
@@ -105,9 +105,10 @@
     return jnp.concatenate([jnp.where(upper, other, rows), jnp.where(upper, rows, other)], axis=0)
 
 
-def gather_rows(rows):
+def gather_rows(rows, beside=None):
     count = pool_size()
     step = 4
+    held = None if beside is None else beside(rows)
     while step < count:
         if step * 4 <= count:
             rows = exchange_quads(rows, step)
@@ -115,8 +116,11 @@
         else:
             rows = exchange_pair(rows, step)
             step *= 2
+    if held is not None:
+        rows, held = lax.optimization_barrier((rows, held))
     fours = [[4 * k + j for j in range(4)] for k in range(count // 4)]
-    return lax.all_gather(rows, "pool", axis=0, axis_index_groups=fours, tiled=True)
+    rows = lax.all_gather(rows, "pool", axis=0, axis_index_groups=fours, tiled=True)
+    return rows if beside is None else (rows, held)
 
 
 def core_halves(partial):
@@ -152,7 +156,8 @@
 
 CHUNKS = 8
 LANES = 128
-KERNEL_VMEM = 52 * 1024 * 1024
+KERNEL_VMEM = 24 * 1024 * 1024
+BRING_VMEM = 40 * 1024 * 1024
 
 
 def whole_block(shape):
@@ -200,30 +205,14 @@
 
 
 def query_kernel(
-    where_ref, rows_ref, marks_ref, query_hbm, keyval_hbm, down_hbm, up_hbm,
-    kept_ref, given_ref, query_vmem, keyval_vmem, down_vmem, up_vmem, sems,
+    where_ref, rows_ref, marks_ref, query_vmem, keyval_vmem, down_vmem, up_vmem,
+    kept_ref, given_ref,
 ):
     me = where_ref[0]
     odd = (me % 2) == 1
     width = down_vmem.shape[1]
     step = width // CHUNKS
-    down_copy = pltpu.make_async_copy(down_hbm, down_vmem, sems.at[CHUNKS])
-    up_copy = pltpu.make_async_copy(up_hbm, up_vmem, sems.at[CHUNKS + 1])
-    keyval_copy = pltpu.make_async_copy(keyval_hbm, keyval_vmem, sems.at[CHUNKS + 2])
-    query_copies = [
-        pltpu.make_async_copy(
-            query_hbm.at[pl.ds(k * step, step)], query_vmem.at[pl.ds(k * step, step)], sems.at[k]
-        )
-        for k in range(CHUNKS)
-    ]
-    down_copy.start()
-    up_copy.start()
-    for copy in query_copies:
-        copy.start()
-    keyval_copy.start()
-    down_copy.wait()
     lifted = own_lift(rows_ref, down_vmem, marks_ref, where_ref[1])
-    up_copy.wait()
     for k in range(CHUNKS):
         spot = slice(k * step, (k + 1) * step)
         delta = adapter_scale * jnp.dot(
@@ -233,14 +222,12 @@
     query = None
     for k in range(CHUNKS):
         spot = slice(k * step, (k + 1) * step)
-        query_copies[k].wait()
         part = jnp.dot(rows_ref[:, spot], query_vmem[spot], preferred_element_type=jnp.float32)
         query = part if query is None else query + part
     columns = query.shape[1]
     split_store(
         query, odd, kept_ref, given_ref, pl.multiple_of(me * columns, LANES), True
     )
-    keyval_copy.wait()
     keyval = None
     for k in range(CHUNKS):
         spot = slice(k * step, (k + 1) * step)
@@ -266,50 +253,25 @@
             whole_block((rows, width)),
             whole_block((rows, LANES)),
         ]
-        + [pl.BlockSpec(memory_space=pl.ANY)] * 4,
+        + [pl.BlockSpec(memory_space=pltpu.VMEM)] * 4,
         out_specs=[whole_block(sent.shape)] * 2,
         out_shape=[sent, sent],
-        scratch_shapes=[
-            pltpu.VMEM((width, columns), jnp.bfloat16),
-            pltpu.VMEM((width, keyval_columns), jnp.bfloat16),
-            pltpu.VMEM((ranks, width), jnp.bfloat16),
-            pltpu.VMEM((ranks, width), jnp.bfloat16),
-            pltpu.SemaphoreType.DMA((CHUNKS + 3,)),
-        ],
         compiler_params=pltpu.CompilerParams(vmem_limit_bytes=KERNEL_VMEM),
         name="query_halves",
     )(where, gathered[:, :width], gathered[:, width:], query_weight, key_value_weight, down, up)
 
 
 def output_kernel(
-    where_ref, rows_ref, marks_ref, output_hbm, down_hbm, up_hbm,
-    kept_ref, given_ref, output_vmem, down_vmem, up_vmem, sems,
+    where_ref, rows_ref, marks_ref, output_vmem, down_vmem, up_vmem, kept_ref, given_ref
 ):
     me = where_ref[0]
     odd = (me % 2) == 1
     depth, width = output_vmem.shape
     step = width // CHUNKS
-    down_copy = pltpu.make_async_copy(down_hbm, down_vmem, sems.at[CHUNKS])
-    up_copy = pltpu.make_async_copy(up_hbm, up_vmem, sems.at[CHUNKS + 1])
-    output_copies = [
-        pltpu.make_async_copy(
-            output_hbm.at[:, pl.ds(k * step, step)],
-            output_vmem.at[:, pl.ds(k * step, step)],
-            sems.at[k],
-        )
-        for k in range(CHUNKS)
-    ]
-    down_copy.start()
-    up_copy.start()
-    for copy in output_copies:
-        copy.start()
-    down_copy.wait()
     lifted = own_lift(rows_ref, down_vmem, marks_ref, where_ref[1])
     columns = rows_ref[:, pl.ds(pl.multiple_of(me * depth, LANES), depth)]
-    up_copy.wait()
     for k in range(CHUNKS):
         spot = slice(k * step, (k + 1) * step)
-        output_copies[k].wait()
         part = jnp.dot(columns, output_vmem[:, spot], preferred_element_type=jnp.float32)
         part = part + adapter_scale * jnp.dot(
             lifted, up_vmem[:, spot], preferred_element_type=jnp.float32
@@ -329,18 +291,44 @@
             whole_block((rows, width)),
             whole_block((rows, LANES)),
         ]
-        + [pl.BlockSpec(memory_space=pl.ANY)] * 3,
+        + [pl.BlockSpec(memory_space=pltpu.VMEM)] * 3,
         out_specs=[whole_block(sent.shape)] * 2,
         out_shape=[sent, sent],
-        scratch_shapes=[
-            pltpu.VMEM((depth, width), jnp.bfloat16),
-            pltpu.VMEM((ranks, width), jnp.bfloat16),
-            pltpu.VMEM((ranks, width), jnp.bfloat16),
-            pltpu.SemaphoreType.DMA((CHUNKS + 2,)),
-        ],
         compiler_params=pltpu.CompilerParams(vmem_limit_bytes=KERNEL_VMEM),
         name="output_halves",
     )(where, every_row, gathered[:, width:], output_weight, down, up)
+
+
+def bring_kernel(*refs):
+    count = (len(refs) - 2) // 2
+    sources, targets, sems = refs[1 : count + 1], refs[count + 1 : -1], refs[-1]
+    copies = []
+    for source, target in zip(sources, targets):
+        step = source.shape[0] // 4
+        for k in range(4):
+            spot = pl.ds(k * step, step)
+            copies.append(
+                pltpu.make_async_copy(source.at[spot], target.at[spot], sems.at[len(copies)])
+            )
+    for copy in copies:
+        copy.start()
+    for copy in copies:
+        copy.wait()
+
+
+def bring(where, arrays):
+    size = sum(2 * array.size for array in arrays)
+    return pl.pallas_call(
+        bring_kernel,
+        in_specs=[pl.BlockSpec(memory_space=pltpu.SMEM)]
+        + [pl.BlockSpec(memory_space=pl.ANY)] * len(arrays),
+        out_specs=[pl.BlockSpec(memory_space=pltpu.VMEM)] * len(arrays),
+        out_shape=[jax.ShapeDtypeStruct(array.shape, array.dtype) for array in arrays],
+        scratch_shapes=[pltpu.SemaphoreType.DMA((4 * len(arrays),))],
+        compiler_params=pltpu.CompilerParams(vmem_limit_bytes=BRING_VMEM),
+        cost_estimate=pl.CostEstimate(flops=0, bytes_accessed=2 * size, transcendentals=0),
+        name="bring",
+    )(where, *arrays)
 
 
 def by_rank(factor):
@@ -372,26 +360,37 @@
     slot_ids = lookup_slots(request_adapter, adapter_slot)
     digits = jnp.stack([slot_ids // 32, slot_ids % 32], axis=1).astype(jnp.bfloat16)
     sent = jnp.concatenate([normalized_input, jnp.pad(digits, ((0, 0), (0, 126)))], axis=1)
-    gathered = gather_rows(sent)
+    first_slot = lax.axis_index("pool") * own_slots
+    where = jnp.stack([lax.axis_index("pool"), first_slot]).astype(jnp.int32)
+    aligned = col_width % LANES == 0 and key_value_weight.shape[1] % LANES == 0
+    if aligned:
+
+        def bring_query(rows):
+            now, _ = lax.optimization_barrier((where, rows))
+            return bring(
+                now,
+                [query_weight],
+            )
+
+        gathered, (query_near,) = gather_rows(sent, bring_query)
+    else:
+        gathered = gather_rows(sent)
     gathered_rows = gathered[:, :MODEL_WIDTH]
     all_digits = gathered[:, MODEL_WIDTH : MODEL_WIDTH + 2].astype(jnp.int32)
     slot_ids = all_digits[:, 0] * 32 + all_digits[:, 1]
     request_total = gathered_rows.shape[0]
 
-    first_slot = lax.axis_index("pool") * own_slots
     owner_mask = (
         slot_ids[:, None] == first_slot + jnp.arange(own_slots, dtype=jnp.int32)[None, :]
     )
     bf_zero = jnp.zeros((), jnp.bfloat16)
 
-    aligned = col_width % LANES == 0 and key_value_weight.shape[1] % LANES == 0
     query_width = MODEL_WIDTH
     if aligned:
-        where = jnp.stack([lax.axis_index("pool"), first_slot]).astype(jnp.int32)
         kept, given = query_halves(
             where,
             gathered,
-            query_weight,
+            query_near,
             key_value_weight,
             by_rank(query_down_factor),
             query_up_factor.reshape(own_slots * ADAPTER_RANK, -1),
@@ -428,19 +427,28 @@
         pair_delta = lax.dynamic_update_slice_in_dim(pair_delta, there + pair_query, first_column, 2)
         leaving = jnp.concatenate([pair_delta, pair_keyval], axis=2)
     arrived = exchange_chips(leaving)
+    arrived, lengths = lax.optimization_barrier((arrived, lengths))
     query_rows = jnp.sum(arrived[:, :, :query_width], axis=0).astype(jnp.bfloat16)
     keyval_rows = arrived[:, :, query_width:].astype(jnp.bfloat16)
     keyval_rows = keyval_rows.reshape(count // 2, local_rows, 2, -1)
     keyval_rows = keyval_rows.transpose(1, 0, 2, 3).reshape(local_rows, -1)
 
     attention_output = attend(query_rows, keyval_rows, key_cache, value_cache, lengths)
-    every_row = gather_rows(attention_output)
+    if aligned:
+
+        def bring_output(rows):
+            now, _ = lax.optimization_barrier((where, rows))
+            return bring(now, [output_weight])
+
+        every_row, (output_near,) = gather_rows(attention_output, bring_output)
+    else:
+        every_row = gather_rows(attention_output)
     if aligned:
         kept, given = output_halves(
             where,
             every_row,
             gathered,
-            output_weight,
+            output_near,
             by_rank(output_down_factor),
             output_up_factor.reshape(own_slots * ADAPTER_RANK, -1),
             count,

time: 92.5 us -> 90.1 us (0.974)
  waiting for transfers between devices: 24.9 us -> 4.64 us
  blocking collectives: 32.8 us -> 52.1 us
  starting transfers between devices: 14.6 us -> 11 us
  Pallas kernels: 11.5 us -> 14.3 us
    all_to_all x1 -> x2, blocking collectives: 18.4 us -> 38.3 us  [exchange_chips(): lax.all_to_all(blocks, 'pool', 0, 0, tiled=True, axis_index_groups=same_c...]
    all_to_all x1 -> x0, waiting for transfers between devices: 15.5 us -> none  [exchange_chips(): lax.all_to_all(blocks, 'pool', 0, 0, tiled=True, axis_index_groups=same_c...]
    pallas_call x0 -> x2, Pallas kernels: none -> 8.16 us  [bring(): pl.pallas_call(bring_kernel, in_specs=[pl.BlockSpec(memory_space=pltpu.SM...]
    ppermute x6, waiting for transfers between devices: 6.28 us -> 1.49 us  [exchange_quads(): lax.ppermute(rows, 'pool', [(i, i ^ k * step) for i in range(count)])]
    all_to_all x1 -> x0, starting transfers between devices: 3.54 us -> none  [exchange_chips(): lax.all_to_all(blocks, 'pool', 0, 0, tiled=True, axis_index_groups=same_c...]
    pallas_call x1, Pallas kernels: 6.12 us -> 3.18 us  [query_halves(): pl.pallas_call(query_kernel, in_specs=[pl.BlockSpec(memory_space=pltpu.SM...]
    pallas_call x1, Pallas kernels: 5.33 us -> 2.97 us  [output_halves(): pl.pallas_call(output_kernel, in_specs=[pl.BlockSpec(memory_space=pltpu.S...]
  transfers between devices with their start and end apart: 9 -> 8, of which waited for: 8 -> 3; matrix products, arithmetic and copies ran while one was open for 0% -> 0% of each run, Pallas kernels for 0% -> 9%
where the time goes in v6:
time: 90.1 us; the launch traced here: 89.8 us
  blocking collectives  52.1 us (58%)
  Pallas kernels  14.3 us (16%)
  starting transfers between devices  11 us (12%)
  other arithmetic  5.42 us (6%)
  waiting for transfers between devices  4.64 us (5%)
  matrix products  1.37 us (2%)
    all_to_all x2, blocking collectives, exchange_chips(): lax.all_to_all(blocks, 'pool', 0, 0, tiled=True, axis_index_groups=same_c...  38.3 us
    all_gather x2, blocking collectives, gather_rows(): lax.all_gather(rows, 'pool', axis=0, axis_index_groups=fours, tiled=True)  13.8 us
    ppermute x6, starting transfers between devices, exchange_quads(): lax.ppermute(rows, 'pool', [(i, i ^ k * step) for i in range(count)])  10.1 us
    pallas_call x2, Pallas kernels, bring(): pl.pallas_call(bring_kernel, in_specs=[pl.BlockSpec(memory_space=pltpu.SM...  8.16 us
    pallas_call x1, Pallas kernels, query_halves(): pl.pallas_call(query_kernel, in_specs=[pl.BlockSpec(memory_space=pltpu.SM...  3.18 us
    ppermute x2, waiting for transfers between devices, swap_cores(): return lax.ppermute(block, 'pool', [(i, i ^ 1) for i in range(count)])  3.15 us
    pallas_call x1, Pallas kernels, output_halves(): pl.pallas_call(output_kernel, in_specs=[pl.BlockSpec(memory_space=pltpu.S...  2.97 us
  transfers between devices with their start and end apart: 8, of which 3 were waited for; matrix products, arithmetic and copies ran while one was open for 0% of the time, Pallas kernels for 9%

profile of v6, /device:TPU:0, one launch (start us, length us, event | category | flops | bytes accessed | tf_op | source)
XLA Modules:
  0.0 89.8 jit_solution(9568180440676621927)
XLA Ops:
  0.0 1.0 %fusion.36 = s32[2]{0:T(128)S(1)} fusion(s32[64]{0:T(128)} %param.27, s32[2]{0:T(128)} %param.26), kind=kLoop, calls=%fused_computation.66 | loop fusion | flops 382 | bytes 272 | tf_op jit(solution)/shard_map/reduce_sum | solution.py:30
  1.1 0.9 %fusion.26 = f32[2]{0:T(128)S(1)} fusion(bf16[2,8192]{1,0:T(2,128)(2,1)} %param.14), kind=kLoop, calls=%fused_computation.31 | loop fusion | flops 49150 | bytes 32776 | tf_op jit(solution)/shard_map/reduce_sum | solution.py:23
  2.1 0.9 fusion.28
  3.1 3.1 %collective-permute-start.2 = (bf16[2,8320]{1,0:T(2,128)(2,1)S(1)}, bf16[2,8320]{1,0:T(2,128)(2,1)S(1)}, u32[]{:S(2)}, u32[]{:S(2)}) collective-permute-start(bf16[2,8320]{1,0:T(2,128)(2,1)S(1)} %pad_maximum_fusion.2), channel_id=1, source_target_pairs={{0,4},{1,5},{2,6},{3,7},{4,0},{5,1},{6,2},{7,3},{8,12},{9,13},{10,... | collective-permute-start | bytes 99848 | tf_op jit(solution)/shard_map/ppermute | solution.py:80
  6.2 2.6 %collective-permute-start.1 = (bf16[2,8320]{1,0:T(2,128)(2,1)S(1)}, bf16[2,8320]{1,0:T(2,128)(2,1)S(1)}, u32[]{:S(2)}, u32[]{:S(2)}) collective-permute-start(bf16[2,8320]{1,0:T(2,128)(2,1)S(1)} %pad_maximum_fusion.2), channel_id=1, source_target_pairs={{0,8},{1,9},{2,10},{3,11},{4,12},{5,13},{6,14},{7,15},{8,0},{9,1},... | collective-permute-start | bytes 99848 | tf_op jit(solution)/shard_map/ppermute | solution.py:80
  8.8 4.1 %bring.2.query_vmem = bf16[8192,512]{1,0:T(8,128)(2,1)S(1)} custom-call(s32[2]{0:T(128)S(1)} %pad_add_fusion.refs_0_.where_ref, bf16[8192,512]{1,0:T(8,128)(2,1)} %refs_1_.2), custom_call_target="tpu_custom_call" | custom-call | bytes 16777216 | tf_op jit(solution)/shard_map/bring/pallas_call | solution.py:321
  13.0 1.5 %collective-permute-done = bf16[2,8320]{1,0:T(2,128)(2,1)S(1)} collective-permute-done((bf16[2,8320]{1,0:T(2,128)(2,1)S(1)}, bf16[2,8320]{1,0:T(2,128)(2,1)S(1)}, u32[]{:S(2)}, u32[]{:S(2)}) %collective-permute-start) | collective-permute-done | bytes 33312 | tf_op jit(solution)/shard_map/ppermute | solution.py:80
  14.5 0.1 broadcast_select_fusion.7
  14.6 0.2 pad_maximum_fusion
  14.8 7.2 %all_gather.6 = bf16[32,8320]{1,0:T(8,128)(2,1)S(1)} all-gather(bf16[8,8320]{1,0:T(8,128)(2,1)S(1)} %pad_maximum_fusion), channel_id=1, replica_groups={{0,1,2,3},{4,5,6,7},{8,9,10,11},{12,13,14,15},{16,17,18,19},{20,21,22,2..., dimensions={0}, use_global_device_ids=true | all-gather | bytes 665600 | tf_op jit(solution)/shard_map/all_gather | solution.py:122
  22.1 3.2 %query_halves.1 = (f32[8,2,8448]{2,1,0:T(2,128)S(1)}, f32[8,2,8448]{2,1,0:T(2,128)S(1)}) custom-call(s32[2]{0:T(128)S(1)} %pad_add_fusion.refs_0_.where_ref, bf16[32,8192]{1,0:T(8,128)(2,1)S(1)} %slice.26.rows_ref, bf16[32,128]{1,0:T(8,128)(2,1)S(1)} %slice.27.marks_ref, bf16[8192,512]{1,0:T(8,128)(2,1)S(1)} %bring.2.query_vmem, ...), custom_call_target="tpu_custom_call" | custom-call | tf_op jit(solution)/shard_map/query_halves/pallas_call | solution.py:249
  25.3 0.4 collective-permute-start.3
  25.7 1.6 %collective-permute-done.3 = f32[8,2,8448]{2,1,0:T(2,128)S(1)} collective-permute-done((f32[8,2,8448]{2,1,0:T(2,128)S(1)}, f32[8,2,8448]{2,1,0:T(2,128)S(1)}, u32[]{:S(2)}, u32[]{:S(2)}) %collective-permute-start.3) | collective-permute-done | bytes 540704 | tf_op jit(solution)/shard_map/ppermute | solution.py:141
  27.3 0.3 add.45
  27.6 20.0 %all_to_all.10 = f32[8,2,8448]{2,1,0:T(2,128)S(1)} all-to-all(f32[8,2,8448]{2,1,0:T(2,128)S(1)} %add.45), channel_id=1, replica_groups={{0,2,4,6,8,10,12,14},{1,3,5,7,9,11,13,15},{16,18,20,22,24,26,28,30},{17..., dimensions={0} | all-to-all | bytes 1081344 | tf_op jit(solution)/shard_map/all_to_all | solution.py:147
  48.0 0.7 fusion.43
  48.8 0.2 fusion.21
  49.0 0.5 copy-done.7
  49.5 0.5 fusion.18
  50.1 0.7 collective-permute-start.6
  50.7 1.4 %collective-permute-start.5 = (bf16[2,8192]{1,0:T(2,128)(2,1)S(1)}, bf16[2,8192]{1,0:T(2,128)(2,1)S(1)}, u32[]{:S(2)}, u32[]{:S(2)}) collective-permute-start(bf16[2,8192]{1,0:T(2,128)(2,1)S(1)} %bitcast.82), channel_id=1, source_target_pairs={{0,8},{1,9},{2,10},{3,11},{4,12},{5,13},{6,14},{7,15},{8,0},{9,1},... | collective-permute-start | bytes 98312 | tf_op jit(solution)/shard_map/ppermute | solution.py:80
  52.2 2.4 %collective-permute-start.4 = (bf16[2,8192]{1,0:T(2,128)(2,1)S(1)}, bf16[2,8192]{1,0:T(2,128)(2,1)S(1)}, u32[]{:S(2)}, u32[]{:S(2)}) collective-permute-start(bf16[2,8192]{1,0:T(2,128)(2,1)S(1)} %bitcast.83), channel_id=1, source_target_pairs={{0,12},{1,13},{2,14},{3,15},{4,8},{5,9},{6,10},{7,11},{8,4},{9,5},... | collective-permute-start | bytes 98312 | tf_op jit(solution)/shard_map/ppermute | solution.py:80
  54.5 4.0 %bring.3.output_vmem = bf16[512,8192]{1,0:T(8,128)(2,1)S(1)} custom-call(s32[2]{0:T(128)S(1)} %pad_add_fusion.refs_0_.where_ref, bf16[512,8192]{1,0:T(8,128)(2,1)} %refs_1_.3), custom_call_target="tpu_custom_call" | custom-call | bytes 16777216 | tf_op jit(solution)/shard_map/bring/pallas_call | solution.py:321
  58.6 0.1 broadcast_select_fusion.15
  58.8 0.2 pad_maximum_fusion.1
  58.9 6.5 %all_gather.7.rows_ref = bf16[32,8192]{1,0:T(8,128)(2,1)S(1)} all-gather(bf16[8,8192]{1,0:T(8,128)(2,1)S(1)} %pad_maximum_fusion.1), channel_id=1, replica_groups={{0,1,2,3},{4,5,6,7},{8,9,10,11},{12,13,14,15},{16,17,18,19},{20,21,22,2..., dimensions={0}, use_global_device_ids=true | all-gather | bytes 655360 | tf_op jit(solution)/shard_map/all_gather | solution.py:122
  65.4 3.0 %output_halves.1 = (f32[8,2,8192]{2,1,0:T(2,128)S(1)}, f32[8,2,8192]{2,1,0:T(2,128)S(1)}) custom-call(s32[2]{0:T(128)S(1)} %pad_add_fusion.refs_0_.where_ref, bf16[32,8192]{1,0:T(8,128)(2,1)S(1)} %all_gather.7.rows_ref, bf16[32,128]{1,0:T(8,128)(2,1)S(1)} %slice.27.marks_ref, bf16[512,8192]{1,0:T(8,128)(2,1)S(1)} %bring.3.output_vmem, ...), custom_call_target="tpu_custom_call" | custom-call | tf_op jit(solution)/shard_map/output_halves/pallas_call | solution.py:287
  68.4 0.4 collective-permute-start.7
  68.8 1.6 %collective-permute-done.7 = f32[8,2,8192]{2,1,0:T(2,128)S(1)} collective-permute-done((f32[8,2,8192]{2,1,0:T(2,128)S(1)}, f32[8,2,8192]{2,1,0:T(2,128)S(1)}, u32[]{:S(2)}, u32[]{:S(2)}) %collective-permute-start.7) | collective-permute-done | bytes 524320 | tf_op jit(solution)/shard_map/ppermute | solution.py:141
  70.4 0.3 add.48
  70.7 18.3 %all_to_all.11 = f32[8,2,8192]{2,1,0:T(2,128)S(1)} all-to-all(f32[8,2,8192]{2,1,0:T(2,128)S(1)} %add.48), channel_id=1, replica_groups={{0,2,4,6,8,10,12,14},{1,3,5,7,9,11,13,15},{16,18,20,22,24,26,28,30},{17..., dimensions={0} | all-to-all | bytes 1048576 | tf_op jit(solution)/shard_map/all_to_all | solution.py:147
  89.0 0.8 reduce_sum.52
  (42 shorter events, 0.8 us)
Async XLA Ops:
  0.0 48.0 %copy-start = (bf16[2,512,1024]{2,1,0:T(8,128)(2,1)S(1)}, bf16[2,512,1024]{2,1,0:T(8,128)(2,1)}, u32[]{:S(2)}) copy-start(bf16[2,512,1024]{2,1,0:T(8,128)(2,1)} %param.23) | copy-start | bytes 6291460
  3.1 9.9 %collective-permute-start.2 = (bf16[2,8320]{1,0:T(2,128)(2,1)S(1)}, bf16[2,8320]{1,0:T(2,128)(2,1)S(1)}, u32[]{:S(2)}, u32[]{:S(2)}) collective-permute-start(bf16[2,8320]{1,0:T(2,128)(2,1)S(1)} %pad_maximum_fusion.2), channel_id=1, source_target_pairs={{0,4},{1,5},{2,6},{3,7},{4,0},{5,1},{6,2},{7,3},{8,12},{9,13},{10,... | collective-permute-start | bytes 99848 | tf_op jit(solution)/shard_map/ppermute | solution.py:80
  6.2 6.8 %collective-permute-start.1 = (bf16[2,8320]{1,0:T(2,128)(2,1)S(1)}, bf16[2,8320]{1,0:T(2,128)(2,1)S(1)}, u32[]{:S(2)}, u32[]{:S(2)}) collective-permute-start(bf16[2,8320]{1,0:T(2,128)(2,1)S(1)} %pad_maximum_fusion.2), channel_id=1, source_target_pairs={{0,8},{1,9},{2,10},{3,11},{4,12},{5,13},{6,14},{7,15},{8,0},{9,1},... | collective-permute-start | bytes 99848 | tf_op jit(solution)/shard_map/ppermute | solution.py:80
  8.7 5.7 %collective-permute-start = (bf16[2,8320]{1,0:T(2,128)(2,1)S(1)}, bf16[2,8320]{1,0:T(2,128)(2,1)S(1)}, u32[]{:S(2)}, u32[]{:S(2)}) collective-permute-start(bf16[2,8320]{1,0:T(2,128)(2,1)S(1)} %pad_maximum_fusion.2), channel_id=1, source_target_pairs={{0,12},{1,13},{2,14},{3,15},{4,8},{5,9},{6,10},{7,11},{8,4},{9,5},... | collective-permute-start | bytes 99848 | tf_op jit(solution)/shard_map/ppermute | solution.py:80
  8.8 13.2 %copy-start.2 = (bf16[4,8192,16]{1,2,0:T(8,128)(2,1)S(1)}, bf16[4,8192,16]{1,2,0:T(8,128)(2,1)}, u32[]{:S(2)}) copy-start(bf16[4,8192,16]{1,2,0:T(8,128)(2,1)} %param.19) | copy-start | bytes 3145732
  8.8 13.3 %copy-start.3 = (bf16[4,16,8192]{2,1,0:T(8,128)(2,1)S(1)}, bf16[4,16,8192]{2,1,0:T(8,128)(2,1)}, u32[]{:S(2)}) copy-start(bf16[4,16,8192]{2,1,0:T(8,128)(2,1)} %param.20) | copy-start | bytes 3145732
  13.0 9.1 %copy-start.1 = (bf16[8192,128]{1,0:T(8,128)(2,1)S(1)}, bf16[8192,128]{1,0:T(8,128)(2,1)}, u32[]{:S(2)}) copy-start(bf16[8192,128]{1,0:T(8,128)(2,1)} %keyval_vmem.1) | copy-start | bytes 6291460
  25.3 22.4 %copy-start.6 = (s32[2]{0:T(128)S(1)}, s32[2]{0:T(128)}, u32[]{:S(2)}) copy-start(s32[2]{0:T(128)} %param.25) | copy-start | bytes 28
  25.3 2.0 %collective-permute-start.3 = (f32[8,2,8448]{2,1,0:T(2,128)S(1)}, f32[8,2,8448]{2,1,0:T(2,128)S(1)}, u32[]{:S(2)}, u32[]{:S(2)}) collective-permute-start(f32[8,2,8448]{2,1,0:T(2,128)S(1)} %get-tuple-element.21), channel_id=1, source_target_pairs={{0,1},{1,0},{2,3},{3,2},{4,5},{5,4},{6,7},{7,6},{8,9},{9,8},{10,11... | collective-permute-start | bytes 1622024 | tf_op jit(solution)/shard_map/ppermute | solution.py:141
  47.9 1.6 %copy-start.7 = (bf16[2,512,1024]{2,1,0:T(8,128)(2,1)S(1)}, bf16[2,512,1024]{2,1,0:T(8,128)(2,1)}, u32[]{:S(2)}) copy-start(bf16[2,512,1024]{2,1,0:T(8,128)(2,1)} %param.24) | copy-start | bytes 6291460
  50.0 15.4 %copy-start.4 = (bf16[4,8192,16]{1,2,0:T(8,128)(2,1)S(1)}, bf16[4,8192,16]{1,2,0:T(8,128)(2,1)}, u32[]{:S(2)}) copy-start(bf16[4,8192,16]{1,2,0:T(8,128)(2,1)} %param.21) | copy-start | bytes 3145732
  50.0 15.4 %copy-start.5 = (bf16[4,16,8192]{2,1,0:T(8,128)(2,1)S(1)}, bf16[4,16,8192]{2,1,0:T(8,128)(2,1)}, u32[]{:S(2)}) copy-start(bf16[4,16,8192]{2,1,0:T(8,128)(2,1)} %param.22) | copy-start | bytes 3145732
  50.1 8.5 %collective-permute-start.6 = (bf16[2,8192]{1,0:T(2,128)(2,1)S(1)}, bf16[2,8192]{1,0:T(2,128)(2,1)S(1)}, u32[]{:S(2)}, u32[]{:S(2)}) collective-permute-start(bf16[2,8192]{1,0:T(2,128)(2,1)S(1)} %bitcast.81), channel_id=1, source_target_pairs={{0,4},{1,5},{2,6},{3,7},{4,0},{5,1},{6,2},{7,3},{8,12},{9,13},{10,... | collective-permute-start | bytes 98312 | tf_op jit(solution)/shard_map/ppermute | solution.py:80
  50.7 7.8 %collective-permute-start.5 = (bf16[2,8192]{1,0:T(2,128)(2,1)S(1)}, bf16[2,8192]{1,0:T(2,128)(2,1)S(1)}, u32[]{:S(2)}, u32[]{:S(2)}) collective-permute-start(bf16[2,8192]{1,0:T(2,128)(2,1)S(1)} %bitcast.82), channel_id=1, source_target_pairs={{0,8},{1,9},{2,10},{3,11},{4,12},{5,13},{6,14},{7,15},{8,0},{9,1},... | collective-permute-start | bytes 98312 | tf_op jit(solution)/shard_map/ppermute | solution.py:80
  52.2 6.4 %collective-permute-start.4 = (bf16[2,8192]{1,0:T(2,128)(2,1)S(1)}, bf16[2,8192]{1,0:T(2,128)(2,1)S(1)}, u32[]{:S(2)}, u32[]{:S(2)}) collective-permute-start(bf16[2,8192]{1,0:T(2,128)(2,1)S(1)} %bitcast.83), channel_id=1, source_target_pairs={{0,12},{1,13},{2,14},{3,15},{4,8},{5,9},{6,10},{7,11},{8,4},{9,5},... | collective-permute-start | bytes 98312 | tf_op jit(solution)/shard_map/ppermute | solution.py:80
  68.4 2.0 %collective-permute-start.7 = (f32[8,2,8192]{2,1,0:T(2,128)S(1)}, f32[8,2,8192]{2,1,0:T(2,128)S(1)}, u32[]{:S(2)}, u32[]{:S(2)}) collective-permute-start(f32[8,2,8192]{2,1,0:T(2,128)S(1)} %get-tuple-element.28), channel_id=1, source_target_pairs={{0,1},{1,0},{2,3},{3,2},{4,5},{5,4},{6,7},{7,6},{8,9},{9,8},{10,11... | collective-permute-start | bytes 1572872 | tf_op jit(solution)/shard_map/ppermute | solution.py:141

commit v7 on v6

--- a/solution.py
+++ b/solution.py
@@ -466,7 +466,8 @@
             columns, output_weight, preferred_element_type=jnp.float32
         ) + adapter_scale * jnp.dot(lifted_rows, up_rows, preferred_element_type=jnp.float32)
         kept, given = core_halves(partial)
-    arrived = exchange_chips(kept + swap_cores(given))
+    pair_sums = (kept + swap_cores(given)).astype(jnp.bfloat16)
+    arrived = exchange_chips(pair_sums).astype(jnp.float32)
     return jnp.sum(arrived, axis=0).astype(jnp.bfloat16)
 
 

time: 90.1 us -> 84.6 us (0.939)
  blocking collectives: 52.1 us -> 46.5 us
    all_to_all x2, blocking collectives: 38.3 us -> 32.8 us  [exchange_chips(): lax.all_to_all(blocks, 'pool', 0, 0, tiled=True, axis_index_groups=same_c...]
  transfers between devices with their start and end apart: 8 -> 8, of which waited for: 3 -> 3; matrix products, arithmetic and copies ran while one was open for 0% -> 0% of each run, Pallas kernels for 9% -> 10%
where the time goes in v7:
time: 84.6 us; the launch traced here: 84.3 us
  blocking collectives  46.5 us (55%)
  Pallas kernels  14.3 us (17%)
  starting transfers between devices  11 us (13%)
  other arithmetic  5.48 us (6%)
  waiting for transfers between devices  4.64 us (5%)
  matrix products  1.37 us (2%)
    all_to_all x2, blocking collectives, exchange_chips(): lax.all_to_all(blocks, 'pool', 0, 0, tiled=True, axis_index_groups=same_c...  32.8 us
    all_gather x2, blocking collectives, gather_rows(): lax.all_gather(rows, 'pool', axis=0, axis_index_groups=fours, tiled=True)  13.8 us
    ppermute x6, starting transfers between devices, exchange_quads(): lax.ppermute(rows, 'pool', [(i, i ^ k * step) for i in range(count)])  10.1 us
    pallas_call x2, Pallas kernels, bring(): pl.pallas_call(bring_kernel, in_specs=[pl.BlockSpec(memory_space=pltpu.SM...  8.16 us
    pallas_call x1, Pallas kernels, query_halves(): pl.pallas_call(query_kernel, in_specs=[pl.BlockSpec(memory_space=pltpu.SM...  3.18 us
    ppermute x2, waiting for transfers between devices, swap_cores(): return lax.ppermute(block, 'pool', [(i, i ^ 1) for i in range(count)])  3.15 us
    pallas_call x1, Pallas kernels, output_halves(): pl.pallas_call(output_kernel, in_specs=[pl.BlockSpec(memory_space=pltpu.S...  2.97 us
  transfers between devices with their start and end apart: 8, of which 3 were waited for; matrix products, arithmetic and copies ran while one was open for 0% of the time, Pallas kernels for 10%

profile of v7, /device:TPU:0, one launch (start us, length us, event | category | flops | bytes accessed | tf_op | source)
XLA Modules:
  0.0 84.3 jit_solution(13217841626841636368)
XLA Ops:
  0.0 1.0 %fusion.36 = s32[2]{0:T(128)S(1)} fusion(s32[64]{0:T(128)} %param.27, s32[2]{0:T(128)} %param.26), kind=kLoop, calls=%fused_computation.67 | loop fusion | flops 382 | bytes 272 | tf_op jit(solution)/shard_map/reduce_sum | solution.py:30
  1.1 0.9 %fusion.26 = f32[2]{0:T(128)S(1)} fusion(bf16[2,8192]{1,0:T(2,128)(2,1)} %param.14), kind=kLoop, calls=%fused_computation.32 | loop fusion | flops 49150 | bytes 32776 | tf_op jit(solution)/shard_map/reduce_sum | solution.py:23
  2.1 0.9 %fusion.28 = bf16[2,8192]{1,0:T(2,128)(2,1)S(1)} fusion(bf16[2,8192]{1,0:T(2,128)(2,1)} %param.14, f32[2]{0:T(128)S(1)} %add_rsqrt_fusion, f32[8192]{0:T(1024)} %param.15), kind=kLoop, calls=%fused_computation.34 | loop fusion | flops 65536 | bytes 98312 | tf_op jit(solution)/shard_map/convert_element_type | solution.py:24
  3.1 3.1 %collective-permute-start.2 = (bf16[2,8320]{1,0:T(2,128)(2,1)S(1)}, bf16[2,8320]{1,0:T(2,128)(2,1)S(1)}, u32[]{:S(2)}, u32[]{:S(2)}) collective-permute-start(bf16[2,8320]{1,0:T(2,128)(2,1)S(1)} %pad_maximum_fusion.2), channel_id=1, source_target_pairs={{0,4},{1,5},{2,6},{3,7},{4,0},{5,1},{6,2},{7,3},{8,12},{9,13},{10,... | collective-permute-start | bytes 99848 | tf_op jit(solution)/shard_map/ppermute | solution.py:80
  6.2 2.6 %collective-permute-start.1 = (bf16[2,8320]{1,0:T(2,128)(2,1)S(1)}, bf16[2,8320]{1,0:T(2,128)(2,1)S(1)}, u32[]{:S(2)}, u32[]{:S(2)}) collective-permute-start(bf16[2,8320]{1,0:T(2,128)(2,1)S(1)} %pad_maximum_fusion.2), channel_id=1, source_target_pairs={{0,8},{1,9},{2,10},{3,11},{4,12},{5,13},{6,14},{7,15},{8,0},{9,1},... | collective-permute-start | bytes 99848 | tf_op jit(solution)/shard_map/ppermute | solution.py:80
  8.8 4.1 %bring.2.query_vmem = bf16[8192,512]{1,0:T(8,128)(2,1)S(1)} custom-call(s32[2]{0:T(128)S(1)} %pad_add_fusion.refs_0_.where_ref, bf16[8192,512]{1,0:T(8,128)(2,1)} %refs_1_.2), custom_call_target="tpu_custom_call" | custom-call | bytes 16777216 | tf_op jit(solution)/shard_map/bring/pallas_call | solution.py:321
  13.0 1.5 %collective-permute-done = bf16[2,8320]{1,0:T(2,128)(2,1)S(1)} collective-permute-done((bf16[2,8320]{1,0:T(2,128)(2,1)S(1)}, bf16[2,8320]{1,0:T(2,128)(2,1)S(1)}, u32[]{:S(2)}, u32[]{:S(2)}) %collective-permute-start) | collective-permute-done | bytes 33312 | tf_op jit(solution)/shard_map/ppermute | solution.py:80
  14.5 0.1 broadcast_select_fusion.7
  14.6 0.2 pad_maximum_fusion
  14.8 7.2 %all_gather.6 = bf16[32,8320]{1,0:T(8,128)(2,1)S(1)} all-gather(bf16[8,8320]{1,0:T(8,128)(2,1)S(1)} %pad_maximum_fusion), channel_id=1, replica_groups={{0,1,2,3},{4,5,6,7},{8,9,10,11},{12,13,14,15},{16,17,18,19},{20,21,22,2..., dimensions={0}, use_global_device_ids=true | all-gather | bytes 665600 | tf_op jit(solution)/shard_map/all_gather | solution.py:122
  22.1 3.2 %query_halves.1 = (f32[8,2,8448]{2,1,0:T(2,128)S(1)}, f32[8,2,8448]{2,1,0:T(2,128)S(1)}) custom-call(s32[2]{0:T(128)S(1)} %pad_add_fusion.refs_0_.where_ref, bf16[32,8192]{1,0:T(8,128)(2,1)S(1)} %slice.26.rows_ref, bf16[32,128]{1,0:T(8,128)(2,1)S(1)} %slice.27.marks_ref, bf16[8192,512]{1,0:T(8,128)(2,1)S(1)} %bring.2.query_vmem, ...), custom_call_target="tpu_custom_call" | custom-call | tf_op jit(solution)/shard_map/query_halves/pallas_call | solution.py:249
  25.3 0.4 collective-permute-start.3
  25.7 1.6 %collective-permute-done.3 = f32[8,2,8448]{2,1,0:T(2,128)S(1)} collective-permute-done((f32[8,2,8448]{2,1,0:T(2,128)S(1)}, f32[8,2,8448]{2,1,0:T(2,128)S(1)}, u32[]{:S(2)}, u32[]{:S(2)}) %collective-permute-start.3) | collective-permute-done | bytes 540704 | tf_op jit(solution)/shard_map/ppermute | solution.py:141
  27.3 0.3 add.45
  27.6 20.0 %all_to_all.10 = f32[8,2,8448]{2,1,0:T(2,128)S(1)} all-to-all(f32[8,2,8448]{2,1,0:T(2,128)S(1)} %add.45), channel_id=1, replica_groups={{0,2,4,6,8,10,12,14},{1,3,5,7,9,11,13,15},{16,18,20,22,24,26,28,30},{17..., dimensions={0} | all-to-all | bytes 1081344 | tf_op jit(solution)/shard_map/all_to_all | solution.py:147
  48.0 0.7 fusion.43
  48.8 0.2 fusion.21
  49.0 0.5 copy-done.7
  49.5 0.5 fusion.18
  50.1 0.7 collective-permute-start.6
  50.7 1.4 %collective-permute-start.5 = (bf16[2,8192]{1,0:T(2,128)(2,1)S(1)}, bf16[2,8192]{1,0:T(2,128)(2,1)S(1)}, u32[]{:S(2)}, u32[]{:S(2)}) collective-permute-start(bf16[2,8192]{1,0:T(2,128)(2,1)S(1)} %bitcast.82), channel_id=1, source_target_pairs={{0,8},{1,9},{2,10},{3,11},{4,12},{5,13},{6,14},{7,15},{8,0},{9,1},... | collective-permute-start | bytes 98312 | tf_op jit(solution)/shard_map/ppermute | solution.py:80
  52.2 2.4 %collective-permute-start.4 = (bf16[2,8192]{1,0:T(2,128)(2,1)S(1)}, bf16[2,8192]{1,0:T(2,128)(2,1)S(1)}, u32[]{:S(2)}, u32[]{:S(2)}) collective-permute-start(bf16[2,8192]{1,0:T(2,128)(2,1)S(1)} %bitcast.83), channel_id=1, source_target_pairs={{0,12},{1,13},{2,14},{3,15},{4,8},{5,9},{6,10},{7,11},{8,4},{9,5},... | collective-permute-start | bytes 98312 | tf_op jit(solution)/shard_map/ppermute | solution.py:80
  54.5 4.0 %bring.3.output_vmem = bf16[512,8192]{1,0:T(8,128)(2,1)S(1)} custom-call(s32[2]{0:T(128)S(1)} %pad_add_fusion.refs_0_.where_ref, bf16[512,8192]{1,0:T(8,128)(2,1)} %refs_1_.3), custom_call_target="tpu_custom_call" | custom-call | bytes 16777216 | tf_op jit(solution)/shard_map/bring/pallas_call | solution.py:321
  58.6 0.1 broadcast_select_fusion.15
  58.8 0.2 pad_maximum_fusion.1
  58.9 6.5 %all_gather.7.rows_ref = bf16[32,8192]{1,0:T(8,128)(2,1)S(1)} all-gather(bf16[8,8192]{1,0:T(8,128)(2,1)S(1)} %pad_maximum_fusion.1), channel_id=1, replica_groups={{0,1,2,3},{4,5,6,7},{8,9,10,11},{12,13,14,15},{16,17,18,19},{20,21,22,2..., dimensions={0}, use_global_device_ids=true | all-gather | bytes 655360 | tf_op jit(solution)/shard_map/all_gather | solution.py:122
  65.4 3.0 %output_halves.1 = (f32[8,2,8192]{2,1,0:T(2,128)S(1)}, f32[8,2,8192]{2,1,0:T(2,128)S(1)}) custom-call(s32[2]{0:T(128)S(1)} %pad_add_fusion.refs_0_.where_ref, bf16[32,8192]{1,0:T(8,128)(2,1)S(1)} %all_gather.7.rows_ref, bf16[32,128]{1,0:T(8,128)(2,1)S(1)} %slice.27.marks_ref, bf16[512,8192]{1,0:T(8,128)(2,1)S(1)} %bring.3.output_vmem, ...), custom_call_target="tpu_custom_call" | custom-call | tf_op jit(solution)/shard_map/output_halves/pallas_call | solution.py:287
  68.4 0.4 collective-permute-start.7
  68.8 1.6 %collective-permute-done.7 = f32[8,2,8192]{2,1,0:T(2,128)S(1)} collective-permute-done((f32[8,2,8192]{2,1,0:T(2,128)S(1)}, f32[8,2,8192]{2,1,0:T(2,128)S(1)}, u32[]{:S(2)}, u32[]{:S(2)}) %collective-permute-start.7) | collective-permute-done | bytes 524320 | tf_op jit(solution)/shard_map/ppermute | solution.py:141
  70.4 0.3 add_convert_fusion
  70.7 12.8 %all_to_all.11 = bf16[8,2,8192]{2,1,0:T(2,128)(2,1)S(1)} all-to-all(bf16[8,2,8192]{2,1,0:T(2,128)(2,1)S(1)} %add_convert_fusion), channel_id=1, replica_groups={{0,2,4,6,8,10,12,14},{1,3,5,7,9,11,13,15},{16,18,20,22,24,26,28,30},{17..., dimensions={0} | all-to-all | bytes 524288 | tf_op jit(solution)/shard_map/all_to_all | solution.py:147
  83.4 0.9 %reduce_sum.55 = bf16[2,8192]{1,0:T(2,128)(2,1)} reduce(bf16[8,2,8192]{2,1,0:T(2,128)(2,1)S(1)} %all_to_all.11, bf16[]{:T(256)} %constant.50.clone.1), dimensions={0}, to_apply=%region_5.6 | reduce | flops 114688 | bytes 294914 | tf_op jit(solution)/shard_map/reduce_sum | solution.py:471
  (42 shorter events, 0.8 us)
Async XLA Ops:
  0.0 48.0 %copy-start = (bf16[2,512,1024]{2,1,0:T(8,128)(2,1)S(1)}, bf16[2,512,1024]{2,1,0:T(8,128)(2,1)}, u32[]{:S(2)}) copy-start(bf16[2,512,1024]{2,1,0:T(8,128)(2,1)} %param.23) | copy-start | bytes 6291460
  3.1 9.9 %collective-permute-start.2 = (bf16[2,8320]{1,0:T(2,128)(2,1)S(1)}, bf16[2,8320]{1,0:T(2,128)(2,1)S(1)}, u32[]{:S(2)}, u32[]{:S(2)}) collective-permute-start(bf16[2,8320]{1,0:T(2,128)(2,1)S(1)} %pad_maximum_fusion.2), channel_id=1, source_target_pairs={{0,4},{1,5},{2,6},{3,7},{4,0},{5,1},{6,2},{7,3},{8,12},{9,13},{10,... | collective-permute-start | bytes 99848 | tf_op jit(solution)/shard_map/ppermute | solution.py:80
  6.2 6.8 %collective-permute-start.1 = (bf16[2,8320]{1,0:T(2,128)(2,1)S(1)}, bf16[2,8320]{1,0:T(2,128)(2,1)S(1)}, u32[]{:S(2)}, u32[]{:S(2)}) collective-permute-start(bf16[2,8320]{1,0:T(2,128)(2,1)S(1)} %pad_maximum_fusion.2), channel_id=1, source_target_pairs={{0,8},{1,9},{2,10},{3,11},{4,12},{5,13},{6,14},{7,15},{8,0},{9,1},... | collective-permute-start | bytes 99848 | tf_op jit(solution)/shard_map/ppermute | solution.py:80
  8.7 5.7 %collective-permute-start = (bf16[2,8320]{1,0:T(2,128)(2,1)S(1)}, bf16[2,8320]{1,0:T(2,128)(2,1)S(1)}, u32[]{:S(2)}, u32[]{:S(2)}) collective-permute-start(bf16[2,8320]{1,0:T(2,128)(2,1)S(1)} %pad_maximum_fusion.2), channel_id=1, source_target_pairs={{0,12},{1,13},{2,14},{3,15},{4,8},{5,9},{6,10},{7,11},{8,4},{9,5},... | collective-permute-start | bytes 99848 | tf_op jit(solution)/shard_map/ppermute | solution.py:80
  8.8 13.2 %copy-start.2 = (bf16[4,8192,16]{1,2,0:T(8,128)(2,1)S(1)}, bf16[4,8192,16]{1,2,0:T(8,128)(2,1)}, u32[]{:S(2)}) copy-start(bf16[4,8192,16]{1,2,0:T(8,128)(2,1)} %param.19) | copy-start | bytes 3145732
  8.8 13.3 %copy-start.3 = (bf16[4,16,8192]{2,1,0:T(8,128)(2,1)S(1)}, bf16[4,16,8192]{2,1,0:T(8,128)(2,1)}, u32[]{:S(2)}) copy-start(bf16[4,16,8192]{2,1,0:T(8,128)(2,1)} %param.20) | copy-start | bytes 3145732
  13.0 9.1 %copy-start.1 = (bf16[8192,128]{1,0:T(8,128)(2,1)S(1)}, bf16[8192,128]{1,0:T(8,128)(2,1)}, u32[]{:S(2)}) copy-start(bf16[8192,128]{1,0:T(8,128)(2,1)} %keyval_vmem.1) | copy-start | bytes 6291460
  25.3 22.4 %copy-start.6 = (s32[2]{0:T(128)S(1)}, s32[2]{0:T(128)}, u32[]{:S(2)}) copy-start(s32[2]{0:T(128)} %param.25) | copy-start | bytes 28
  25.3 2.0 %collective-permute-start.3 = (f32[8,2,8448]{2,1,0:T(2,128)S(1)}, f32[8,2,8448]{2,1,0:T(2,128)S(1)}, u32[]{:S(2)}, u32[]{:S(2)}) collective-permute-start(f32[8,2,8448]{2,1,0:T(2,128)S(1)} %get-tuple-element.21), channel_id=1, source_target_pairs={{0,1},{1,0},{2,3},{3,2},{4,5},{5,4},{6,7},{7,6},{8,9},{9,8},{10,11... | collective-permute-start | bytes 1622024 | tf_op jit(solution)/shard_map/ppermute | solution.py:141
  47.9 1.6 %copy-start.7 = (bf16[2,512,1024]{2,1,0:T(8,128)(2,1)S(1)}, bf16[2,512,1024]{2,1,0:T(8,128)(2,1)}, u32[]{:S(2)}) copy-start(bf16[2,512,1024]{2,1,0:T(8,128)(2,1)} %param.24) | copy-start | bytes 6291460
  50.0 15.4 %copy-start.4 = (bf16[4,8192,16]{1,2,0:T(8,128)(2,1)S(1)}, bf16[4,8192,16]{1,2,0:T(8,128)(2,1)}, u32[]{:S(2)}) copy-start(bf16[4,8192,16]{1,2,0:T(8,128)(2,1)} %param.21) | copy-start | bytes 3145732
  50.0 15.4 %copy-start.5 = (bf16[4,16,8192]{2,1,0:T(8,128)(2,1)S(1)}, bf16[4,16,8192]{2,1,0:T(8,128)(2,1)}, u32[]{:S(2)}) copy-start(bf16[4,16,8192]{2,1,0:T(8,128)(2,1)} %param.22) | copy-start | bytes 3145732
  50.1 8.5 %collective-permute-start.6 = (bf16[2,8192]{1,0:T(2,128)(2,1)S(1)}, bf16[2,8192]{1,0:T(2,128)(2,1)S(1)}, u32[]{:S(2)}, u32[]{:S(2)}) collective-permute-start(bf16[2,8192]{1,0:T(2,128)(2,1)S(1)} %bitcast.81), channel_id=1, source_target_pairs={{0,4},{1,5},{2,6},{3,7},{4,0},{5,1},{6,2},{7,3},{8,12},{9,13},{10,... | collective-permute-start | bytes 98312 | tf_op jit(solution)/shard_map/ppermute | solution.py:80
  50.7 7.8 %collective-permute-start.5 = (bf16[2,8192]{1,0:T(2,128)(2,1)S(1)}, bf16[2,8192]{1,0:T(2,128)(2,1)S(1)}, u32[]{:S(2)}, u32[]{:S(2)}) collective-permute-start(bf16[2,8192]{1,0:T(2,128)(2,1)S(1)} %bitcast.82), channel_id=1, source_target_pairs={{0,8},{1,9},{2,10},{3,11},{4,12},{5,13},{6,14},{7,15},{8,0},{9,1},... | collective-permute-start | bytes 98312 | tf_op jit(solution)/shard_map/ppermute | solution.py:80
  52.2 6.4 %collective-permute-start.4 = (bf16[2,8192]{1,0:T(2,128)(2,1)S(1)}, bf16[2,8192]{1,0:T(2,128)(2,1)S(1)}, u32[]{:S(2)}, u32[]{:S(2)}) collective-permute-start(bf16[2,8192]{1,0:T(2,128)(2,1)S(1)} %bitcast.83), channel_id=1, source_target_pairs={{0,12},{1,13},{2,14},{3,15},{4,8},{5,9},{6,10},{7,11},{8,4},{9,5},... | collective-permute-start | bytes 98312 | tf_op jit(solution)/shard_map/ppermute | solution.py:80
  68.4 2.0 %collective-permute-start.7 = (f32[8,2,8192]{2,1,0:T(2,128)S(1)}, f32[8,2,8192]{2,1,0:T(2,128)S(1)}, u32[]{:S(2)}, u32[]{:S(2)}) collective-permute-start(f32[8,2,8192]{2,1,0:T(2,128)S(1)} %get-tuple-element.28), channel_id=1, source_target_pairs={{0,1},{1,0},{2,3},{3,2},{4,5},{5,4},{6,7},{7,6},{8,9},{9,8},{10,11... | collective-permute-start | bytes 1572872 | tf_op jit(solution)/shard_map/ppermute | solution.py:141

commit v8 on v7

--- a/solution.py
+++ b/solution.py
@@ -155,6 +155,7 @@
 
 
 CHUNKS = 8
+NORM_VMEM = 57000 * 1024
 LANES = 128
 KERNEL_VMEM = 24 * 1024 * 1024
 BRING_VMEM = 40 * 1024 * 1024
@@ -331,6 +332,60 @@
     )(where, *arrays)
 
 
+def norm_kernel(
+    hidden_hbm, gain_hbm, adapter_hbm, slot_hbm,
+    sent_ref, hidden_ref, gain_ref, adapter_ref, slot_ref, sems,
+):
+    copies = [
+        pltpu.make_async_copy(source, target, sems.at[k])
+        for k, (source, target) in enumerate(
+            (
+                (adapter_hbm, adapter_ref),
+                (slot_hbm, slot_ref),
+                (hidden_hbm, hidden_ref),
+                (gain_hbm, gain_ref),
+            )
+        )
+    ]
+    for copy in copies:
+        copy.start()
+    rows, width = hidden_ref.shape
+    copies[2].wait()
+    values = hidden_ref[...].astype(jnp.float32)
+    factor = lax.rsqrt(jnp.mean(values * values, axis=-1, keepdims=True) + norm_eps)
+    copies[3].wait()
+    sent_ref[:, :width] = (values * factor * gain_ref[...]).astype(jnp.bfloat16)
+    copies[0].wait()
+    copies[1].wait()
+    row = lax.broadcasted_iota(jnp.int32, (rows, LANES), 0)
+    lane = lax.broadcasted_iota(jnp.int32, (rows, LANES), 1)
+    marks = jnp.zeros((rows, LANES), jnp.int32)
+    for r in range(rows):
+        slot = slot_ref[adapter_ref[r]]
+        digit = jnp.where(lane == 0, slot // 32, jnp.where(lane == 1, slot % 32, 0))
+        marks = jnp.where(row == r, digit, marks)
+    sent_ref[:, width:] = marks.astype(jnp.float32).astype(jnp.bfloat16)
+
+
+def norm_and_marks(hidden, gain, request_adapter, adapter_slot):
+    rows, width = hidden.shape
+    return pl.pallas_call(
+        norm_kernel,
+        in_specs=[pl.BlockSpec(memory_space=pl.ANY)] * 4,
+        out_specs=whole_block((rows, width + LANES)),
+        out_shape=jax.ShapeDtypeStruct((rows, width + LANES), jnp.bfloat16),
+        scratch_shapes=[
+            pltpu.VMEM(hidden.shape, jnp.bfloat16),
+            pltpu.VMEM((1, width), jnp.float32),
+            pltpu.SMEM(request_adapter.shape, jnp.int32),
+            pltpu.SMEM(adapter_slot.shape, jnp.int32),
+            pltpu.SemaphoreType.DMA((4,)),
+        ],
+        compiler_params=pltpu.CompilerParams(vmem_limit_bytes=NORM_VMEM),
+        name="norm_and_marks",
+    )(hidden, gain.reshape(1, width), request_adapter, adapter_slot)
+
+
 def by_rank(factor):
     return factor.transpose(0, 2, 1).reshape(-1, factor.shape[1])
 
@@ -356,13 +411,16 @@
     local_rows = hidden.shape[0]
     col_width = query_weight.shape[1]
 
-    normalized_input = norm_rows(hidden, gain)
-    slot_ids = lookup_slots(request_adapter, adapter_slot)
-    digits = jnp.stack([slot_ids // 32, slot_ids % 32], axis=1).astype(jnp.bfloat16)
-    sent = jnp.concatenate([normalized_input, jnp.pad(digits, ((0, 0), (0, 126)))], axis=1)
+    aligned = col_width % LANES == 0 and key_value_weight.shape[1] % LANES == 0
+    if aligned:
+        sent = norm_and_marks(hidden, gain, request_adapter, adapter_slot)
+    else:
+        normalized_input = norm_rows(hidden, gain)
+        slot_ids = lookup_slots(request_adapter, adapter_slot)
+        digits = jnp.stack([slot_ids // 32, slot_ids % 32], axis=1).astype(jnp.bfloat16)
+        sent = jnp.concatenate([normalized_input, jnp.pad(digits, ((0, 0), (0, 126)))], axis=1)
     first_slot = lax.axis_index("pool") * own_slots
     where = jnp.stack([lax.axis_index("pool"), first_slot]).astype(jnp.int32)
-    aligned = col_width % LANES == 0 and key_value_weight.shape[1] % LANES == 0
     if aligned:
 
         def bring_query(rows):

time: 84.6 us -> 83.3 us (0.985)
  other arithmetic: 5.48 us -> 2.51 us
  Pallas kernels: 14.3 us -> 16.1 us
    reduce_sum x2 -> x0, other arithmetic: 1.94 us -> none  [the longest x1 1 us: lookup_slots(): return jnp.sum(jnp.where(matches, adapter_slot[None, :], 0), axis=1)]
    pallas_call x0 -> x1, Pallas kernels: none -> 1.8 us  [norm_and_marks(): pl.pallas_call(norm_kernel, in_specs=[pl.BlockSpec(memory_space=pl.ANY)]...]
    convert_element_type x1 -> x0, other arithmetic: 0.88 us -> none  [norm_rows(): return (values * factor * gain).astype(jnp.bfloat16)]
where the time goes in v8:
time: 83.3 us; the launch traced here: 83 us
  blocking collectives  46.3 us (56%)
  Pallas kernels  16.1 us (19%)
  starting transfers between devices  11 us (13%)
  waiting for transfers between devices  4.83 us (6%)
  other arithmetic  2.51 us (3%)
  matrix products  1.38 us (2%)
    all_to_all x2, blocking collectives, exchange_chips(): lax.all_to_all(blocks, 'pool', 0, 0, tiled=True, axis_index_groups=same_c...  32.6 us
    all_gather x2, blocking collectives, gather_rows(): lax.all_gather(rows, 'pool', axis=0, axis_index_groups=fours, tiled=True)  13.8 us
    ppermute x6, starting transfers between devices, exchange_quads(): lax.ppermute(rows, 'pool', [(i, i ^ k * step) for i in range(count)])  10.1 us
    pallas_call x2, Pallas kernels, bring(): pl.pallas_call(bring_kernel, in_specs=[pl.BlockSpec(memory_space=pltpu.SM...  8.17 us
    pallas_call x1, Pallas kernels, query_halves(): pl.pallas_call(query_kernel, in_specs=[pl.BlockSpec(memory_space=pltpu.SM...  3.18 us
    ppermute x2, waiting for transfers between devices, swap_cores(): return lax.ppermute(block, 'pool', [(i, i ^ 1) for i in range(count)])  3.15 us
    pallas_call x1, Pallas kernels, output_halves(): pl.pallas_call(output_kernel, in_specs=[pl.BlockSpec(memory_space=pltpu.S...  2.95 us
    pallas_call x1, Pallas kernels, norm_and_marks(): pl.pallas_call(norm_kernel, in_specs=[pl.BlockSpec(memory_space=pl.ANY)]...  1.8 us
  transfers between devices with their start and end apart: 8, of which 3 were waited for; matrix products, arithmetic and copies ran while one was open for 0% of the time, Pallas kernels for 10%

profile of v8, /device:TPU:0, one launch (start us, length us, event | category | flops | bytes accessed | tf_op | source)
XLA Modules:
  0.0 83.0 jit_solution(4708917900884890690)
XLA Ops:
  0.0 1.8 %norm_and_marks.1 = bf16[2,8320]{1,0:T(2,128)(2,1)} custom-call(bf16[2,8192]{1,0:T(2,128)(2,1)} %hidden_hbm.1, f32[1,8192]{1,0:T(1,128)} %bitcast.79, s32[2]{0:T(128)} %adapter_hbm.1, s32[64]{0:T(128)} %slot_hbm.1), custom_call_target="tpu_custom_call" | custom-call | tf_op jit(solution)/shard_map/norm_and_marks/pallas_call | solution.py:372
  1.8 3.1 %collective-permute-start.2 = (bf16[2,8320]{1,0:T(2,128)(2,1)}, bf16[2,8320]{1,0:T(2,128)(2,1)S(1)}, u32[]{:S(2)}, u32[]{:S(2)}) collective-permute-start(bf16[2,8320]{1,0:T(2,128)(2,1)} %norm_and_marks.1), channel_id=1, source_target_pairs={{0,4},{1,5},{2,6},{3,7},{4,0},{5,1},{6,2},{7,3},{8,12},{9,13},{10,... | collective-permute-start | bytes 99848 | tf_op jit(solution)/shard_map/ppermute | solution.py:80
  4.9 2.6 %collective-permute-start.1 = (bf16[2,8320]{1,0:T(2,128)(2,1)}, bf16[2,8320]{1,0:T(2,128)(2,1)S(1)}, u32[]{:S(2)}, u32[]{:S(2)}) collective-permute-start(bf16[2,8320]{1,0:T(2,128)(2,1)} %norm_and_marks.1), channel_id=1, source_target_pairs={{0,8},{1,9},{2,10},{3,11},{4,12},{5,13},{6,14},{7,15},{8,0},{9,1},... | collective-permute-start | bytes 99848 | tf_op jit(solution)/shard_map/ppermute | solution.py:80
  7.6 4.1 %bring.2.query_vmem = bf16[8192,512]{1,0:T(8,128)(2,1)S(1)} custom-call(s32[2]{0:T(128)S(1)} %pad_add_fusion.refs_0_.where_ref, bf16[8192,512]{1,0:T(8,128)(2,1)} %refs_1_.2), custom_call_target="tpu_custom_call" | custom-call | bytes 16777216 | tf_op jit(solution)/shard_map/bring/pallas_call | solution.py:322
  11.8 1.7 %collective-permute-done = bf16[2,8320]{1,0:T(2,128)(2,1)S(1)} collective-permute-done((bf16[2,8320]{1,0:T(2,128)(2,1)}, bf16[2,8320]{1,0:T(2,128)(2,1)S(1)}, u32[]{:S(2)}, u32[]{:S(2)}) %collective-permute-start) | collective-permute-done | bytes 33312 | tf_op jit(solution)/shard_map/ppermute | solution.py:80
  13.4 0.1 broadcast_select_fusion.7
  13.6 0.2 pad_maximum_fusion
  13.7 7.2 %all_gather.6 = bf16[32,8320]{1,0:T(8,128)(2,1)S(1)} all-gather(bf16[8,8320]{1,0:T(8,128)(2,1)S(1)} %pad_maximum_fusion), channel_id=1, replica_groups={{0,1,2,3},{4,5,6,7},{8,9,10,11},{12,13,14,15},{16,17,18,19},{20,21,22,2..., dimensions={0}, use_global_device_ids=true | all-gather | bytes 665600 | tf_op jit(solution)/shard_map/all_gather | solution.py:122
  21.0 3.2 %query_halves.1 = (f32[8,2,8448]{2,1,0:T(2,128)S(1)}, f32[8,2,8448]{2,1,0:T(2,128)S(1)}) custom-call(s32[2]{0:T(128)S(1)} %pad_add_fusion.refs_0_.where_ref, bf16[32,8192]{1,0:T(8,128)(2,1)S(1)} %slice.26.rows_ref, bf16[32,128]{1,0:T(8,128)(2,1)S(1)} %slice.27.marks_ref, bf16[8192,512]{1,0:T(8,128)(2,1)S(1)} %bring.2.query_vmem, ...), custom_call_target="tpu_custom_call" | custom-call | tf_op jit(solution)/shard_map/query_halves/pallas_call | solution.py:250
  24.2 0.4 collective-permute-start.3
  24.7 1.6 %collective-permute-done.3 = f32[8,2,8448]{2,1,0:T(2,128)S(1)} collective-permute-done((f32[8,2,8448]{2,1,0:T(2,128)S(1)}, f32[8,2,8448]{2,1,0:T(2,128)S(1)}, u32[]{:S(2)}, u32[]{:S(2)}) %collective-permute-start.3) | collective-permute-done | bytes 540704 | tf_op jit(solution)/shard_map/ppermute | solution.py:141
  26.2 0.3 add.12
  26.5 19.8 %all_to_all.10 = f32[8,2,8448]{2,1,0:T(2,128)S(1)} all-to-all(f32[8,2,8448]{2,1,0:T(2,128)S(1)} %add.12), channel_id=1, replica_groups={{0,2,4,6,8,10,12,14},{1,3,5,7,9,11,13,15},{16,18,20,22,24,26,28,30},{17..., dimensions={0} | all-to-all | bytes 1081344 | tf_op jit(solution)/shard_map/all_to_all | solution.py:147
  46.3 0.1 slice_reduce_fusion
  46.7 0.1 fusion.26
  46.8 0.7 fusion.34
  47.5 0.2 fusion.21
  47.8 0.5 copy-done.8
  48.2 0.5 fusion.18
  48.8 0.7 collective-permute-start.6
  49.5 1.4 %collective-permute-start.5 = (bf16[2,8192]{1,0:T(2,128)(2,1)S(1)}, bf16[2,8192]{1,0:T(2,128)(2,1)S(1)}, u32[]{:S(2)}, u32[]{:S(2)}) collective-permute-start(bf16[2,8192]{1,0:T(2,128)(2,1)S(1)} %bitcast.83), channel_id=1, source_target_pairs={{0,8},{1,9},{2,10},{3,11},{4,12},{5,13},{6,14},{7,15},{8,0},{9,1},... | collective-permute-start | bytes 98312 | tf_op jit(solution)/shard_map/ppermute | solution.py:80
  50.9 2.4 %collective-permute-start.4 = (bf16[2,8192]{1,0:T(2,128)(2,1)S(1)}, bf16[2,8192]{1,0:T(2,128)(2,1)S(1)}, u32[]{:S(2)}, u32[]{:S(2)}) collective-permute-start(bf16[2,8192]{1,0:T(2,128)(2,1)S(1)} %bitcast.84), channel_id=1, source_target_pairs={{0,12},{1,13},{2,14},{3,15},{4,8},{5,9},{6,10},{7,11},{8,4},{9,5},... | collective-permute-start | bytes 98312 | tf_op jit(solution)/shard_map/ppermute | solution.py:80
  53.3 4.0 %bring.3.output_vmem = bf16[512,8192]{1,0:T(8,128)(2,1)S(1)} custom-call(s32[2]{0:T(128)S(1)} %pad_add_fusion.refs_0_.where_ref, bf16[512,8192]{1,0:T(8,128)(2,1)} %refs_1_.3), custom_call_target="tpu_custom_call" | custom-call | bytes 16777216 | tf_op jit(solution)/shard_map/bring/pallas_call | solution.py:322
  57.3 0.1 broadcast_select_fusion.15
  57.5 0.2 pad_maximum_fusion.1
  57.7 6.5 %all_gather.7.rows_ref = bf16[32,8192]{1,0:T(8,128)(2,1)S(1)} all-gather(bf16[8,8192]{1,0:T(8,128)(2,1)S(1)} %pad_maximum_fusion.1), channel_id=1, replica_groups={{0,1,2,3},{4,5,6,7},{8,9,10,11},{12,13,14,15},{16,17,18,19},{20,21,22,2..., dimensions={0}, use_global_device_ids=true | all-gather | bytes 655360 | tf_op jit(solution)/shard_map/all_gather | solution.py:122
  64.2 3.0 %output_halves.1 = (f32[8,2,8192]{2,1,0:T(2,128)S(1)}, f32[8,2,8192]{2,1,0:T(2,128)S(1)}) custom-call(s32[2]{0:T(128)S(1)} %pad_add_fusion.refs_0_.where_ref, bf16[32,8192]{1,0:T(8,128)(2,1)S(1)} %all_gather.7.rows_ref, bf16[32,128]{1,0:T(8,128)(2,1)S(1)} %slice.27.marks_ref, bf16[512,8192]{1,0:T(8,128)(2,1)S(1)} %bring.3.output_vmem, ...), custom_call_target="tpu_custom_call" | custom-call | tf_op jit(solution)/shard_map/output_halves/pallas_call | solution.py:288
  67.1 0.4 collective-permute-start.7
  67.6 1.6 %collective-permute-done.7 = f32[8,2,8192]{2,1,0:T(2,128)S(1)} collective-permute-done((f32[8,2,8192]{2,1,0:T(2,128)S(1)}, f32[8,2,8192]{2,1,0:T(2,128)S(1)}, u32[]{:S(2)}, u32[]{:S(2)}) %collective-permute-start.7) | collective-permute-done | bytes 524320 | tf_op jit(solution)/shard_map/ppermute | solution.py:141
  69.1 0.3 add_convert_fusion
  69.4 12.8 %all_to_all.11 = bf16[8,2,8192]{2,1,0:T(2,128)(2,1)S(1)} all-to-all(bf16[8,2,8192]{2,1,0:T(2,128)(2,1)S(1)} %add_convert_fusion), channel_id=1, replica_groups={{0,2,4,6,8,10,12,14},{1,3,5,7,9,11,13,15},{16,18,20,22,24,26,28,30},{17..., dimensions={0} | all-to-all | bytes 524288 | tf_op jit(solution)/shard_map/all_to_all | solution.py:147
  82.2 0.9 %reduce_sum.32 = bf16[2,8192]{1,0:T(2,128)(2,1)} reduce(bf16[8,2,8192]{2,1,0:T(2,128)(2,1)S(1)} %all_to_all.11, bf16[]{:T(256)} %constant.20.clone.1), dimensions={0}, to_apply=%region_3.4 | reduce | flops 114688 | bytes 294914 | tf_op jit(solution)/shard_map/reduce_sum | solution.py:529
  (37 shorter events, 0.4 us)
Async XLA Ops:
  0.0 46.8 %copy-start = (bf16[2,512,1024]{2,1,0:T(8,128)(2,1)S(1)}, bf16[2,512,1024]{2,1,0:T(8,128)(2,1)}, u32[]{:S(2)}) copy-start(bf16[2,512,1024]{2,1,0:T(8,128)(2,1)} %param.23) | copy-start | bytes 6291460
  1.8 9.9 %collective-permute-start.2 = (bf16[2,8320]{1,0:T(2,128)(2,1)}, bf16[2,8320]{1,0:T(2,128)(2,1)S(1)}, u32[]{:S(2)}, u32[]{:S(2)}) collective-permute-start(bf16[2,8320]{1,0:T(2,128)(2,1)} %norm_and_marks.1), channel_id=1, source_target_pairs={{0,4},{1,5},{2,6},{3,7},{4,0},{5,1},{6,2},{7,3},{8,12},{9,13},{10,... | collective-permute-start | bytes 99848 | tf_op jit(solution)/shard_map/ppermute | solution.py:80
  4.9 6.8 %collective-permute-start.1 = (bf16[2,8320]{1,0:T(2,128)(2,1)}, bf16[2,8320]{1,0:T(2,128)(2,1)S(1)}, u32[]{:S(2)}, u32[]{:S(2)}) collective-permute-start(bf16[2,8320]{1,0:T(2,128)(2,1)} %norm_and_marks.1), channel_id=1, source_target_pairs={{0,8},{1,9},{2,10},{3,11},{4,12},{5,13},{6,14},{7,15},{8,0},{9,1},... | collective-permute-start | bytes 99848 | tf_op jit(solution)/shard_map/ppermute | solution.py:80
  7.5 5.9 %collective-permute-start = (bf16[2,8320]{1,0:T(2,128)(2,1)}, bf16[2,8320]{1,0:T(2,128)(2,1)S(1)}, u32[]{:S(2)}, u32[]{:S(2)}) collective-permute-start(bf16[2,8320]{1,0:T(2,128)(2,1)} %norm_and_marks.1), channel_id=1, source_target_pairs={{0,12},{1,13},{2,14},{3,15},{4,8},{5,9},{6,10},{7,11},{8,4},{9,5},... | collective-permute-start | bytes 99848 | tf_op jit(solution)/shard_map/ppermute | solution.py:80
  7.6 5.9 %copy-start.6 = (bf16[2,8320]{1,0:T(2,128)(2,1)S(1)}, bf16[2,8320]{1,0:T(2,128)(2,1)}, u32[]{:S(2)}) copy-start(bf16[2,8320]{1,0:T(2,128)(2,1)} %norm_and_marks.1) | copy-start | bytes 99844
  7.6 13.4 %copy-start.2 = (bf16[4,8192,16]{1,2,0:T(8,128)(2,1)S(1)}, bf16[4,8192,16]{1,2,0:T(8,128)(2,1)}, u32[]{:S(2)}) copy-start(bf16[4,8192,16]{1,2,0:T(8,128)(2,1)} %param.19) | copy-start | bytes 3145732
  7.6 13.5 %copy-start.3 = (bf16[4,16,8192]{2,1,0:T(8,128)(2,1)S(1)}, bf16[4,16,8192]{2,1,0:T(8,128)(2,1)}, u32[]{:S(2)}) copy-start(bf16[4,16,8192]{2,1,0:T(8,128)(2,1)} %param.20) | copy-start | bytes 3145732
  11.7 9.3 %copy-start.1 = (bf16[8192,128]{1,0:T(8,128)(2,1)S(1)}, bf16[8192,128]{1,0:T(8,128)(2,1)}, u32[]{:S(2)}) copy-start(bf16[8192,128]{1,0:T(8,128)(2,1)} %keyval_vmem.1) | copy-start | bytes 6291460
  24.2 22.2 %copy-start.7 = (s32[2]{0:T(128)S(1)}, s32[2]{0:T(128)}, u32[]{:S(2)}) copy-start(s32[2]{0:T(128)} %param.25) | copy-start | bytes 28
  24.2 2.0 %collective-permute-start.3 = (f32[8,2,8448]{2,1,0:T(2,128)S(1)}, f32[8,2,8448]{2,1,0:T(2,128)S(1)}, u32[]{:S(2)}, u32[]{:S(2)}) collective-permute-start(f32[8,2,8448]{2,1,0:T(2,128)S(1)} %get-tuple-element.21), channel_id=1, source_target_pairs={{0,1},{1,0},{2,3},{3,2},{4,5},{5,4},{6,7},{7,6},{8,9},{9,8},{10,11... | collective-permute-start | bytes 1622024 | tf_op jit(solution)/shard_map/ppermute | solution.py:141
  46.6 1.6 %copy-start.8 = (bf16[2,512,1024]{2,1,0:T(8,128)(2,1)S(1)}, bf16[2,512,1024]{2,1,0:T(8,128)(2,1)}, u32[]{:S(2)}) copy-start(bf16[2,512,1024]{2,1,0:T(8,128)(2,1)} %param.24) | copy-start | bytes 6291460
  48.8 15.4 %copy-start.4 = (bf16[4,8192,16]{1,2,0:T(8,128)(2,1)S(1)}, bf16[4,8192,16]{1,2,0:T(8,128)(2,1)}, u32[]{:S(2)}) copy-start(bf16[4,8192,16]{1,2,0:T(8,128)(2,1)} %param.21) | copy-start | bytes 3145732
  48.8 15.4 %copy-start.5 = (bf16[4,16,8192]{2,1,0:T(8,128)(2,1)S(1)}, bf16[4,16,8192]{2,1,0:T(8,128)(2,1)}, u32[]{:S(2)}) copy-start(bf16[4,16,8192]{2,1,0:T(8,128)(2,1)} %param.22) | copy-start | bytes 3145732
  48.8 8.5 %collective-permute-start.6 = (bf16[2,8192]{1,0:T(2,128)(2,1)S(1)}, bf16[2,8192]{1,0:T(2,128)(2,1)S(1)}, u32[]{:S(2)}, u32[]{:S(2)}) collective-permute-start(bf16[2,8192]{1,0:T(2,128)(2,1)S(1)} %bitcast.82), channel_id=1, source_target_pairs={{0,4},{1,5},{2,6},{3,7},{4,0},{5,1},{6,2},{7,3},{8,12},{9,13},{10,... | collective-permute-start | bytes 98312 | tf_op jit(solution)/shard_map/ppermute | solution.py:80
  49.5 7.8 %collective-permute-start.5 = (bf16[2,8192]{1,0:T(2,128)(2,1)S(1)}, bf16[2,8192]{1,0:T(2,128)(2,1)S(1)}, u32[]{:S(2)}, u32[]{:S(2)}) collective-permute-start(bf16[2,8192]{1,0:T(2,128)(2,1)S(1)} %bitcast.83), channel_id=1, source_target_pairs={{0,8},{1,9},{2,10},{3,11},{4,12},{5,13},{6,14},{7,15},{8,0},{9,1},... | collective-permute-start | bytes 98312 | tf_op jit(solution)/shard_map/ppermute | solution.py:80
  50.9 6.4 %collective-permute-start.4 = (bf16[2,8192]{1,0:T(2,128)(2,1)S(1)}, bf16[2,8192]{1,0:T(2,128)(2,1)S(1)}, u32[]{:S(2)}, u32[]{:S(2)}) collective-permute-start(bf16[2,8192]{1,0:T(2,128)(2,1)S(1)} %bitcast.84), channel_id=1, source_target_pairs={{0,12},{1,13},{2,14},{3,15},{4,8},{5,9},{6,10},{7,11},{8,4},{9,5},... | collective-permute-start | bytes 98312 | tf_op jit(solution)/shard_map/ppermute | solution.py:80
  67.1 2.0 %collective-permute-start.7 = (f32[8,2,8192]{2,1,0:T(2,128)S(1)}, f32[8,2,8192]{2,1,0:T(2,128)S(1)}, u32[]{:S(2)}, u32[]{:S(2)}) collective-permute-start(f32[8,2,8192]{2,1,0:T(2,128)S(1)} %get-tuple-element.28), channel_id=1, source_target_pairs={{0,1},{1,0},{2,3},{3,2},{4,5},{5,4},{6,7},{7,6},{8,9},{9,8},{10,11... | collective-permute-start | bytes 1572872 | tf_op jit(solution)/shard_map/ppermute | solution.py:141

commit v9 on v8

--- a/solution.py
+++ b/solution.py
@@ -184,7 +184,7 @@
     return jnp.where(slots == place, total, 0.0).astype(jnp.bfloat16)
 
 
-def split_store(values, odd, kept_ref, given_ref, first, add):
+def split_store(values, odd, place, kept_ref, given_ref, first, add):
     width = values.shape[1]
     size = values.shape[0] // 4
     local = kept_ref.shape[1]
@@ -195,7 +195,7 @@
         kept = jnp.where(odd, odd_rows, even_rows)
         given = jnp.where(odd, even_rows, odd_rows)
         for z in range(size // local):
-            k = 2 * z + y
+            k = place(z, y)
             kept_piece = kept[z * local : (z + 1) * local]
             given_piece = given[z * local : (z + 1) * local]
             if add:
@@ -211,6 +211,11 @@
 ):
     me = where_ref[0]
     odd = (me % 2) == 1
+    far = kept_ref.shape[0] // 2
+
+    def place(z, y):
+        return jnp.bitwise_xor((me // 2) % 2, y) * far + jnp.bitwise_xor(me // 4, z)
+
     width = down_vmem.shape[1]
     step = width // CHUNKS
     lifted = own_lift(rows_ref, down_vmem, marks_ref, where_ref[1])
@@ -219,7 +224,7 @@
         delta = adapter_scale * jnp.dot(
             lifted, up_vmem[:, spot], preferred_element_type=jnp.float32
         )
-        split_store(delta, odd, kept_ref, given_ref, k * step, False)
+        split_store(delta, odd, place, kept_ref, given_ref, k * step, False)
     query = None
     for k in range(CHUNKS):
         spot = slice(k * step, (k + 1) * step)
@@ -227,7 +232,7 @@
         query = part if query is None else query + part
     columns = query.shape[1]
     split_store(
-        query, odd, kept_ref, given_ref, pl.multiple_of(me * columns, LANES), True
+        query, odd, place, kept_ref, given_ref, pl.multiple_of(me * columns, LANES), True
     )
     keyval = None
     for k in range(CHUNKS):
@@ -236,7 +241,7 @@
         keyval = part if keyval is None else keyval + part
     none = jnp.zeros_like(keyval)
     both = jnp.concatenate([jnp.where(odd, none, keyval), jnp.where(odd, keyval, none)], axis=1)
-    split_store(both, odd, kept_ref, given_ref, width, False)
+    split_store(both, odd, place, kept_ref, given_ref, width, False)
 
 
 def query_halves(where, gathered, query_weight, key_value_weight, down, up, count, local_rows):
@@ -277,7 +282,7 @@
         part = part + adapter_scale * jnp.dot(
             lifted, up_vmem[:, spot], preferred_element_type=jnp.float32
         )
-        split_store(part, odd, kept_ref, given_ref, k * step, False)
+        split_store(part, odd, lambda z, y: 2 * z + y, kept_ref, given_ref, k * step, False)
 
 
 def output_halves(where, every_row, gathered, output_weight, down, up, count, local_rows):
@@ -390,6 +395,35 @@
     return factor.transpose(0, 2, 1).reshape(-1, factor.shape[1])
 
 
+def permuted(block, offset):
+    count = pool_size()
+    return lax.ppermute(block, "pool", [(i, i ^ offset) for i in range(count)])
+
+
+def in_order(upper, own, other, axis):
+    return jnp.concatenate(
+        [jnp.where(upper, other, own), jnp.where(upper, own, other)], axis=axis
+    )
+
+
+def scatter_chips(pair_sums, query_width):
+    me = lax.axis_index("pool")
+    chips, local, width = pair_sums.shape
+    blocks = pair_sums.reshape(2, chips // 2, local, width)
+    other = permuted(blocks[1], 2)
+    own = blocks[0]
+    query = own[..., :query_width] + other[..., :query_width]
+    keyval = in_order((me & 2) != 0, own[..., query_width:], other[..., query_width:], -1)
+    line = jnp.concatenate([query, keyval], axis=-1)
+    parts = [line[0]] + [permuted(line[k], 4 * k) for k in (1, 2, 3)]
+    query = sum(part[:, :query_width] for part in parts).astype(jnp.bfloat16)
+    pieces = [part[:, query_width:].astype(jnp.bfloat16) for part in parts]
+    low, high = (me & 4) != 0, (me & 8) != 0
+    near = in_order(low, pieces[0], pieces[1], -1)
+    far = in_order(low, pieces[2], pieces[3], -1)
+    return query, in_order(high, near, far, -1)
+
+
 def body(
     hidden,
     gain,
@@ -411,7 +445,9 @@
     local_rows = hidden.shape[0]
     col_width = query_weight.shape[1]
 
-    aligned = col_width % LANES == 0 and key_value_weight.shape[1] % LANES == 0
+    aligned = (
+        count == 16 and col_width % LANES == 0 and key_value_weight.shape[1] % LANES == 0
+    )
     if aligned:
         sent = norm_and_marks(hidden, gain, request_adapter, adapter_slot)
     else:
@@ -455,7 +491,7 @@
             count,
             local_rows,
         )
-        leaving = kept + swap_cores(given)
+        query_rows, keyval_rows = scatter_chips(kept + swap_cores(given), query_width)
     else:
         query_shrunk = owner_shrunk(gathered_rows, query_down_factor, owner_mask)
         lifted_rows = jnp.where(owner_mask[:, :, None], query_shrunk[:, None, :], bf_zero).reshape(
@@ -484,12 +520,11 @@
         there = lax.dynamic_slice_in_dim(pair_delta, first_column, 2 * col_width, 2)
         pair_delta = lax.dynamic_update_slice_in_dim(pair_delta, there + pair_query, first_column, 2)
         leaving = jnp.concatenate([pair_delta, pair_keyval], axis=2)
-    arrived = exchange_chips(leaving)
-    arrived, lengths = lax.optimization_barrier((arrived, lengths))
-    query_rows = jnp.sum(arrived[:, :, :query_width], axis=0).astype(jnp.bfloat16)
-    keyval_rows = arrived[:, :, query_width:].astype(jnp.bfloat16)
-    keyval_rows = keyval_rows.reshape(count // 2, local_rows, 2, -1)
-    keyval_rows = keyval_rows.transpose(1, 0, 2, 3).reshape(local_rows, -1)
+        arrived = exchange_chips(leaving)
+        query_rows = jnp.sum(arrived[:, :, :query_width], axis=0).astype(jnp.bfloat16)
+        keyval_rows = arrived[:, :, query_width:].astype(jnp.bfloat16)
+        keyval_rows = keyval_rows.reshape(count // 2, local_rows, 2, -1)
+        keyval_rows = keyval_rows.transpose(1, 0, 2, 3).reshape(local_rows, -1)
 
     attention_output = attend(query_rows, keyval_rows, key_cache, value_cache, lengths)
     if aligned:

time: 83.3 us -> 80.6 us (0.968)
  blocking collectives: 46.3 us -> 27.3 us
  waiting for transfers between devices: 4.83 us -> 16.6 us
  starting transfers between devices: 11 us -> 15.5 us
    all_to_all x2 -> x1, blocking collectives: 32.6 us -> 13.3 us  [exchange_chips(): lax.all_to_all(blocks, 'pool', 0, 0, tiled=True, axis_index_groups=same_c...]
    ppermute x0 -> x4, waiting for transfers between devices: none -> 12.6 us  [permuted(): return lax.ppermute(block, 'pool', [(i, i ^ offset) for i in range(count)])]
    ppermute x0 -> x4, starting transfers between devices: none -> 5.11 us  [permuted(): return lax.ppermute(block, 'pool', [(i, i ^ offset) for i in range(count)])]
  transfers between devices with their start and end apart: 8 -> 12, of which waited for: 3 -> 8; matrix products, arithmetic and copies ran while one was open for 0% -> 0% of each run, Pallas kernels for 10% -> 10%
where the time goes in v9:
time: 80.6 us; the launch traced here: 80.4 us
  blocking collectives  27.3 us (34%)
  waiting for transfers between devices  16.6 us (21%)
  Pallas kernels  16.1 us (20%)
  starting transfers between devices  15.5 us (19%)
  other arithmetic  2.75 us (3%)
  matrix products  1.38 us (2%)
    all_gather x2, blocking collectives, gather_rows(): lax.all_gather(rows, 'pool', axis=0, axis_index_groups=fours, tiled=True)  13.9 us
    all_to_all x1, blocking collectives, exchange_chips(): lax.all_to_all(blocks, 'pool', 0, 0, tiled=True, axis_index_groups=same_c...  13.3 us
    ppermute x4, waiting for transfers between devices, permuted(): return lax.ppermute(block, 'pool', [(i, i ^ offset) for i in range(count)])  12.6 us
    ppermute x6, starting transfers between devices, exchange_quads(): lax.ppermute(rows, 'pool', [(i, i ^ k * step) for i in range(count)])  9.54 us
    pallas_call x2, Pallas kernels, bring(): pl.pallas_call(bring_kernel, in_specs=[pl.BlockSpec(memory_space=pltpu.SM...  8.17 us
    ppermute x4, starting transfers between devices, permuted(): return lax.ppermute(block, 'pool', [(i, i ^ offset) for i in range(count)])  5.11 us
    ppermute x2, waiting for transfers between devices, swap_cores(): return lax.ppermute(block, 'pool', [(i, i ^ 1) for i in range(count)])  3.15 us
    pallas_call x1, Pallas kernels, query_halves(): pl.pallas_call(query_kernel, in_specs=[pl.BlockSpec(memory_space=pltpu.SM...  3.15 us
  transfers between devices with their start and end apart: 12, of which 8 were waited for; matrix products, arithmetic and copies ran while one was open for 0% of the time, Pallas kernels for 10%

profile of v9, /device:TPU:0, one launch (start us, length us, event | category | flops | bytes accessed | tf_op | source)
XLA Modules:
  0.0 80.4 jit_solution(17796563120533377012)
XLA Ops:
  0.0 1.8 %norm_and_marks.1 = bf16[2,8320]{1,0:T(2,128)(2,1)} custom-call(bf16[2,8192]{1,0:T(2,128)(2,1)} %hidden_hbm.1, f32[1,8192]{1,0:T(1,128)} %bitcast.77, s32[2]{0:T(128)} %adapter_hbm.1, s32[64]{0:T(128)} %slot_hbm.1), custom_call_target="tpu_custom_call" | custom-call | tf_op jit(solution)/shard_map/norm_and_marks/pallas_call | solution.py:377
  1.8 5.1 %collective-permute-start = (bf16[2,8320]{1,0:T(2,128)(2,1)}, bf16[2,8320]{1,0:T(2,128)(2,1)S(1)}, u32[]{:S(2)}, u32[]{:S(2)}) collective-permute-start(bf16[2,8320]{1,0:T(2,128)(2,1)} %norm_and_marks.1), channel_id=1, source_target_pairs={{0,12},{1,13},{2,14},{3,15},{4,8},{5,9},{6,10},{7,11},{8,4},{9,5},... | collective-permute-start | bytes 99848 | tf_op jit(solution)/shard_map/ppermute | solution.py:80
  6.9 0.6 collective-permute-start.2
  7.6 4.1 %bring.2.query_vmem = bf16[8192,512]{1,0:T(8,128)(2,1)S(1)} custom-call(s32[2]{0:T(128)S(1)} %pad_add_fusion.refs_0_.where_ref, bf16[8192,512]{1,0:T(8,128)(2,1)} %refs_1_.2), custom_call_target="tpu_custom_call" | custom-call | bytes 16777216 | tf_op jit(solution)/shard_map/bring/pallas_call | solution.py:327
  12.3 7.4 %all_gather.6 = bf16[32,8320]{1,0:T(8,128)(2,1)S(1)} all-gather(bf16[8,8320]{1,0:T(8,128)(2,1)S(1)} %pad_maximum_fusion.1), channel_id=1, replica_groups={{0,1,2,3},{4,5,6,7},{8,9,10,11},{12,13,14,15},{16,17,18,19},{20,21,22,2..., dimensions={0}, use_global_device_ids=true | all-gather | bytes 665600 | tf_op jit(solution)/shard_map/all_gather | solution.py:122
  19.8 3.1 %query_halves.1 = (f32[8,2,8448]{2,1,0:T(2,128)S(1)}, f32[8,2,8448]{2,1,0:T(2,128)S(1)}) custom-call(s32[2]{0:T(128)S(1)} %pad_add_fusion.refs_0_.where_ref, bf16[32,8192]{1,0:T(8,128)(2,1)S(1)} %slice.86.rows_ref, bf16[32,128]{1,0:T(8,128)(2,1)S(1)} %slice.87.marks_ref, bf16[8192,512]{1,0:T(8,128)(2,1)S(1)} %bring.2.query_vmem, ...), custom_call_target="tpu_custom_call" | custom-call | tf_op jit(solution)/shard_map/query_halves/pallas_call | solution.py:255
  22.9 0.4 collective-permute-start.3
  23.3 1.6 %collective-permute-done.3 = f32[8,2,8448]{2,1,0:T(2,128)S(1)} collective-permute-done((f32[8,2,8448]{2,1,0:T(2,128)S(1)}, f32[8,2,8448]{2,1,0:T(2,128)S(1)}, u32[]{:S(2)}, u32[]{:S(2)}) %collective-permute-start.3) | collective-permute-done | bytes 540704 | tf_op jit(solution)/shard_map/ppermute | solution.py:141
  24.9 0.3 add.24
  25.2 0.9 %collective-permute-start.4 = (f32[4,2,8448]{2,1,0:T(2,128)S(1)}, f32[4,2,8448]{2,1,0:T(2,128)S(1)}, u32[]{:S(2)}, u32[]{:S(2)}) collective-permute-start(f32[4,2,8448]{2,1,0:T(2,128)S(1)} %slice.89), channel_id=1, source_target_pairs={{0,2},{1,3},{2,0},{3,1},{4,6},{5,7},{6,4},{7,5},{8,10},{9,11},{10,... | collective-permute-start | bytes 811016 | tf_op jit(solution)/shard_map/ppermute | solution.py:400
  26.1 7.9 %collective-permute-done.4 = f32[4,2,8448]{2,1,0:T(2,128)S(1)} collective-permute-done((f32[4,2,8448]{2,1,0:T(2,128)S(1)}, f32[4,2,8448]{2,1,0:T(2,128)S(1)}, u32[]{:S(2)}, u32[]{:S(2)}) %collective-permute-start.4) | collective-permute-done | bytes 270368 | tf_op jit(solution)/shard_map/ppermute | solution.py:400
  34.4 2.2 %collective-permute-start.6 = (f32[2,8704]{1,0:T(2,128)S(1)}, f32[2,8704]{1,0:T(2,128)S(1)}, u32[]{:S(2)}, u32[]{:S(2)}) collective-permute-start(f32[2,8704]{1,0:T(2,128)S(1)} %get-tuple-element.29), channel_id=1, source_target_pairs={{0,8},{1,9},{2,10},{3,11},{4,12},{5,13},{6,14},{7,15},{8,0},{9,1},... | collective-permute-start | bytes 208904 | tf_op jit(solution)/shard_map/ppermute | solution.py:400
  36.6 1.5 %collective-permute-start.7 = (f32[2,8704]{1,0:T(2,128)S(1)}, f32[2,8704]{1,0:T(2,128)S(1)}, u32[]{:S(2)}, u32[]{:S(2)}) collective-permute-start(f32[2,8704]{1,0:T(2,128)S(1)} %get-tuple-element.28), channel_id=1, source_target_pairs={{0,12},{1,13},{2,14},{3,15},{4,8},{5,9},{6,10},{7,11},{8,4},{9,5},... | collective-permute-start | bytes 208904 | tf_op jit(solution)/shard_map/ppermute | solution.py:400
  38.2 0.5 collective-permute-start.5
  38.7 3.1 %collective-permute-done.6 = f32[2,8704]{1,0:T(2,128)S(1)} collective-permute-done((f32[2,8704]{1,0:T(2,128)S(1)}, f32[2,8704]{1,0:T(2,128)S(1)}, u32[]{:S(2)}, u32[]{:S(2)}) %collective-permute-start.6) | collective-permute-done | bytes 69664 | tf_op jit(solution)/shard_map/ppermute | solution.py:400
  41.8 1.1 %collective-permute-done.7 = f32[2,8704]{1,0:T(2,128)S(1)} collective-permute-done((f32[2,8704]{1,0:T(2,128)S(1)}, f32[2,8704]{1,0:T(2,128)S(1)}, u32[]{:S(2)}, u32[]{:S(2)}) %collective-permute-start.7) | collective-permute-done | bytes 69664 | tf_op jit(solution)/shard_map/ppermute | solution.py:400
  42.9 0.5 collective-permute-done.5
  43.6 0.7 fusion.37
  44.4 0.2 fusion.21
  44.6 0.4 copy-done.8
  45.0 0.5 fusion.18
  45.6 1.0 %collective-permute-start.10 = (bf16[2,8192]{1,0:T(2,128)(2,1)S(1)}, bf16[2,8192]{1,0:T(2,128)(2,1)S(1)}, u32[]{:S(2)}, u32[]{:S(2)}) collective-permute-start(bf16[2,8192]{1,0:T(2,128)(2,1)S(1)} %bitcast.80), channel_id=1, source_target_pairs={{0,4},{1,5},{2,6},{3,7},{4,0},{5,1},{6,2},{7,3},{8,12},{9,13},{10,... | collective-permute-start | bytes 98312 | tf_op jit(solution)/shard_map/ppermute | solution.py:80
  46.5 2.8 %collective-permute-start.8 = (bf16[2,8192]{1,0:T(2,128)(2,1)S(1)}, bf16[2,8192]{1,0:T(2,128)(2,1)S(1)}, u32[]{:S(2)}, u32[]{:S(2)}) collective-permute-start(bf16[2,8192]{1,0:T(2,128)(2,1)S(1)} %bitcast.81), channel_id=1, source_target_pairs={{0,12},{1,13},{2,14},{3,15},{4,8},{5,9},{6,10},{7,11},{8,4},{9,5},... | collective-permute-start | bytes 98312 | tf_op jit(solution)/shard_map/ppermute | solution.py:80
  49.4 4.0 %bring.3.output_vmem = bf16[512,8192]{1,0:T(8,128)(2,1)S(1)} custom-call(s32[2]{0:T(128)S(1)} %pad_add_fusion.refs_0_.where_ref, bf16[512,8192]{1,0:T(8,128)(2,1)} %refs_1_.3), custom_call_target="tpu_custom_call" | custom-call | bytes 16777216 | tf_op jit(solution)/shard_map/bring/pallas_call | solution.py:327
  53.4 0.7 collective-permute-done.9
  54.5 6.5 %all_gather.7.rows_ref = bf16[32,8192]{1,0:T(8,128)(2,1)S(1)} all-gather(bf16[8,8192]{1,0:T(8,128)(2,1)S(1)} %pad_maximum_fusion.2), channel_id=1, replica_groups={{0,1,2,3},{4,5,6,7},{8,9,10,11},{12,13,14,15},{16,17,18,19},{20,21,22,2..., dimensions={0}, use_global_device_ids=true | all-gather | bytes 655360 | tf_op jit(solution)/shard_map/all_gather | solution.py:122
  61.0 3.0 %output_halves.1 = (f32[8,2,8192]{2,1,0:T(2,128)S(1)}, f32[8,2,8192]{2,1,0:T(2,128)S(1)}) custom-call(s32[2]{0:T(128)S(1)} %pad_add_fusion.refs_0_.where_ref, bf16[32,8192]{1,0:T(8,128)(2,1)S(1)} %all_gather.7.rows_ref, bf16[32,128]{1,0:T(8,128)(2,1)S(1)} %slice.87.marks_ref, bf16[512,8192]{1,0:T(8,128)(2,1)S(1)} %bring.3.output_vmem, ...), custom_call_target="tpu_custom_call" | custom-call | tf_op jit(solution)/shard_map/output_halves/pallas_call | solution.py:293
  64.0 0.4 collective-permute-start.11
  64.4 1.6 %collective-permute-done.11 = f32[8,2,8192]{2,1,0:T(2,128)S(1)} collective-permute-done((f32[8,2,8192]{2,1,0:T(2,128)S(1)}, f32[8,2,8192]{2,1,0:T(2,128)S(1)}, u32[]{:S(2)}, u32[]{:S(2)}) %collective-permute-start.11) | collective-permute-done | bytes 524320 | tf_op jit(solution)/shard_map/ppermute | solution.py:141
  65.9 0.3 add_convert_fusion
  66.2 13.3 %all_to_all.5 = bf16[8,2,8192]{2,1,0:T(2,128)(2,1)S(1)} all-to-all(bf16[8,2,8192]{2,1,0:T(2,128)(2,1)S(1)} %add_convert_fusion), channel_id=1, replica_groups={{0,2,4,6,8,10,12,14},{1,3,5,7,9,11,13,15},{16,18,20,22,24,26,28,30},{17..., dimensions={0} | all-to-all | bytes 524288 | tf_op jit(solution)/shard_map/all_to_all | solution.py:147
  79.6 0.9 %reduce_sum.22 = bf16[2,8192]{1,0:T(2,128)(2,1)} reduce(bf16[8,2,8192]{2,1,0:T(2,128)(2,1)S(1)} %all_to_all.5, bf16[]{:T(256)} %constant.22.clone.1), dimensions={0}, to_apply=%region_2.3 | reduce | flops 114688 | bytes 294914 | tf_op jit(solution)/shard_map/reduce_sum | solution.py:564
  (49 shorter events, 1.6 us)
Async XLA Ops:
  0.0 43.6 %copy-start = (bf16[2,512,1024]{2,1,0:T(8,128)(2,1)S(1)}, bf16[2,512,1024]{2,1,0:T(8,128)(2,1)}, u32[]{:S(2)}) copy-start(bf16[2,512,1024]{2,1,0:T(8,128)(2,1)} %param.23) | copy-start | bytes 6291460
  1.8 10.0 %collective-permute-start = (bf16[2,8320]{1,0:T(2,128)(2,1)}, bf16[2,8320]{1,0:T(2,128)(2,1)S(1)}, u32[]{:S(2)}, u32[]{:S(2)}) collective-permute-start(bf16[2,8320]{1,0:T(2,128)(2,1)} %norm_and_marks.1), channel_id=1, source_target_pairs={{0,12},{1,13},{2,14},{3,15},{4,8},{5,9},{6,10},{7,11},{8,4},{9,5},... | collective-permute-start | bytes 99848 | tf_op jit(solution)/shard_map/ppermute | solution.py:80
  6.9 5.0 %collective-permute-start.1 = (bf16[2,8320]{1,0:T(2,128)(2,1)}, bf16[2,8320]{1,0:T(2,128)(2,1)S(1)}, u32[]{:S(2)}, u32[]{:S(2)}) collective-permute-start(bf16[2,8320]{1,0:T(2,128)(2,1)} %norm_and_marks.1), channel_id=1, source_target_pairs={{0,8},{1,9},{2,10},{3,11},{4,12},{5,13},{6,14},{7,15},{8,0},{9,1},... | collective-permute-start | bytes 99848 | tf_op jit(solution)/shard_map/ppermute | solution.py:80
  6.9 5.0 %collective-permute-start.2 = (bf16[2,8320]{1,0:T(2,128)(2,1)}, bf16[2,8320]{1,0:T(2,128)(2,1)S(1)}, u32[]{:S(2)}, u32[]{:S(2)}) collective-permute-start(bf16[2,8320]{1,0:T(2,128)(2,1)} %norm_and_marks.1), channel_id=1, source_target_pairs={{0,4},{1,5},{2,6},{3,7},{4,0},{5,1},{6,2},{7,3},{8,12},{9,13},{10,... | collective-permute-start | bytes 99848 | tf_op jit(solution)/shard_map/ppermute | solution.py:80
  7.6 4.3 %copy-start.6 = (bf16[2,8320]{1,0:T(2,128)(2,1)S(1)}, bf16[2,8320]{1,0:T(2,128)(2,1)}, u32[]{:S(2)}) copy-start(bf16[2,8320]{1,0:T(2,128)(2,1)} %norm_and_marks.1) | copy-start | bytes 99844
  7.6 12.1 %copy-start.2 = (bf16[4,8192,16]{1,2,0:T(8,128)(2,1)S(1)}, bf16[4,8192,16]{1,2,0:T(8,128)(2,1)}, u32[]{:S(2)}) copy-start(bf16[4,8192,16]{1,2,0:T(8,128)(2,1)} %param.19) | copy-start | bytes 3145732
  7.6 12.1 %copy-start.3 = (bf16[4,16,8192]{2,1,0:T(8,128)(2,1)S(1)}, bf16[4,16,8192]{2,1,0:T(8,128)(2,1)}, u32[]{:S(2)}) copy-start(bf16[4,16,8192]{2,1,0:T(8,128)(2,1)} %param.20) | copy-start | bytes 3145732
  11.8 8.0 %copy-start.1 = (bf16[8192,128]{1,0:T(8,128)(2,1)S(1)}, bf16[8192,128]{1,0:T(8,128)(2,1)}, u32[]{:S(2)}) copy-start(bf16[8192,128]{1,0:T(8,128)(2,1)} %keyval_vmem.1) | copy-start | bytes 6291460
  22.9 15.2 %copy-start.7 = (s32[2]{0:T(128)S(1)}, s32[2]{0:T(128)}, u32[]{:S(2)}) copy-start(s32[2]{0:T(128)} %param.25) | copy-start | bytes 28
  22.9 2.0 %collective-permute-start.3 = (f32[8,2,8448]{2,1,0:T(2,128)S(1)}, f32[8,2,8448]{2,1,0:T(2,128)S(1)}, u32[]{:S(2)}, u32[]{:S(2)}) collective-permute-start(f32[8,2,8448]{2,1,0:T(2,128)S(1)} %get-tuple-element.19), channel_id=1, source_target_pairs={{0,1},{1,0},{2,3},{3,2},{4,5},{5,4},{6,7},{7,6},{8,9},{9,8},{10,11... | collective-permute-start | bytes 1622024 | tf_op jit(solution)/shard_map/ppermute | solution.py:141
  25.2 8.8 %collective-permute-start.4 = (f32[4,2,8448]{2,1,0:T(2,128)S(1)}, f32[4,2,8448]{2,1,0:T(2,128)S(1)}, u32[]{:S(2)}, u32[]{:S(2)}) collective-permute-start(f32[4,2,8448]{2,1,0:T(2,128)S(1)} %slice.89), channel_id=1, source_target_pairs={{0,2},{1,3},{2,0},{3,1},{4,6},{5,7},{6,4},{7,5},{8,10},{9,11},{10,... | collective-permute-start | bytes 811016 | tf_op jit(solution)/shard_map/ppermute | solution.py:400
  34.4 7.4 %collective-permute-start.6 = (f32[2,8704]{1,0:T(2,128)S(1)}, f32[2,8704]{1,0:T(2,128)S(1)}, u32[]{:S(2)}, u32[]{:S(2)}) collective-permute-start(f32[2,8704]{1,0:T(2,128)S(1)} %get-tuple-element.29), channel_id=1, source_target_pairs={{0,8},{1,9},{2,10},{3,11},{4,12},{5,13},{6,14},{7,15},{8,0},{9,1},... | collective-permute-start | bytes 208904 | tf_op jit(solution)/shard_map/ppermute | solution.py:400
  36.6 6.3 %collective-permute-start.7 = (f32[2,8704]{1,0:T(2,128)S(1)}, f32[2,8704]{1,0:T(2,128)S(1)}, u32[]{:S(2)}, u32[]{:S(2)}) collective-permute-start(f32[2,8704]{1,0:T(2,128)S(1)} %get-tuple-element.28), channel_id=1, source_target_pairs={{0,12},{1,13},{2,14},{3,15},{4,8},{5,9},{6,10},{7,11},{8,4},{9,5},... | collective-permute-start | bytes 208904 | tf_op jit(solution)/shard_map/ppermute | solution.py:400
  38.2 5.2 %collective-permute-start.5 = (f32[2,8704]{1,0:T(2,128)S(1)}, f32[2,8704]{1,0:T(2,128)S(1)}, u32[]{:S(2)}, u32[]{:S(2)}) collective-permute-start(f32[2,8704]{1,0:T(2,128)S(1)} %get-tuple-element.30), channel_id=1, source_target_pairs={{0,4},{1,5},{2,6},{3,7},{4,0},{5,1},{6,2},{7,3},{8,12},{9,13},{10,... | collective-permute-start | bytes 208904 | tf_op jit(solution)/shard_map/ppermute | solution.py:400
  43.4 1.6 %copy-start.8 = (bf16[2,512,1024]{2,1,0:T(8,128)(2,1)S(1)}, bf16[2,512,1024]{2,1,0:T(8,128)(2,1)}, u32[]{:S(2)}) copy-start(bf16[2,512,1024]{2,1,0:T(8,128)(2,1)} %param.24) | copy-start | bytes 6291460
  45.5 15.4 %copy-start.4 = (bf16[4,8192,16]{1,2,0:T(8,128)(2,1)S(1)}, bf16[4,8192,16]{1,2,0:T(8,128)(2,1)}, u32[]{:S(2)}) copy-start(bf16[4,8192,16]{1,2,0:T(8,128)(2,1)} %param.21) | copy-start | bytes 3145732
  45.6 15.4 %copy-start.5 = (bf16[4,16,8192]{2,1,0:T(8,128)(2,1)S(1)}, bf16[4,16,8192]{2,1,0:T(8,128)(2,1)}, u32[]{:S(2)}) copy-start(bf16[4,16,8192]{2,1,0:T(8,128)(2,1)} %param.22) | copy-start | bytes 3145732
  45.6 7.8 %collective-permute-start.10 = (bf16[2,8192]{1,0:T(2,128)(2,1)S(1)}, bf16[2,8192]{1,0:T(2,128)(2,1)S(1)}, u32[]{:S(2)}, u32[]{:S(2)}) collective-permute-start(bf16[2,8192]{1,0:T(2,128)(2,1)S(1)} %bitcast.80), channel_id=1, source_target_pairs={{0,4},{1,5},{2,6},{3,7},{4,0},{5,1},{6,2},{7,3},{8,12},{9,13},{10,... | collective-permute-start | bytes 98312 | tf_op jit(solution)/shard_map/ppermute | solution.py:80
  46.5 6.9 %collective-permute-start.8 = (bf16[2,8192]{1,0:T(2,128)(2,1)S(1)}, bf16[2,8192]{1,0:T(2,128)(2,1)S(1)}, u32[]{:S(2)}, u32[]{:S(2)}) collective-permute-start(bf16[2,8192]{1,0:T(2,128)(2,1)S(1)} %bitcast.81), channel_id=1, source_target_pairs={{0,12},{1,13},{2,14},{3,15},{4,8},{5,9},{6,10},{7,11},{8,4},{9,5},... | collective-permute-start | bytes 98312 | tf_op jit(solution)/shard_map/ppermute | solution.py:80
  49.4 4.8 %collective-permute-start.9 = (bf16[2,8192]{1,0:T(2,128)(2,1)S(1)}, bf16[2,8192]{1,0:T(2,128)(2,1)S(1)}, u32[]{:S(2)}, u32[]{:S(2)}) collective-permute-start(bf16[2,8192]{1,0:T(2,128)(2,1)S(1)} %bitcast.82), channel_id=1, source_target_pairs={{0,8},{1,9},{2,10},{3,11},{4,12},{5,13},{6,14},{7,15},{8,0},{9,1},... | collective-permute-start | bytes 98312 | tf_op jit(solution)/shard_map/ppermute | solution.py:80
  64.0 2.0 %collective-permute-start.11 = (f32[8,2,8192]{2,1,0:T(2,128)S(1)}, f32[8,2,8192]{2,1,0:T(2,128)S(1)}, u32[]{:S(2)}, u32[]{:S(2)}) collective-permute-start(f32[8,2,8192]{2,1,0:T(2,128)S(1)} %get-tuple-element.24), channel_id=1, source_target_pairs={{0,1},{1,0},{2,3},{3,2},{4,5},{5,4},{6,7},{7,6},{8,9},{9,8},{10,11... | collective-permute-start | bytes 1572872 | tf_op jit(solution)/shard_map/ppermute | solution.py:141

commit v10 on v9

--- a/solution.py
+++ b/solution.py
@@ -205,17 +205,20 @@
             given_ref[k, :, spot] = given_piece
 
 
+def relative_place(me, chips):
+    def place(z, y):
+        return jnp.bitwise_xor((me // 2) % 2, y) * (chips // 2) + jnp.bitwise_xor(me // 4, z)
+
+    return place
+
+
 def query_kernel(
     where_ref, rows_ref, marks_ref, query_vmem, keyval_vmem, down_vmem, up_vmem,
     kept_ref, given_ref,
 ):
     me = where_ref[0]
     odd = (me % 2) == 1
-    far = kept_ref.shape[0] // 2
-
-    def place(z, y):
-        return jnp.bitwise_xor((me // 2) % 2, y) * far + jnp.bitwise_xor(me // 4, z)
-
+    place = relative_place(me, kept_ref.shape[0])
     width = down_vmem.shape[1]
     step = width // CHUNKS
     lifted = own_lift(rows_ref, down_vmem, marks_ref, where_ref[1])
@@ -272,6 +275,7 @@
 ):
     me = where_ref[0]
     odd = (me % 2) == 1
+    place = relative_place(me, kept_ref.shape[0])
     depth, width = output_vmem.shape
     step = width // CHUNKS
     lifted = own_lift(rows_ref, down_vmem, marks_ref, where_ref[1])
@@ -282,7 +286,7 @@
         part = part + adapter_scale * jnp.dot(
             lifted, up_vmem[:, spot], preferred_element_type=jnp.float32
         )
-        split_store(part, odd, lambda z, y: 2 * z + y, kept_ref, given_ref, k * step, False)
+        split_store(part, odd, place, kept_ref, given_ref, k * step, False)
 
 
 def output_halves(where, every_row, gathered, output_weight, down, up, count, local_rows):
@@ -424,6 +428,13 @@
     return query, in_order(high, near, far, -1)
 
 
+def scatter_output(pair_sums):
+    chips, local, width = pair_sums.shape
+    blocks = pair_sums.reshape(2, chips // 2, local, width)
+    line = blocks[0] + permuted(blocks[1], 2)
+    return line[0] + sum(permuted(line[k], 4 * k) for k in (1, 2, 3))
+
+
 def body(
     hidden,
     gain,
@@ -559,8 +570,9 @@
             columns, output_weight, preferred_element_type=jnp.float32
         ) + adapter_scale * jnp.dot(lifted_rows, up_rows, preferred_element_type=jnp.float32)
         kept, given = core_halves(partial)
-    pair_sums = (kept + swap_cores(given)).astype(jnp.bfloat16)
-    arrived = exchange_chips(pair_sums).astype(jnp.float32)
+    if aligned:
+        return scatter_output(kept + swap_cores(given)).astype(jnp.bfloat16)
+    arrived = exchange_chips(kept + swap_cores(given))
     return jnp.sum(arrived, axis=0).astype(jnp.bfloat16)
 
 

time: 80.6 us -> 84.7 us (1.051)
  blocking collectives: 27.3 us -> 13.9 us
  waiting for transfers between devices: 16.6 us -> 28.3 us
  starting transfers between devices: 15.5 us -> 21.2 us
    all_to_all x1 -> x0, blocking collectives: 13.3 us -> none  [exchange_chips(): lax.all_to_all(blocks, 'pool', 0, 0, tiled=True, axis_index_groups=same_c...]
    ppermute x4 -> x8, waiting for transfers between devices: 12.6 us -> 24.3 us  [permuted(): return lax.ppermute(block, 'pool', [(i, i ^ offset) for i in range(count)])]
    ppermute x4 -> x8, starting transfers between devices: 5.11 us -> 10.8 us  [permuted(): return lax.ppermute(block, 'pool', [(i, i ^ offset) for i in range(count)])]
    reduce_sum x1 -> x0, other arithmetic: 0.85 us -> none  [body(): return jnp.sum(arrived, axis=0).astype(jnp.bfloat16)]
  transfers between devices with their start and end apart: 12 -> 16, of which waited for: 8 -> 11; matrix products, arithmetic and copies ran while one was open for 0% -> 0% of each run, Pallas kernels for 10% -> 10%
where the time goes in v10:
time: 84.7 us; the launch traced here: 84.5 us
  waiting for transfers between devices  28.3 us (33%)
  starting transfers between devices  21.2 us (25%)
  Pallas kernels  16.1 us (19%)
  blocking collectives  13.9 us (16%)
  other arithmetic  2.71 us (3%)
  matrix products  1.37 us (2%)
    ppermute x8, waiting for transfers between devices, permuted(): return lax.ppermute(block, 'pool', [(i, i ^ offset) for i in range(count)])  24.3 us
    all_gather x2, blocking collectives, gather_rows(): lax.all_gather(rows, 'pool', axis=0, axis_index_groups=fours, tiled=True)  13.9 us
    ppermute x8, starting transfers between devices, permuted(): return lax.ppermute(block, 'pool', [(i, i ^ offset) for i in range(count)])  10.8 us
    ppermute x6, starting transfers between devices, exchange_quads(): lax.ppermute(rows, 'pool', [(i, i ^ k * step) for i in range(count)])  9.54 us
    pallas_call x2, Pallas kernels, bring(): pl.pallas_call(bring_kernel, in_specs=[pl.BlockSpec(memory_space=pltpu.SM...  8.17 us
    ppermute x2, waiting for transfers between devices, swap_cores(): return lax.ppermute(block, 'pool', [(i, i ^ 1) for i in range(count)])  3.15 us
    pallas_call x1, Pallas kernels, query_halves(): pl.pallas_call(query_kernel, in_specs=[pl.BlockSpec(memory_space=pltpu.SM...  3.14 us
    pallas_call x1, Pallas kernels, output_halves(): pl.pallas_call(output_kernel, in_specs=[pl.BlockSpec(memory_space=pltpu.S...  2.96 us
  transfers between devices with their start and end apart: 16, of which 11 were waited for; matrix products, arithmetic and copies ran while one was open for 0% of the time, Pallas kernels for 10%

profile of v10, /device:TPU:0, one launch (start us, length us, event | category | flops | bytes accessed | tf_op | source)
XLA Modules:
  0.0 84.5 jit_solution(1043167166393299515)
XLA Ops:
  0.0 1.8 %norm_and_marks.1 = bf16[2,8320]{1,0:T(2,128)(2,1)} custom-call(bf16[2,8192]{1,0:T(2,128)(2,1)} %hidden_hbm.1, f32[1,8192]{1,0:T(1,128)} %bitcast.89, s32[2]{0:T(128)} %adapter_hbm.1, s32[64]{0:T(128)} %slot_hbm.1), custom_call_target="tpu_custom_call" | custom-call | tf_op jit(solution)/shard_map/norm_and_marks/pallas_call | solution.py:381
  1.8 5.1 %collective-permute-start = (bf16[2,8320]{1,0:T(2,128)(2,1)}, bf16[2,8320]{1,0:T(2,128)(2,1)S(1)}, u32[]{:S(2)}, u32[]{:S(2)}) collective-permute-start(bf16[2,8320]{1,0:T(2,128)(2,1)} %norm_and_marks.1), channel_id=1, source_target_pairs={{0,12},{1,13},{2,14},{3,15},{4,8},{5,9},{6,10},{7,11},{8,4},{9,5},... | collective-permute-start | bytes 99848 | tf_op jit(solution)/shard_map/ppermute | solution.py:80
  6.9 0.6 collective-permute-start.2
  7.6 4.1 %bring.2.query_vmem = bf16[8192,512]{1,0:T(8,128)(2,1)S(1)} custom-call(s32[2]{0:T(128)S(1)} %pad_add_fusion.refs_0_.where_ref, bf16[8192,512]{1,0:T(8,128)(2,1)} %refs_1_.2), custom_call_target="tpu_custom_call" | custom-call | bytes 16777216 | tf_op jit(solution)/shard_map/bring/pallas_call | solution.py:331
  12.3 7.4 %all_gather.6 = bf16[32,8320]{1,0:T(8,128)(2,1)S(1)} all-gather(bf16[8,8320]{1,0:T(8,128)(2,1)S(1)} %pad_maximum_fusion.1), channel_id=1, replica_groups={{0,1,2,3},{4,5,6,7},{8,9,10,11},{12,13,14,15},{16,17,18,19},{20,21,22,2..., dimensions={0}, use_global_device_ids=true | all-gather | bytes 665600 | tf_op jit(solution)/shard_map/all_gather | solution.py:122
  19.7 3.1 %query_halves.1 = (f32[8,2,8448]{2,1,0:T(2,128)S(1)}, f32[8,2,8448]{2,1,0:T(2,128)S(1)}) custom-call(s32[2]{0:T(128)S(1)} %pad_add_fusion.refs_0_.where_ref, bf16[32,8192]{1,0:T(8,128)(2,1)S(1)} %slice.112.rows_ref, bf16[32,128]{1,0:T(8,128)(2,1)S(1)} %slice.113.marks_ref, bf16[8192,512]{1,0:T(8,128)(2,1)S(1)} %bring.2.query_vmem, ...), custom_call_target="tpu_custom_call" | custom-call | tf_op jit(solution)/shard_map/query_halves/pallas_call | solution.py:258
  23.3 1.6 %collective-permute-done.3 = f32[8,2,8448]{2,1,0:T(2,128)S(1)} collective-permute-done((f32[8,2,8448]{2,1,0:T(2,128)S(1)}, f32[8,2,8448]{2,1,0:T(2,128)S(1)}, u32[]{:S(2)}, u32[]{:S(2)}) %collective-permute-start.3) | collective-permute-done | bytes 540704 | tf_op jit(solution)/shard_map/ppermute | solution.py:141
  25.2 0.9 %collective-permute-start.4 = (f32[4,2,8448]{2,1,0:T(2,128)S(1)}, f32[4,2,8448]{2,1,0:T(2,128)S(1)}, u32[]{:S(2)}, u32[]{:S(2)}) collective-permute-start(f32[4,2,8448]{2,1,0:T(2,128)S(1)} %slice.115), channel_id=1, source_target_pairs={{0,2},{1,3},{2,0},{3,1},{4,6},{5,7},{6,4},{7,5},{8,10},{9,11},{10,... | collective-permute-start | bytes 811016 | tf_op jit(solution)/shard_map/ppermute | solution.py:404
  26.1 7.9 %collective-permute-done.4 = f32[4,2,8448]{2,1,0:T(2,128)S(1)} collective-permute-done((f32[4,2,8448]{2,1,0:T(2,128)S(1)}, f32[4,2,8448]{2,1,0:T(2,128)S(1)}, u32[]{:S(2)}, u32[]{:S(2)}) %collective-permute-start.4) | collective-permute-done | bytes 270368 | tf_op jit(solution)/shard_map/ppermute | solution.py:404
  34.3 2.2 %collective-permute-start.6 = (f32[2,8704]{1,0:T(2,128)S(1)}, f32[2,8704]{1,0:T(2,128)S(1)}, u32[]{:S(2)}, u32[]{:S(2)}) collective-permute-start(f32[2,8704]{1,0:T(2,128)S(1)} %get-tuple-element.29), channel_id=1, source_target_pairs={{0,8},{1,9},{2,10},{3,11},{4,12},{5,13},{6,14},{7,15},{8,0},{9,1},... | collective-permute-start | bytes 208904 | tf_op jit(solution)/shard_map/ppermute | solution.py:404
  36.6 1.5 %collective-permute-start.7 = (f32[2,8704]{1,0:T(2,128)S(1)}, f32[2,8704]{1,0:T(2,128)S(1)}, u32[]{:S(2)}, u32[]{:S(2)}) collective-permute-start(f32[2,8704]{1,0:T(2,128)S(1)} %get-tuple-element.28), channel_id=1, source_target_pairs={{0,12},{1,13},{2,14},{3,15},{4,8},{5,9},{6,10},{7,11},{8,4},{9,5},... | collective-permute-start | bytes 208904 | tf_op jit(solution)/shard_map/ppermute | solution.py:404
  38.2 0.5 collective-permute-start.5
  38.7 3.1 %collective-permute-done.6 = f32[2,8704]{1,0:T(2,128)S(1)} collective-permute-done((f32[2,8704]{1,0:T(2,128)S(1)}, f32[2,8704]{1,0:T(2,128)S(1)}, u32[]{:S(2)}, u32[]{:S(2)}) %collective-permute-start.6) | collective-permute-done | bytes 69664 | tf_op jit(solution)/shard_map/ppermute | solution.py:404
  41.7 1.1 %collective-permute-done.7 = f32[2,8704]{1,0:T(2,128)S(1)} collective-permute-done((f32[2,8704]{1,0:T(2,128)S(1)}, f32[2,8704]{1,0:T(2,128)S(1)}, u32[]{:S(2)}, u32[]{:S(2)}) %collective-permute-start.7) | collective-permute-done | bytes 69664 | tf_op jit(solution)/shard_map/ppermute | solution.py:404
  42.9 0.5 collective-permute-done.5
  43.6 0.7 fusion.39
  45.0 0.5 fusion.18
  45.6 1.0 %collective-permute-start.10 = (bf16[2,8192]{1,0:T(2,128)(2,1)S(1)}, bf16[2,8192]{1,0:T(2,128)(2,1)S(1)}, u32[]{:S(2)}, u32[]{:S(2)}) collective-permute-start(bf16[2,8192]{1,0:T(2,128)(2,1)S(1)} %bitcast.92), channel_id=1, source_target_pairs={{0,4},{1,5},{2,6},{3,7},{4,0},{5,1},{6,2},{7,3},{8,12},{9,13},{10,... | collective-permute-start | bytes 98312 | tf_op jit(solution)/shard_map/ppermute | solution.py:80
  46.5 2.8 %collective-permute-start.8 = (bf16[2,8192]{1,0:T(2,128)(2,1)S(1)}, bf16[2,8192]{1,0:T(2,128)(2,1)S(1)}, u32[]{:S(2)}, u32[]{:S(2)}) collective-permute-start(bf16[2,8192]{1,0:T(2,128)(2,1)S(1)} %bitcast.93), channel_id=1, source_target_pairs={{0,12},{1,13},{2,14},{3,15},{4,8},{5,9},{6,10},{7,11},{8,4},{9,5},... | collective-permute-start | bytes 98312 | tf_op jit(solution)/shard_map/ppermute | solution.py:80
  49.3 4.0 %bring.3.output_vmem = bf16[512,8192]{1,0:T(8,128)(2,1)S(1)} custom-call(s32[2]{0:T(128)S(1)} %pad_add_fusion.refs_0_.where_ref, bf16[512,8192]{1,0:T(8,128)(2,1)} %refs_1_.3), custom_call_target="tpu_custom_call" | custom-call | bytes 16777216 | tf_op jit(solution)/shard_map/bring/pallas_call | solution.py:331
  53.4 0.7 collective-permute-done.9
  54.5 6.5 %all_gather.7.rows_ref = bf16[32,8192]{1,0:T(8,128)(2,1)S(1)} all-gather(bf16[8,8192]{1,0:T(8,128)(2,1)S(1)} %pad_maximum_fusion.2), channel_id=1, replica_groups={{0,1,2,3},{4,5,6,7},{8,9,10,11},{12,13,14,15},{16,17,18,19},{20,21,22,2..., dimensions={0}, use_global_device_ids=true | all-gather | bytes 655360 | tf_op jit(solution)/shard_map/all_gather | solution.py:122
  61.0 3.0 %output_halves.1 = (f32[8,2,8192]{2,1,0:T(2,128)S(1)}, f32[8,2,8192]{2,1,0:T(2,128)S(1)}) custom-call(s32[2]{0:T(128)S(1)} %pad_add_fusion.refs_0_.where_ref, bf16[32,8192]{1,0:T(8,128)(2,1)S(1)} %all_gather.7.rows_ref, bf16[32,128]{1,0:T(8,128)(2,1)S(1)} %slice.113.marks_ref, bf16[512,8192]{1,0:T(8,128)(2,1)S(1)} %bring.3.output_vmem, ...), custom_call_target="tpu_custom_call" | custom-call | tf_op jit(solution)/shard_map/output_halves/pallas_call | solution.py:297
  64.4 1.6 %collective-permute-done.11 = f32[8,2,8192]{2,1,0:T(2,128)S(1)} collective-permute-done((f32[8,2,8192]{2,1,0:T(2,128)S(1)}, f32[8,2,8192]{2,1,0:T(2,128)S(1)}, u32[]{:S(2)}, u32[]{:S(2)}) %collective-permute-start.11) | collective-permute-done | bytes 524320 | tf_op jit(solution)/shard_map/ppermute | solution.py:141
  66.2 1.3 %collective-permute-start.12 = (f32[4,2,8192]{2,1,0:T(2,128)S(1)}, f32[4,2,8192]{2,1,0:T(2,128)S(1)}, u32[]{:S(2)}, u32[]{:S(2)}) collective-permute-start(f32[4,2,8192]{2,1,0:T(2,128)S(1)} %slice.132), channel_id=1, source_target_pairs={{0,2},{1,3},{2,0},{3,1},{4,6},{5,7},{6,4},{7,5},{8,10},{9,11},{10,... | collective-permute-start | bytes 786440 | tf_op jit(solution)/shard_map/ppermute | solution.py:404
  67.5 7.4 %collective-permute-done.12 = f32[4,2,8192]{2,1,0:T(2,128)S(1)} collective-permute-done((f32[4,2,8192]{2,1,0:T(2,128)S(1)}, f32[4,2,8192]{2,1,0:T(2,128)S(1)}, u32[]{:S(2)}, u32[]{:S(2)}) %collective-permute-start.12) | collective-permute-done | bytes 262176 | tf_op jit(solution)/shard_map/ppermute | solution.py:404
  75.0 0.9 %collective-permute-start.13 = (f32[2,8192]{1,0:T(2,128)S(1)}, f32[2,8192]{1,0:T(2,128)S(1)}, u32[]{:S(2)}, u32[]{:S(2)}) collective-permute-start(f32[2,8192]{1,0:T(2,128)S(1)} %get-tuple-element.33), channel_id=1, source_target_pairs={{0,4},{1,5},{2,6},{3,7},{4,0},{5,1},{6,2},{7,3},{8,12},{9,13},{10,... | collective-permute-start | bytes 196616 | tf_op jit(solution)/shard_map/ppermute | solution.py:404
  75.9 1.4 %collective-permute-start.14 = (f32[2,8192]{1,0:T(2,128)S(1)}, f32[2,8192]{1,0:T(2,128)S(1)}, u32[]{:S(2)}, u32[]{:S(2)}) collective-permute-start(f32[2,8192]{1,0:T(2,128)S(1)} %get-tuple-element.31), channel_id=1, source_target_pairs={{0,8},{1,9},{2,10},{3,11},{4,12},{5,13},{6,14},{7,15},{8,0},{9,1},... | collective-permute-start | bytes 196616 | tf_op jit(solution)/shard_map/ppermute | solution.py:404
  77.4 2.1 %collective-permute-start.15 = (f32[2,8192]{1,0:T(2,128)S(1)}, f32[2,8192]{1,0:T(2,128)S(1)}, u32[]{:S(2)}, u32[]{:S(2)}) collective-permute-start(f32[2,8192]{1,0:T(2,128)S(1)} %get-tuple-element.32), channel_id=1, source_target_pairs={{0,12},{1,13},{2,14},{3,15},{4,8},{5,9},{6,10},{7,11},{8,4},{9,5},... | collective-permute-start | bytes 196616 | tf_op jit(solution)/shard_map/ppermute | solution.py:404
  79.5 0.6 collective-permute-done.13
  80.1 3.8 %collective-permute-done.14 = f32[2,8192]{1,0:T(2,128)S(1)} collective-permute-done((f32[2,8192]{1,0:T(2,128)S(1)}, f32[2,8192]{1,0:T(2,128)S(1)}, u32[]{:S(2)}, u32[]{:S(2)}) %collective-permute-start.14) | collective-permute-done | bytes 65568 | tf_op jit(solution)/shard_map/ppermute | solution.py:404
  83.8 0.7 fusion.27
  (59 shorter events, 3.8 us)
Async XLA Ops:
  0.0 43.6 %copy-start = (bf16[2,512,1024]{2,1,0:T(8,128)(2,1)S(1)}, bf16[2,512,1024]{2,1,0:T(8,128)(2,1)}, u32[]{:S(2)}) copy-start(bf16[2,512,1024]{2,1,0:T(8,128)(2,1)} %param.23) | copy-start | bytes 6291460
  1.8 10.0 %collective-permute-start = (bf16[2,8320]{1,0:T(2,128)(2,1)}, bf16[2,8320]{1,0:T(2,128)(2,1)S(1)}, u32[]{:S(2)}, u32[]{:S(2)}) collective-permute-start(bf16[2,8320]{1,0:T(2,128)(2,1)} %norm_and_marks.1), channel_id=1, source_target_pairs={{0,12},{1,13},{2,14},{3,15},{4,8},{5,9},{6,10},{7,11},{8,4},{9,5},... | collective-permute-start | bytes 99848 | tf_op jit(solution)/shard_map/ppermute | solution.py:80
  6.9 5.0 %collective-permute-start.1 = (bf16[2,8320]{1,0:T(2,128)(2,1)}, bf16[2,8320]{1,0:T(2,128)(2,1)S(1)}, u32[]{:S(2)}, u32[]{:S(2)}) collective-permute-start(bf16[2,8320]{1,0:T(2,128)(2,1)} %norm_and_marks.1), channel_id=1, source_target_pairs={{0,8},{1,9},{2,10},{3,11},{4,12},{5,13},{6,14},{7,15},{8,0},{9,1},... | collective-permute-start | bytes 99848 | tf_op jit(solution)/shard_map/ppermute | solution.py:80
  6.9 5.0 %collective-permute-start.2 = (bf16[2,8320]{1,0:T(2,128)(2,1)}, bf16[2,8320]{1,0:T(2,128)(2,1)S(1)}, u32[]{:S(2)}, u32[]{:S(2)}) collective-permute-start(bf16[2,8320]{1,0:T(2,128)(2,1)} %norm_and_marks.1), channel_id=1, source_target_pairs={{0,4},{1,5},{2,6},{3,7},{4,0},{5,1},{6,2},{7,3},{8,12},{9,13},{10,... | collective-permute-start | bytes 99848 | tf_op jit(solution)/shard_map/ppermute | solution.py:80
  7.6 4.3 %copy-start.6 = (bf16[2,8320]{1,0:T(2,128)(2,1)S(1)}, bf16[2,8320]{1,0:T(2,128)(2,1)}, u32[]{:S(2)}) copy-start(bf16[2,8320]{1,0:T(2,128)(2,1)} %norm_and_marks.1) | copy-start | bytes 99844
  7.6 12.1 %copy-start.2 = (bf16[4,8192,16]{1,2,0:T(8,128)(2,1)S(1)}, bf16[4,8192,16]{1,2,0:T(8,128)(2,1)}, u32[]{:S(2)}) copy-start(bf16[4,8192,16]{1,2,0:T(8,128)(2,1)} %param.19) | copy-start | bytes 3145732
  7.6 12.1 %copy-start.3 = (bf16[4,16,8192]{2,1,0:T(8,128)(2,1)S(1)}, bf16[4,16,8192]{2,1,0:T(8,128)(2,1)}, u32[]{:S(2)}) copy-start(bf16[4,16,8192]{2,1,0:T(8,128)(2,1)} %param.20) | copy-start | bytes 3145732
  11.8 8.0 %copy-start.1 = (bf16[8192,128]{1,0:T(8,128)(2,1)S(1)}, bf16[8192,128]{1,0:T(8,128)(2,1)}, u32[]{:S(2)}) copy-start(bf16[8192,128]{1,0:T(8,128)(2,1)} %keyval_vmem.1) | copy-start | bytes 6291460
  22.9 15.2 %copy-start.7 = (s32[2]{0:T(128)S(1)}, s32[2]{0:T(128)}, u32[]{:S(2)}) copy-start(s32[2]{0:T(128)} %param.25) | copy-start | bytes 28
  22.9 2.0 %collective-permute-start.3 = (f32[8,2,8448]{2,1,0:T(2,128)S(1)}, f32[8,2,8448]{2,1,0:T(2,128)S(1)}, u32[]{:S(2)}, u32[]{:S(2)}) collective-permute-start(f32[8,2,8448]{2,1,0:T(2,128)S(1)} %get-tuple-element.19), channel_id=1, source_target_pairs={{0,1},{1,0},{2,3},{3,2},{4,5},{5,4},{6,7},{7,6},{8,9},{9,8},{10,11... | collective-permute-start | bytes 1622024 | tf_op jit(solution)/shard_map/ppermute | solution.py:141
  25.2 8.8 %collective-permute-start.4 = (f32[4,2,8448]{2,1,0:T(2,128)S(1)}, f32[4,2,8448]{2,1,0:T(2,128)S(1)}, u32[]{:S(2)}, u32[]{:S(2)}) collective-permute-start(f32[4,2,8448]{2,1,0:T(2,128)S(1)} %slice.115), channel_id=1, source_target_pairs={{0,2},{1,3},{2,0},{3,1},{4,6},{5,7},{6,4},{7,5},{8,10},{9,11},{10,... | collective-permute-start | bytes 811016 | tf_op jit(solution)/shard_map/ppermute | solution.py:404
  34.3 7.4 %collective-permute-start.6 = (f32[2,8704]{1,0:T(2,128)S(1)}, f32[2,8704]{1,0:T(2,128)S(1)}, u32[]{:S(2)}, u32[]{:S(2)}) collective-permute-start(f32[2,8704]{1,0:T(2,128)S(1)} %get-tuple-element.29), channel_id=1, source_target_pairs={{0,8},{1,9},{2,10},{3,11},{4,12},{5,13},{6,14},{7,15},{8,0},{9,1},... | collective-permute-start | bytes 208904 | tf_op jit(solution)/shard_map/ppermute | solution.py:404
  36.6 6.3 %collective-permute-start.7 = (f32[2,8704]{1,0:T(2,128)S(1)}, f32[2,8704]{1,0:T(2,128)S(1)}, u32[]{:S(2)}, u32[]{:S(2)}) collective-permute-start(f32[2,8704]{1,0:T(2,128)S(1)} %get-tuple-element.28), channel_id=1, source_target_pairs={{0,12},{1,13},{2,14},{3,15},{4,8},{5,9},{6,10},{7,11},{8,4},{9,5},... | collective-permute-start | bytes 208904 | tf_op jit(solution)/shard_map/ppermute | solution.py:404
  38.2 5.2 %collective-permute-start.5 = (f32[2,8704]{1,0:T(2,128)S(1)}, f32[2,8704]{1,0:T(2,128)S(1)}, u32[]{:S(2)}, u32[]{:S(2)}) collective-permute-start(f32[2,8704]{1,0:T(2,128)S(1)} %get-tuple-element.30), channel_id=1, source_target_pairs={{0,4},{1,5},{2,6},{3,7},{4,0},{5,1},{6,2},{7,3},{8,12},{9,13},{10,... | collective-permute-start | bytes 208904 | tf_op jit(solution)/shard_map/ppermute | solution.py:404
  43.4 1.6 %copy-start.8 = (bf16[2,512,1024]{2,1,0:T(8,128)(2,1)S(1)}, bf16[2,512,1024]{2,1,0:T(8,128)(2,1)}, u32[]{:S(2)}) copy-start(bf16[2,512,1024]{2,1,0:T(8,128)(2,1)} %param.24) | copy-start | bytes 6291460
  45.5 15.4 %copy-start.4 = (bf16[4,8192,16]{1,2,0:T(8,128)(2,1)S(1)}, bf16[4,8192,16]{1,2,0:T(8,128)(2,1)}, u32[]{:S(2)}) copy-start(bf16[4,8192,16]{1,2,0:T(8,128)(2,1)} %param.21) | copy-start | bytes 3145732
  45.5 15.4 %copy-start.5 = (bf16[4,16,8192]{2,1,0:T(8,128)(2,1)S(1)}, bf16[4,16,8192]{2,1,0:T(8,128)(2,1)}, u32[]{:S(2)}) copy-start(bf16[4,16,8192]{2,1,0:T(8,128)(2,1)} %param.22) | copy-start | bytes 3145732
  45.6 7.8 %collective-permute-start.10 = (bf16[2,8192]{1,0:T(2,128)(2,1)S(1)}, bf16[2,8192]{1,0:T(2,128)(2,1)S(1)}, u32[]{:S(2)}, u32[]{:S(2)}) collective-permute-start(bf16[2,8192]{1,0:T(2,128)(2,1)S(1)} %bitcast.92), channel_id=1, source_target_pairs={{0,4},{1,5},{2,6},{3,7},{4,0},{5,1},{6,2},{7,3},{8,12},{9,13},{10,... | collective-permute-start | bytes 98312 | tf_op jit(solution)/shard_map/ppermute | solution.py:80
  46.5 6.9 %collective-permute-start.8 = (bf16[2,8192]{1,0:T(2,128)(2,1)S(1)}, bf16[2,8192]{1,0:T(2,128)(2,1)S(1)}, u32[]{:S(2)}, u32[]{:S(2)}) collective-permute-start(bf16[2,8192]{1,0:T(2,128)(2,1)S(1)} %bitcast.93), channel_id=1, source_target_pairs={{0,12},{1,13},{2,14},{3,15},{4,8},{5,9},{6,10},{7,11},{8,4},{9,5},... | collective-permute-start | bytes 98312 | tf_op jit(solution)/shard_map/ppermute | solution.py:80
  49.3 4.8 %collective-permute-start.9 = (bf16[2,8192]{1,0:T(2,128)(2,1)S(1)}, bf16[2,8192]{1,0:T(2,128)(2,1)S(1)}, u32[]{:S(2)}, u32[]{:S(2)}) collective-permute-start(bf16[2,8192]{1,0:T(2,128)(2,1)S(1)} %bitcast.94), channel_id=1, source_target_pairs={{0,8},{1,9},{2,10},{3,11},{4,12},{5,13},{6,14},{7,15},{8,0},{9,1},... | collective-permute-start | bytes 98312 | tf_op jit(solution)/shard_map/ppermute | solution.py:80
  64.0 2.0 %collective-permute-start.11 = (f32[8,2,8192]{2,1,0:T(2,128)S(1)}, f32[8,2,8192]{2,1,0:T(2,128)S(1)}, u32[]{:S(2)}, u32[]{:S(2)}) collective-permute-start(f32[8,2,8192]{2,1,0:T(2,128)S(1)} %get-tuple-element.24), channel_id=1, source_target_pairs={{0,1},{1,0},{2,3},{3,2},{4,5},{5,4},{6,7},{7,6},{8,9},{9,8},{10,11... | collective-permute-start | bytes 1572872 | tf_op jit(solution)/shard_map/ppermute | solution.py:141
  66.2 8.6 %collective-permute-start.12 = (f32[4,2,8192]{2,1,0:T(2,128)S(1)}, f32[4,2,8192]{2,1,0:T(2,128)S(1)}, u32[]{:S(2)}, u32[]{:S(2)}) collective-permute-start(f32[4,2,8192]{2,1,0:T(2,128)S(1)} %slice.132), channel_id=1, source_target_pairs={{0,2},{1,3},{2,0},{3,1},{4,6},{5,7},{6,4},{7,5},{8,10},{9,11},{10,... | collective-permute-start | bytes 786440 | tf_op jit(solution)/shard_map/ppermute | solution.py:404
  75.0 5.0 %collective-permute-start.13 = (f32[2,8192]{1,0:T(2,128)S(1)}, f32[2,8192]{1,0:T(2,128)S(1)}, u32[]{:S(2)}, u32[]{:S(2)}) collective-permute-start(f32[2,8192]{1,0:T(2,128)S(1)} %get-tuple-element.33), channel_id=1, source_target_pairs={{0,4},{1,5},{2,6},{3,7},{4,0},{5,1},{6,2},{7,3},{8,12},{9,13},{10,... | collective-permute-start | bytes 196616 | tf_op jit(solution)/shard_map/ppermute | solution.py:404
  75.9 7.9 %collective-permute-start.14 = (f32[2,8192]{1,0:T(2,128)S(1)}, f32[2,8192]{1,0:T(2,128)S(1)}, u32[]{:S(2)}, u32[]{:S(2)}) collective-permute-start(f32[2,8192]{1,0:T(2,128)S(1)} %get-tuple-element.31), channel_id=1, source_target_pairs={{0,8},{1,9},{2,10},{3,11},{4,12},{5,13},{6,14},{7,15},{8,0},{9,1},... | collective-permute-start | bytes 196616 | tf_op jit(solution)/shard_map/ppermute | solution.py:404
  77.4 6.5 %collective-permute-start.15 = (f32[2,8192]{1,0:T(2,128)S(1)}, f32[2,8192]{1,0:T(2,128)S(1)}, u32[]{:S(2)}, u32[]{:S(2)}) collective-permute-start(f32[2,8192]{1,0:T(2,128)S(1)} %get-tuple-element.32), channel_id=1, source_target_pairs={{0,12},{1,13},{2,14},{3,15},{4,8},{5,9},{6,10},{7,11},{8,4},{9,5},... | collective-permute-start | bytes 196616 | tf_op jit(solution)/shard_map/ppermute | solution.py:404

commit v11 on v9

--- a/solution.py
+++ b/solution.py
@@ -110,7 +110,10 @@
     step = 4
     held = None if beside is None else beside(rows)
     while step < count:
-        if step * 4 <= count:
+        if beside is not None:
+            rows = jnp.concatenate([rows] + [permuted(rows, k * step) for k in (1, 2, 3)], axis=0)
+            step *= 4
+        elif step * 4 <= count:
             rows = exchange_quads(rows, step)
             step *= 4
         else:
@@ -214,7 +217,7 @@
     far = kept_ref.shape[0] // 2
 
     def place(z, y):
-        return jnp.bitwise_xor((me // 2) % 2, y) * far + jnp.bitwise_xor(me // 4, z)
+        return jnp.bitwise_xor((me // 2) % 2, y) * far + z
 
     width = down_vmem.shape[1]
     step = width // CHUNKS
@@ -272,6 +275,10 @@
 ):
     me = where_ref[0]
     odd = (me % 2) == 1
+
+    def place(z, y):
+        return 2 * jnp.bitwise_xor(me // 4, z) + y
+
     depth, width = output_vmem.shape
     step = width // CHUNKS
     lifted = own_lift(rows_ref, down_vmem, marks_ref, where_ref[1])
@@ -282,7 +289,7 @@
         part = part + adapter_scale * jnp.dot(
             lifted, up_vmem[:, spot], preferred_element_type=jnp.float32
         )
-        split_store(part, odd, lambda z, y: 2 * z + y, kept_ref, given_ref, k * step, False)
+        split_store(part, odd, place, kept_ref, given_ref, k * step, False)
 
 
 def output_halves(where, every_row, gathered, output_weight, down, up, count, local_rows):

time: 80.6 us -> 80.5 us (level)
    ppermute x6 -> x0, starting transfers between devices: 9.54 us -> none  [exchange_quads(): lax.ppermute(rows, 'pool', [(i, i ^ k * step) for i in range(count)])]
    ppermute x4 -> x10, starting transfers between devices: 5.11 us -> 14.6 us  [permuted(): return lax.ppermute(block, 'pool', [(i, i ^ offset) for i in range(count)])]
    ppermute x4 -> x10, waiting for transfers between devices: 12.6 us -> 14.3 us  [permuted(): return lax.ppermute(block, 'pool', [(i, i ^ offset) for i in range(count)])]
    ppermute x6 -> x0, waiting for transfers between devices: 0.89 us -> none  [exchange_quads(): lax.ppermute(rows, 'pool', [(i, i ^ k * step) for i in range(count)])]
  transfers between devices with their start and end apart: 12 -> 12, of which waited for: 8 -> 6; matrix products, arithmetic and copies ran while one was open for 0% -> 0% of each run, Pallas kernels for 10% -> 10%
where the time goes in v11:
time: 80.5 us; the launch traced here: 80.3 us
  blocking collectives  26.5 us (33%)
  waiting for transfers between devices  17.4 us (22%)
  Pallas kernels  16.3 us (20%)
  starting transfers between devices  15.4 us (19%)
  other arithmetic  2.48 us (3%)
  matrix products  1.37 us (2%)
    ppermute x10, starting transfers between devices, permuted(): return lax.ppermute(block, 'pool', [(i, i ^ offset) for i in range(count)])  14.6 us
    ppermute x10, waiting for transfers between devices, permuted(): return lax.ppermute(block, 'pool', [(i, i ^ offset) for i in range(count)])  14.3 us
    all_gather x2, blocking collectives, gather_rows(): lax.all_gather(rows, 'pool', axis=0, axis_index_groups=fours, tiled=True)  13.8 us
    all_to_all x1, blocking collectives, exchange_chips(): lax.all_to_all(blocks, 'pool', 0, 0, tiled=True, axis_index_groups=same_c...  12.7 us
    pallas_call x2, Pallas kernels, bring(): pl.pallas_call(bring_kernel, in_specs=[pl.BlockSpec(memory_space=pltpu.SM...  8.34 us
    pallas_call x1, Pallas kernels, query_halves(): pl.pallas_call(query_kernel, in_specs=[pl.BlockSpec(memory_space=pltpu.SM...  3.17 us
    ppermute x2, waiting for transfers between devices, swap_cores(): return lax.ppermute(block, 'pool', [(i, i ^ 1) for i in range(count)])  3.15 us
    pallas_call x1, Pallas kernels, output_halves(): pl.pallas_call(output_kernel, in_specs=[pl.BlockSpec(memory_space=pltpu.S...  2.96 us
  transfers between devices with their start and end apart: 12, of which 6 were waited for; matrix products, arithmetic and copies ran while one was open for 0% of the time, Pallas kernels for 10%

profile of v11, /device:TPU:0, one launch (start us, length us, event | category | flops | bytes accessed | tf_op | source)
XLA Modules:
  0.0 80.3 jit_solution(2771279242395901374)
XLA Ops:
  0.0 1.8 %norm_and_marks.1 = bf16[2,8320]{1,0:T(2,128)(2,1)} custom-call(bf16[2,8192]{1,0:T(2,128)(2,1)} %hidden_hbm.1, f32[1,8192]{1,0:T(1,128)} %bitcast.73, s32[2]{0:T(128)} %adapter_hbm.1, s32[64]{0:T(128)} %slot_hbm.1), custom_call_target="tpu_custom_call" | custom-call | tf_op jit(solution)/shard_map/norm_and_marks/pallas_call | solution.py:384
  1.8 3.1 %collective-permute-start = (bf16[2,8320]{1,0:T(2,128)(2,1)}, bf16[2,8320]{1,0:T(2,128)(2,1)S(1)}, u32[]{:S(2)}, u32[]{:S(2)}) collective-permute-start(bf16[2,8320]{1,0:T(2,128)(2,1)} %norm_and_marks.1), channel_id=1, source_target_pairs={{0,4},{1,5},{2,6},{3,7},{4,0},{5,1},{6,2},{7,3},{8,12},{9,13},{10,... | collective-permute-start | bytes 99848 | tf_op jit(solution)/shard_map/ppermute | solution.py:407
  4.9 2.6 %collective-permute-start.1 = (bf16[2,8320]{1,0:T(2,128)(2,1)}, bf16[2,8320]{1,0:T(2,128)(2,1)S(1)}, u32[]{:S(2)}, u32[]{:S(2)}) collective-permute-start(bf16[2,8320]{1,0:T(2,128)(2,1)} %norm_and_marks.1), channel_id=1, source_target_pairs={{0,8},{1,9},{2,10},{3,11},{4,12},{5,13},{6,14},{7,15},{8,0},{9,1},... | collective-permute-start | bytes 99848 | tf_op jit(solution)/shard_map/ppermute | solution.py:407
  7.6 4.3 %bring.2.query_vmem = bf16[8192,512]{1,0:T(8,128)(2,1)S(1)} custom-call(s32[2]{0:T(128)S(1)} %pad_add_fusion.refs_0_.where_ref, bf16[8192,512]{1,0:T(8,128)(2,1)} %refs_1_.2), custom_call_target="tpu_custom_call" | custom-call | bytes 16777216 | tf_op jit(solution)/shard_map/bring/pallas_call | solution.py:334
  11.9 1.5 %collective-permute-done.2 = bf16[2,8320]{1,0:T(2,128)(2,1)S(1)} collective-permute-done((bf16[2,8320]{1,0:T(2,128)(2,1)}, bf16[2,8320]{1,0:T(2,128)(2,1)S(1)}, u32[]{:S(2)}, u32[]{:S(2)}) %collective-permute-start.2) | collective-permute-done | bytes 33312 | tf_op jit(solution)/shard_map/ppermute | solution.py:407
  13.6 7.2 %all_gather.6 = bf16[32,8320]{1,0:T(8,128)(2,1)S(1)} all-gather(bf16[8,8320]{1,0:T(8,128)(2,1)S(1)} %pad_maximum_fusion.1), channel_id=1, replica_groups={{0,1,2,3},{4,5,6,7},{8,9,10,11},{12,13,14,15},{16,17,18,19},{20,21,22,2..., dimensions={0}, use_global_device_ids=true | all-gather | bytes 665600 | tf_op jit(solution)/shard_map/all_gather | solution.py:125
  20.9 3.2 %query_halves.1 = (f32[8,2,8448]{2,1,0:T(2,128)S(1)}, f32[8,2,8448]{2,1,0:T(2,128)S(1)}) custom-call(s32[2]{0:T(128)S(1)} %pad_add_fusion.refs_0_.where_ref, bf16[32,8192]{1,0:T(8,128)(2,1)S(1)} %slice.86.rows_ref, bf16[32,128]{1,0:T(8,128)(2,1)S(1)} %slice.87.marks_ref, bf16[8192,512]{1,0:T(8,128)(2,1)S(1)} %bring.2.query_vmem, ...), custom_call_target="tpu_custom_call" | custom-call | tf_op jit(solution)/shard_map/query_halves/pallas_call | solution.py:258
  24.1 0.4 collective-permute-start.3
  24.5 1.6 %collective-permute-done.3 = f32[8,2,8448]{2,1,0:T(2,128)S(1)} collective-permute-done((f32[8,2,8448]{2,1,0:T(2,128)S(1)}, f32[8,2,8448]{2,1,0:T(2,128)S(1)}, u32[]{:S(2)}, u32[]{:S(2)}) %collective-permute-start.3) | collective-permute-done | bytes 540704 | tf_op jit(solution)/shard_map/ppermute | solution.py:144
  26.1 0.3 add.24
  26.4 0.9 %collective-permute-start.4 = (f32[4,2,8448]{2,1,0:T(2,128)S(1)}, f32[4,2,8448]{2,1,0:T(2,128)S(1)}, u32[]{:S(2)}, u32[]{:S(2)}) collective-permute-start(f32[4,2,8448]{2,1,0:T(2,128)S(1)} %slice.89), channel_id=1, source_target_pairs={{0,2},{1,3},{2,0},{3,1},{4,6},{5,7},{6,4},{7,5},{8,10},{9,11},{10,... | collective-permute-start | bytes 811016 | tf_op jit(solution)/shard_map/ppermute | solution.py:407
  27.3 7.9 %collective-permute-done.4 = f32[4,2,8448]{2,1,0:T(2,128)S(1)} collective-permute-done((f32[4,2,8448]{2,1,0:T(2,128)S(1)}, f32[4,2,8448]{2,1,0:T(2,128)S(1)}, u32[]{:S(2)}, u32[]{:S(2)}) %collective-permute-start.4) | collective-permute-done | bytes 270368 | tf_op jit(solution)/shard_map/ppermute | solution.py:407
  35.5 0.6 collective-permute-start.6
  36.2 2.0 %collective-permute-start.7 = (f32[2,8704]{1,0:T(2,128)S(1)}, f32[2,8704]{1,0:T(2,128)S(1)}, u32[]{:S(2)}, u32[]{:S(2)}) collective-permute-start(f32[2,8704]{1,0:T(2,128)S(1)} %get-tuple-element.28), channel_id=1, source_target_pairs={{0,12},{1,13},{2,14},{3,15},{4,8},{5,9},{6,10},{7,11},{8,4},{9,5},... | collective-permute-start | bytes 208904 | tf_op jit(solution)/shard_map/ppermute | solution.py:407
  38.2 0.9 %collective-permute-start.5 = (f32[2,8704]{1,0:T(2,128)S(1)}, f32[2,8704]{1,0:T(2,128)S(1)}, u32[]{:S(2)}, u32[]{:S(2)}) collective-permute-start(f32[2,8704]{1,0:T(2,128)S(1)} %get-tuple-element.30), channel_id=1, source_target_pairs={{0,4},{1,5},{2,6},{3,7},{4,0},{5,1},{6,2},{7,3},{8,12},{9,13},{10,... | collective-permute-start | bytes 208904 | tf_op jit(solution)/shard_map/ppermute | solution.py:407
  39.2 4.3 %collective-permute-done.6 = f32[2,8704]{1,0:T(2,128)S(1)} collective-permute-done((f32[2,8704]{1,0:T(2,128)S(1)}, f32[2,8704]{1,0:T(2,128)S(1)}, u32[]{:S(2)}, u32[]{:S(2)}) %collective-permute-start.6) | collective-permute-done | bytes 69664 | tf_op jit(solution)/shard_map/ppermute | solution.py:407
  43.5 0.5 collective-permute-done.5
  44.3 0.7 fusion.37
  45.1 0.2 fusion.21
  45.3 0.4 copy-done.8
  45.7 0.5 fusion.18
  46.2 1.7 %collective-permute-start.10 = (bf16[2,8192]{1,0:T(2,128)(2,1)S(1)}, bf16[2,8192]{1,0:T(2,128)(2,1)S(1)}, u32[]{:S(2)}, u32[]{:S(2)}) collective-permute-start(bf16[2,8192]{1,0:T(2,128)(2,1)S(1)} %bitcast.69), channel_id=1, source_target_pairs={{0,12},{1,13},{2,14},{3,15},{4,8},{5,9},{6,10},{7,11},{8,4},{9,5},... | collective-permute-start | bytes 98312 | tf_op jit(solution)/shard_map/ppermute | solution.py:407
  47.9 0.4 collective-permute-start.8
  48.3 2.4 %collective-permute-start.9 = (bf16[2,8192]{1,0:T(2,128)(2,1)S(1)}, bf16[2,8192]{1,0:T(2,128)(2,1)S(1)}, u32[]{:S(2)}, u32[]{:S(2)}) collective-permute-start(bf16[2,8192]{1,0:T(2,128)(2,1)S(1)} %bitcast.71), channel_id=1, source_target_pairs={{0,8},{1,9},{2,10},{3,11},{4,12},{5,13},{6,14},{7,15},{8,0},{9,1},... | collective-permute-start | bytes 98312 | tf_op jit(solution)/shard_map/ppermute | solution.py:407
  50.7 4.0 %bring.3.output_vmem = bf16[512,8192]{1,0:T(8,128)(2,1)S(1)} custom-call(s32[2]{0:T(128)S(1)} %pad_add_fusion.refs_0_.where_ref, bf16[512,8192]{1,0:T(8,128)(2,1)} %refs_1_.3), custom_call_target="tpu_custom_call" | custom-call | bytes 16777216 | tf_op jit(solution)/shard_map/bring/pallas_call | solution.py:334
  54.9 6.5 %all_gather.7.rows_ref = bf16[32,8192]{1,0:T(8,128)(2,1)S(1)} all-gather(bf16[8,8192]{1,0:T(8,128)(2,1)S(1)} %pad_maximum_fusion.2), channel_id=1, replica_groups={{0,1,2,3},{4,5,6,7},{8,9,10,11},{12,13,14,15},{16,17,18,19},{20,21,22,2..., dimensions={0}, use_global_device_ids=true | all-gather | bytes 655360 | tf_op jit(solution)/shard_map/all_gather | solution.py:125
  61.4 3.0 %output_halves.1 = (f32[8,2,8192]{2,1,0:T(2,128)S(1)}, f32[8,2,8192]{2,1,0:T(2,128)S(1)}) custom-call(s32[2]{0:T(128)S(1)} %pad_add_fusion.refs_0_.where_ref, bf16[32,8192]{1,0:T(8,128)(2,1)S(1)} %all_gather.7.rows_ref, bf16[32,128]{1,0:T(8,128)(2,1)S(1)} %slice.87.marks_ref, bf16[512,8192]{1,0:T(8,128)(2,1)S(1)} %bring.3.output_vmem, ...), custom_call_target="tpu_custom_call" | custom-call | tf_op jit(solution)/shard_map/output_halves/pallas_call | solution.py:300
  64.4 0.4 collective-permute-start.11
  64.8 1.6 %collective-permute-done.11 = f32[8,2,8192]{2,1,0:T(2,128)S(1)} collective-permute-done((f32[8,2,8192]{2,1,0:T(2,128)S(1)}, f32[8,2,8192]{2,1,0:T(2,128)S(1)}, u32[]{:S(2)}, u32[]{:S(2)}) %collective-permute-start.11) | collective-permute-done | bytes 524320 | tf_op jit(solution)/shard_map/ppermute | solution.py:144
  66.4 0.3 add_convert_fusion
  66.7 12.7 %all_to_all.5 = bf16[8,2,8192]{2,1,0:T(2,128)(2,1)S(1)} all-to-all(bf16[8,2,8192]{2,1,0:T(2,128)(2,1)S(1)} %add_convert_fusion), channel_id=1, replica_groups={{0,2,4,6,8,10,12,14},{1,3,5,7,9,11,13,15},{16,18,20,22,24,26,28,30},{17..., dimensions={0} | all-to-all | bytes 524288 | tf_op jit(solution)/shard_map/all_to_all | solution.py:150
  79.4 0.9 %reduce_sum.22 = bf16[2,8192]{1,0:T(2,128)(2,1)} reduce(bf16[8,2,8192]{2,1,0:T(2,128)(2,1)S(1)} %all_to_all.5, bf16[]{:T(256)} %constant.22.clone.1), dimensions={0}, to_apply=%region_2.3 | reduce | flops 114688 | bytes 294914 | tf_op jit(solution)/shard_map/reduce_sum | solution.py:571
  (47 shorter events, 1.2 us)
Async XLA Ops:
  0.0 44.3 %copy-start = (bf16[2,512,1024]{2,1,0:T(8,128)(2,1)S(1)}, bf16[2,512,1024]{2,1,0:T(8,128)(2,1)}, u32[]{:S(2)}) copy-start(bf16[2,512,1024]{2,1,0:T(8,128)(2,1)} %param.23) | copy-start | bytes 6291460
  1.8 10.1 %collective-permute-start = (bf16[2,8320]{1,0:T(2,128)(2,1)}, bf16[2,8320]{1,0:T(2,128)(2,1)S(1)}, u32[]{:S(2)}, u32[]{:S(2)}) collective-permute-start(bf16[2,8320]{1,0:T(2,128)(2,1)} %norm_and_marks.1), channel_id=1, source_target_pairs={{0,4},{1,5},{2,6},{3,7},{4,0},{5,1},{6,2},{7,3},{8,12},{9,13},{10,... | collective-permute-start | bytes 99848 | tf_op jit(solution)/shard_map/ppermute | solution.py:407
  4.9 7.0 %collective-permute-start.1 = (bf16[2,8320]{1,0:T(2,128)(2,1)}, bf16[2,8320]{1,0:T(2,128)(2,1)S(1)}, u32[]{:S(2)}, u32[]{:S(2)}) collective-permute-start(bf16[2,8320]{1,0:T(2,128)(2,1)} %norm_and_marks.1), channel_id=1, source_target_pairs={{0,8},{1,9},{2,10},{3,11},{4,12},{5,13},{6,14},{7,15},{8,0},{9,1},... | collective-permute-start | bytes 99848 | tf_op jit(solution)/shard_map/ppermute | solution.py:407
  7.5 5.9 %collective-permute-start.2 = (bf16[2,8320]{1,0:T(2,128)(2,1)}, bf16[2,8320]{1,0:T(2,128)(2,1)S(1)}, u32[]{:S(2)}, u32[]{:S(2)}) collective-permute-start(bf16[2,8320]{1,0:T(2,128)(2,1)} %norm_and_marks.1), channel_id=1, source_target_pairs={{0,12},{1,13},{2,14},{3,15},{4,8},{5,9},{6,10},{7,11},{8,4},{9,5},... | collective-permute-start | bytes 99848 | tf_op jit(solution)/shard_map/ppermute | solution.py:407
  7.6 5.9 %copy-start.6 = (bf16[2,8320]{1,0:T(2,128)(2,1)S(1)}, bf16[2,8320]{1,0:T(2,128)(2,1)}, u32[]{:S(2)}) copy-start(bf16[2,8320]{1,0:T(2,128)(2,1)} %norm_and_marks.1) | copy-start | bytes 99844
  7.6 13.3 %copy-start.1 = (bf16[8192,128]{1,0:T(8,128)(2,1)S(1)}, bf16[8192,128]{1,0:T(8,128)(2,1)}, u32[]{:S(2)}) copy-start(bf16[8192,128]{1,0:T(8,128)(2,1)} %keyval_vmem.1) | copy-start | bytes 6291460
  7.6 13.3 %copy-start.3 = (bf16[4,16,8192]{2,1,0:T(8,128)(2,1)S(1)}, bf16[4,16,8192]{2,1,0:T(8,128)(2,1)}, u32[]{:S(2)}) copy-start(bf16[4,16,8192]{2,1,0:T(8,128)(2,1)} %param.20) | copy-start | bytes 3145732
  11.9 9.0 %copy-start.2 = (bf16[4,8192,16]{1,2,0:T(8,128)(2,1)S(1)}, bf16[4,8192,16]{1,2,0:T(8,128)(2,1)}, u32[]{:S(2)}) copy-start(bf16[4,8192,16]{1,2,0:T(8,128)(2,1)} %param.19) | copy-start | bytes 3145732
  24.1 14.1 %copy-start.7 = (s32[2]{0:T(128)S(1)}, s32[2]{0:T(128)}, u32[]{:S(2)}) copy-start(s32[2]{0:T(128)} %param.25) | copy-start | bytes 28
  24.1 2.0 %collective-permute-start.3 = (f32[8,2,8448]{2,1,0:T(2,128)S(1)}, f32[8,2,8448]{2,1,0:T(2,128)S(1)}, u32[]{:S(2)}, u32[]{:S(2)}) collective-permute-start(f32[8,2,8448]{2,1,0:T(2,128)S(1)} %get-tuple-element.19), channel_id=1, source_target_pairs={{0,1},{1,0},{2,3},{3,2},{4,5},{5,4},{6,7},{7,6},{8,9},{9,8},{10,11... | collective-permute-start | bytes 1622024 | tf_op jit(solution)/shard_map/ppermute | solution.py:144
  26.4 8.8 %collective-permute-start.4 = (f32[4,2,8448]{2,1,0:T(2,128)S(1)}, f32[4,2,8448]{2,1,0:T(2,128)S(1)}, u32[]{:S(2)}, u32[]{:S(2)}) collective-permute-start(f32[4,2,8448]{2,1,0:T(2,128)S(1)} %slice.89), channel_id=1, source_target_pairs={{0,2},{1,3},{2,0},{3,1},{4,6},{5,7},{6,4},{7,5},{8,10},{9,11},{10,... | collective-permute-start | bytes 811016 | tf_op jit(solution)/shard_map/ppermute | solution.py:407
  35.5 7.9 %collective-permute-start.6 = (f32[2,8704]{1,0:T(2,128)S(1)}, f32[2,8704]{1,0:T(2,128)S(1)}, u32[]{:S(2)}, u32[]{:S(2)}) collective-permute-start(f32[2,8704]{1,0:T(2,128)S(1)} %get-tuple-element.29), channel_id=1, source_target_pairs={{0,8},{1,9},{2,10},{3,11},{4,12},{5,13},{6,14},{7,15},{8,0},{9,1},... | collective-permute-start | bytes 208904 | tf_op jit(solution)/shard_map/ppermute | solution.py:407
  36.2 7.3 %collective-permute-start.7 = (f32[2,8704]{1,0:T(2,128)S(1)}, f32[2,8704]{1,0:T(2,128)S(1)}, u32[]{:S(2)}, u32[]{:S(2)}) collective-permute-start(f32[2,8704]{1,0:T(2,128)S(1)} %get-tuple-element.28), channel_id=1, source_target_pairs={{0,12},{1,13},{2,14},{3,15},{4,8},{5,9},{6,10},{7,11},{8,4},{9,5},... | collective-permute-start | bytes 208904 | tf_op jit(solution)/shard_map/ppermute | solution.py:407
  38.2 5.8 %collective-permute-start.5 = (f32[2,8704]{1,0:T(2,128)S(1)}, f32[2,8704]{1,0:T(2,128)S(1)}, u32[]{:S(2)}, u32[]{:S(2)}) collective-permute-start(f32[2,8704]{1,0:T(2,128)S(1)} %get-tuple-element.30), channel_id=1, source_target_pairs={{0,4},{1,5},{2,6},{3,7},{4,0},{5,1},{6,2},{7,3},{8,12},{9,13},{10,... | collective-permute-start | bytes 208904 | tf_op jit(solution)/shard_map/ppermute | solution.py:407
  44.1 1.6 %copy-start.8 = (bf16[2,512,1024]{2,1,0:T(8,128)(2,1)S(1)}, bf16[2,512,1024]{2,1,0:T(8,128)(2,1)}, u32[]{:S(2)}) copy-start(bf16[2,512,1024]{2,1,0:T(8,128)(2,1)} %param.24) | copy-start | bytes 6291460
  46.2 15.2 %copy-start.4 = (bf16[4,8192,16]{1,2,0:T(8,128)(2,1)S(1)}, bf16[4,8192,16]{1,2,0:T(8,128)(2,1)}, u32[]{:S(2)}) copy-start(bf16[4,8192,16]{1,2,0:T(8,128)(2,1)} %param.21) | copy-start | bytes 3145732
  46.2 15.2 %copy-start.5 = (bf16[4,16,8192]{2,1,0:T(8,128)(2,1)S(1)}, bf16[4,16,8192]{2,1,0:T(8,128)(2,1)}, u32[]{:S(2)}) copy-start(bf16[4,16,8192]{2,1,0:T(8,128)(2,1)} %param.22) | copy-start | bytes 3145732
  46.2 8.5 %collective-permute-start.10 = (bf16[2,8192]{1,0:T(2,128)(2,1)S(1)}, bf16[2,8192]{1,0:T(2,128)(2,1)S(1)}, u32[]{:S(2)}, u32[]{:S(2)}) collective-permute-start(bf16[2,8192]{1,0:T(2,128)(2,1)S(1)} %bitcast.69), channel_id=1, source_target_pairs={{0,12},{1,13},{2,14},{3,15},{4,8},{5,9},{6,10},{7,11},{8,4},{9,5},... | collective-permute-start | bytes 98312 | tf_op jit(solution)/shard_map/ppermute | solution.py:407
  47.9 6.9 %collective-permute-start.8 = (bf16[2,8192]{1,0:T(2,128)(2,1)S(1)}, bf16[2,8192]{1,0:T(2,128)(2,1)S(1)}, u32[]{:S(2)}, u32[]{:S(2)}) collective-permute-start(bf16[2,8192]{1,0:T(2,128)(2,1)S(1)} %bitcast.70), channel_id=1, source_target_pairs={{0,4},{1,5},{2,6},{3,7},{4,0},{5,1},{6,2},{7,3},{8,12},{9,13},{10,... | collective-permute-start | bytes 98312 | tf_op jit(solution)/shard_map/ppermute | solution.py:407
  48.3 6.4 %collective-permute-start.9 = (bf16[2,8192]{1,0:T(2,128)(2,1)S(1)}, bf16[2,8192]{1,0:T(2,128)(2,1)S(1)}, u32[]{:S(2)}, u32[]{:S(2)}) collective-permute-start(bf16[2,8192]{1,0:T(2,128)(2,1)S(1)} %bitcast.71), channel_id=1, source_target_pairs={{0,8},{1,9},{2,10},{3,11},{4,12},{5,13},{6,14},{7,15},{8,0},{9,1},... | collective-permute-start | bytes 98312 | tf_op jit(solution)/shard_map/ppermute | solution.py:407
  64.4 2.0 %collective-permute-start.11 = (f32[8,2,8192]{2,1,0:T(2,128)S(1)}, f32[8,2,8192]{2,1,0:T(2,128)S(1)}, u32[]{:S(2)}, u32[]{:S(2)}) collective-permute-start(f32[8,2,8192]{2,1,0:T(2,128)S(1)} %get-tuple-element.24), channel_id=1, source_target_pairs={{0,1},{1,0},{2,3},{3,2},{4,5},{5,4},{6,7},{7,6},{8,9},{9,8},{10,11... | collective-permute-start | bytes 1572872 | tf_op jit(solution)/shard_map/ppermute | solution.py:144
